TPU v7x, 32 devices: a whole 2x2x4 slice. The times are simulated.
32 devices in a mesh: seq: 8 (over y, x, core), head: 4 (over z).
Axes of the slice: x: 2, y: 2, z: 4, core: 2. Of those that a mesh axis runs over, the one named last changes fastest.
Arguments:
- tokens: bfloat16 [4, 4096, 768], P(None, 'seq'), may hold values from -6 to 6
- memory: bfloat16 [4, 1024, 768], P(None, 'seq'), may hold values from -6 to 6
- seq_lengths: int32 [4, 4], replicated, may hold values from 0 to 4096, as said below
- pack_query: bfloat16 [768, 768], P(None, 'head'), may hold values from -0.4375 to 0.4375
- pack_key: bfloat16 [768, 768], P(None, 'head'), may hold values from -0.21875 to 0.21875
- pack_value: bfloat16 [768, 768], P(None, 'head'), may hold values from -0.21875 to 0.21875
- pack_out: bfloat16 [768, 768], P('head'), may hold values from -0.875 to 0.875
- unpack_query: bfloat16 [768, 768], P(None, 'head'), may hold values from -0.21875 to 0.21875
- unpack_key: bfloat16 [768, 768], P(None, 'head'), may hold values from -0.21875 to 0.21875
- unpack_value: bfloat16 [768, 768], P(None, 'head'), may hold values from -0.21875 to 0.21875
- unpack_out: bfloat16 [768, 768], P('head'), may hold values from -1.75 to 1.75
- ffn_in: bfloat16 [768, 3072], P(None, 'head'), may hold values from -0.21875 to 0.21875
- ffn_in_bias: float32 [3072], P('head'), may hold values from -3 to 3
- ffn_out: bfloat16 [3072, 768], P('head'), may hold values from -0.109375 to 0.109375
- ffn_out_bias: float32 [768], replicated, may hold values from -3 to 3
- mem_gain: float32 [768], replicated, may hold values from 0.5 to 1.5
- mem_bias: float32 [768], replicated, may hold values from -2 to 2
- attn_gain: float32 [768], replicated, may hold values from 0.5 to 1.5
- attn_bias: float32 [768], replicated, may hold values from -2 to 2
- out_gain: float32 [768], replicated, may hold values from 0.5 to 1.5
- out_bias: float32 [768], replicated, may hold values from -2 to 2
- cot_tokens: bfloat16 [4, 4096, 768], P(None, 'seq'), may hold values from -6 to 6
- cot_memory: bfloat16 [4, 1024, 768], P(None, 'seq'), may hold values from -0.59765625 to 0.59765625
Outputs:
- out_tokens: bfloat16 [4, 4096, 768], P(None, 'seq')
- out_memory: bfloat16 [4, 1024, 768], P(None, 'seq')
- grad_tokens: bfloat16 [4, 4096, 768], P(None, 'seq')
- grad_memory: bfloat16 [4, 1024, 768], P(None, 'seq')
- grad_pack_query: float32 [768, 768], P('seq', 'head')
- grad_pack_key: float32 [768, 768], P('seq', 'head')
- grad_pack_value: float32 [768, 768], P('seq', 'head')
- grad_pack_out: float32 [768, 768], P(('head', 'seq'))
- grad_unpack_query: float32 [768, 768], P('seq', 'head')
- grad_unpack_key: float32 [768, 768], P('seq', 'head')
- grad_unpack_value: float32 [768, 768], P('seq', 'head')
- grad_unpack_out: float32 [768, 768], P(('head', 'seq'))
- grad_ffn_in: float32 [768, 3072], P('seq', 'head')
- grad_ffn_in_bias: float32 [3072], P(('head', 'seq'))
- grad_ffn_out: float32 [3072, 768], P(('head', 'seq'))
- grad_ffn_out_bias: float32 [768], P('seq')
- grad_mem_gain: float32 [768], P('seq')
- grad_mem_bias: float32 [768], P('seq')
- grad_attn_gain: float32 [768], P('seq')
- grad_attn_bias: float32 [768], P('seq')
- grad_out_gain: float32 [768], P('seq')
- grad_out_bias: float32 [768], P('seq')
Inputs may be any that keep to these rules, and one draw needn't show every extreme that they name: `seq_lengths`: each row lists the lengths of the sequences of one pack in the order in which they lie in it, each a multiple of 1024, then zeros; a row begins with a nonzero length and sums to 4096; in some row a single sequence fills the pack.
All inputs are finite; a program needn't handle non-finite values.
Results may differ from a plain program's by a relative error of at most 0.025.
Values may be sent and summed in bfloat16 or wider, within the bound.
No kernel may reach another device: no remote copies, remote signals or barrier semaphores. Data moves between devices by JAX's collectives and lax.ppermute only.
A program may use at most 192 MiB of HBM per device.

v0:
```python
import math

import jax
import jax.numpy as jnp
from jax import lax
from jax.sharding import PartitionSpec as P

HD = 64
MEM = 256
SLOTS = 4


EPSILON = 1e-05
NEG_FILL = -1e30


def norm_forward(summed, gain_vec, bias_vec):
    centre = summed - jnp.mean(summed, axis=-1, keepdims=True)
    inv_std = lax.rsqrt(jnp.mean(centre * centre, axis=-1, keepdims=True) + EPSILON)
    normed = centre * inv_std
    return (normed * gain_vec + bias_vec, normed, inv_std)


def norm_backward(upstream, normed, inv_std, gain_vec):
    scaled = upstream * gain_vec
    centred_grad = (
        scaled
        - jnp.mean(scaled, axis=-1, keepdims=True)
        - normed * jnp.mean(scaled * normed, axis=-1, keepdims=True)
    )
    flat_up = upstream.reshape(-1, upstream.shape[-1])
    flat_norm = normed.reshape(-1, normed.shape[-1])
    return (inv_std * centred_grad, jnp.sum(flat_up * flat_norm, axis=0), jnp.sum(flat_up, axis=0))


def project(values, weight):
    return jnp.einsum("pti,io->pto", values, weight, preferred_element_type=jnp.float32)


def back_project(grad_rows, weight):
    return jnp.einsum("pto,io->pti", grad_rows, weight, preferred_element_type=jnp.float32)


def weight_grad(inputs, grad_rows):
    return jnp.einsum("pti,pto->io", inputs, grad_rows, preferred_element_type=jnp.float32)


def split_heads(values):
    return values.reshape(values.shape[0], values.shape[1], -1, HD)


def join_heads(values):
    return values.reshape(values.shape[0], values.shape[1], -1)


def pick_slot(values, slot_of_pack):
    grouped = values.reshape(values.shape[0], SLOTS, MEM, values.shape[2])
    index = slot_of_pack[:, None, None, None]
    return jnp.take_along_axis(grouped, index, axis=1)[:, 0]


def spread_slot(values, slot_of_pack, fill):
    onehot = jnp.arange(SLOTS, dtype=jnp.int32)[None, :] == slot_of_pack[:, None]
    placed = jnp.where(onehot[:, :, None, None], values[:, None], fill)
    return placed.reshape(values.shape[0], SLOTS * MEM, values.shape[2])


def gather_queries(query_loc):
    return lax.all_gather(query_loc, "seq", axis=1, tiled=True)


def gather_keys(key_mem, value_mem):
    return (
        lax.all_gather(key_mem, "seq", axis=1, tiled=True),
        lax.all_gather(value_mem, "seq", axis=1, tiled=True),
    )


def local(
    tokens,
    memory,
    seq_lengths,
    pack_query,
    pack_key,
    pack_value,
    pack_out,
    unpack_query,
    unpack_key,
    unpack_value,
    unpack_out,
    ffn_in,
    ffn_in_bias,
    ffn_out,
    ffn_out_bias,
    mem_gain,
    mem_bias,
    attn_gain,
    attn_bias,
    out_gain,
    out_bias,
    cot_tokens,
    cot_memory,
):
    seq_index = lax.axis_index("seq")
    block_len = tokens.shape[1]
    model_width = tokens.shape[2]
    score_scale = 1.0 / math.sqrt(HD)
    seq_ends = jnp.cumsum(seq_lengths, axis=1)
    block_slot = jnp.sum((seq_ends <= seq_index * block_len).astype(jnp.int32), axis=1)
    tok_f32 = tokens.astype(jnp.float32)
    mem_f32 = memory.astype(jnp.float32)
    query_loc = project(memory, pack_query).astype(jnp.bfloat16)
    key_tok = project(tokens, pack_key).astype(jnp.bfloat16)
    value_tok = project(tokens, pack_value).astype(jnp.bfloat16)
    query_all = gather_queries(query_loc)
    query_slot = pick_slot(query_all, block_slot)

    def pack_scores(query_rows):
        raw = jnp.einsum(
            "prhd,pthd->phtr",
            split_heads(query_rows),
            split_heads(key_tok),
            preferred_element_type=jnp.float32,
        )
        return raw * score_scale

    scores = pack_scores(query_slot)
    local_top = jnp.swapaxes(jnp.max(scores, axis=2), 1, 2)
    top_dense = lax.pmax(spread_slot(local_top, block_slot, NEG_FILL), "seq")
    pack_top = jnp.swapaxes(pick_slot(top_dense, block_slot), 1, 2)[:, :, None, :]
    weights = jnp.exp(scores - pack_top)
    num_part = join_heads(
        jnp.einsum(
            "phtr,pthd->prhd",
            weights.astype(jnp.bfloat16),
            split_heads(value_tok),
            preferred_element_type=jnp.float32,
        )
    )
    den_part = jnp.swapaxes(jnp.sum(weights, axis=2), 1, 2)
    pack_num, pack_den = (
        lax.psum_scatter(
            spread_slot(num_part, block_slot, 0.0), "seq", scatter_dimension=1, tiled=True
        ),
        lax.psum_scatter(
            spread_slot(den_part, block_slot, 0.0), "seq", scatter_dimension=1, tiled=True
        ),
    )
    pack_inv = 1.0 / jnp.maximum(pack_den, 1.0)
    pack_ctx = split_heads(pack_num) * pack_inv[..., None]
    pack_ctx_low = join_heads(pack_ctx).astype(jnp.bfloat16)
    mem_mix = lax.psum(project(pack_ctx_low, pack_out), "head")
    mem_result, mem_normed, mem_inv = norm_forward(mem_mix + mem_f32, mem_gain, mem_bias)
    mix_low = mem_mix.astype(jnp.bfloat16)
    key_mem = project(mix_low, unpack_key).astype(jnp.bfloat16)
    value_mem = project(mix_low, unpack_value).astype(jnp.bfloat16)
    key_all, value_all = gather_keys(key_mem, value_mem)
    key_slot = pick_slot(key_all, block_slot)
    value_slot = pick_slot(value_all, block_slot)
    query_tok = project(tokens, unpack_query).astype(jnp.bfloat16)

    def unpack_scores(key_rows):
        raw = jnp.einsum(
            "pthd,prhd->phtr",
            split_heads(query_tok),
            split_heads(key_rows),
            preferred_element_type=jnp.float32,
        )
        return raw * score_scale

    tok_scores = unpack_scores(key_slot)
    tok_top = jnp.max(tok_scores, axis=3, keepdims=True)
    tok_weights = jnp.exp(tok_scores - tok_top)
    tok_inv = jnp.swapaxes(1.0 / jnp.sum(tok_weights, axis=3), 1, 2)
    tok_num = jnp.einsum(
        "phtr,prhd->pthd",
        tok_weights.astype(jnp.bfloat16),
        split_heads(value_slot),
        preferred_element_type=jnp.float32,
    )
    tok_ctx = tok_num * tok_inv[..., None]
    tok_ctx_low = join_heads(tok_ctx).astype(jnp.bfloat16)
    attn_mix = lax.psum(project(tok_ctx_low, unpack_out), "head")
    attn_result, attn_normed, attn_inv = norm_forward(attn_mix + tok_f32, attn_gain, attn_bias)
    attn_low = attn_result.astype(jnp.bfloat16)
    hidden = project(attn_low, ffn_in) + ffn_in_bias
    gelu_out, gelu_pull = jax.vjp(lambda pre_act: jax.nn.gelu(pre_act, approximate=True), hidden)
    gelu_low = gelu_out.astype(jnp.bfloat16)
    ffn_mix = lax.psum(project(gelu_low, ffn_out), "head") + ffn_out_bias
    out_result, out_normed, out_inv = norm_forward(ffn_mix + attn_result, out_gain, out_bias)
    grad_sum, grad_out_gain, grad_out_bias = norm_backward(
        cot_tokens.astype(jnp.float32), out_normed, out_inv, out_gain
    )
    ffn_grad = grad_sum.astype(jnp.bfloat16)
    grad_ffn_out_bias = jnp.sum(ffn_grad.astype(jnp.float32).reshape(-1, model_width), axis=0)
    grad_ffn_out = weight_grad(gelu_low, ffn_grad)
    grad_hidden = gelu_pull(back_project(ffn_grad, ffn_out))[0].astype(jnp.bfloat16)
    grad_ffn_in_bias = jnp.sum(
        grad_hidden.astype(jnp.float32).reshape(-1, grad_hidden.shape[-1]), axis=0
    )
    grad_ffn_in = weight_grad(attn_low, grad_hidden)
    grad_attn = grad_sum + lax.psum(back_project(grad_hidden, ffn_in), "head")
    grad_mixsum, grad_attn_gain, grad_attn_bias = norm_backward(
        grad_attn, attn_normed, attn_inv, attn_gain
    )
    mix_grad = grad_mixsum.astype(jnp.bfloat16)
    grad_unpack_out = weight_grad(tok_ctx_low, mix_grad)
    ctx_grad = split_heads(back_project(mix_grad, unpack_out))
    num_grad = (ctx_grad * tok_inv[..., None]).astype(jnp.bfloat16)
    den_grad = -tok_inv * jnp.sum(ctx_grad * tok_ctx, axis=3)
    key_back, value_back = gather_keys(key_mem, value_mem)
    query_back = gather_queries(query_loc)
    key_back = pick_slot(key_back, block_slot)
    value_back = pick_slot(value_back, block_slot)
    query_back = pick_slot(query_back, block_slot)
    tok_weights_back = jnp.exp(unpack_scores(key_back) - tok_top)
    tok_dweights = (
        jnp.einsum(
            "pthd,prhd->phtr", num_grad, split_heads(value_back), preferred_element_type=jnp.float32
        )
        + jnp.swapaxes(den_grad, 1, 2)[..., None]
    )
    tok_score_grad = (tok_weights_back * tok_dweights).astype(jnp.bfloat16)
    query_grad_low = join_heads(
        jnp.einsum(
            "phtr,prhd->pthd",
            tok_score_grad,
            split_heads(key_back),
            preferred_element_type=jnp.float32,
        )
        * score_scale
    ).astype(jnp.bfloat16)
    key_part = join_heads(
        jnp.einsum(
            "phtr,pthd->prhd",
            tok_score_grad,
            split_heads(query_tok),
            preferred_element_type=jnp.float32,
        )
        * score_scale
    )
    value_part = join_heads(
        jnp.einsum(
            "phtr,pthd->prhd",
            tok_weights_back.astype(jnp.bfloat16),
            num_grad,
            preferred_element_type=jnp.float32,
        )
    )
    key_grad_mem, value_grad_mem = (
        lax.psum_scatter(
            spread_slot(key_part, block_slot, 0.0), "seq", scatter_dimension=1, tiled=True
        ),
        lax.psum_scatter(
            spread_slot(value_part, block_slot, 0.0), "seq", scatter_dimension=1, tiled=True
        ),
    )
    key_grad_low = key_grad_mem.astype(jnp.bfloat16)
    value_grad_low = value_grad_mem.astype(jnp.bfloat16)
    grad_unpack_key = weight_grad(mix_low, key_grad_low)
    grad_unpack_value = weight_grad(mix_low, value_grad_low)
    grad_unpack_query = weight_grad(tokens, query_grad_low)
    grad_memsum, grad_mem_gain, grad_mem_bias = norm_backward(
        cot_memory.astype(jnp.float32), mem_normed, mem_inv, mem_gain
    )
    mix_part = back_project(key_grad_low, unpack_key) + back_project(value_grad_low, unpack_value)
    mem_mix_grad = (grad_memsum + lax.psum(mix_part, "head")).astype(jnp.bfloat16)
    grad_pack_out = weight_grad(pack_ctx_low, mem_mix_grad)
    pctx_grad = split_heads(back_project(mem_mix_grad, pack_out))
    pack_num_grad = (pctx_grad * pack_inv[..., None]).astype(jnp.bfloat16)
    pack_den_grad = -pack_inv * jnp.sum(pctx_grad * pack_ctx, axis=3)
    num_all, den_all = (
        lax.all_gather(join_heads(pack_num_grad).astype(jnp.float32), "seq", axis=1, tiled=True),
        lax.all_gather(pack_den_grad, "seq", axis=1, tiled=True),
    )
    num_slot = split_heads(pick_slot(num_all, block_slot).astype(jnp.bfloat16))
    den_slot = pick_slot(den_all, block_slot)
    pack_weights_back = jnp.exp(pack_scores(query_back) - pack_top)
    pack_dweights = (
        jnp.einsum(
            "prhd,pthd->phtr", num_slot, split_heads(value_tok), preferred_element_type=jnp.float32
        )
        + jnp.swapaxes(den_slot, 1, 2)[:, :, None, :]
    )
    pack_score_grad = (pack_weights_back * pack_dweights).astype(jnp.bfloat16)
    query_part = join_heads(
        jnp.einsum(
            "phtr,pthd->prhd",
            pack_score_grad,
            split_heads(key_tok),
            preferred_element_type=jnp.float32,
        )
        * score_scale
    )
    key_grad_tok = join_heads(
        jnp.einsum(
            "phtr,prhd->pthd",
            pack_score_grad,
            split_heads(query_back),
            preferred_element_type=jnp.float32,
        )
        * score_scale
    ).astype(jnp.bfloat16)
    value_grad_tok = join_heads(
        jnp.einsum(
            "phtr,prhd->pthd",
            pack_weights_back.astype(jnp.bfloat16),
            num_slot,
            preferred_element_type=jnp.float32,
        )
    ).astype(jnp.bfloat16)
    query_grad_mem = lax.psum_scatter(
        spread_slot(query_part, block_slot, 0.0), "seq", scatter_dimension=1, tiled=True
    ).astype(jnp.bfloat16)
    grad_pack_query = weight_grad(memory, query_grad_mem)
    grad_pack_key = weight_grad(tokens, key_grad_tok)
    grad_pack_value = weight_grad(tokens, value_grad_tok)
    tok_part = (
        back_project(key_grad_tok, pack_key)
        + back_project(value_grad_tok, pack_value)
        + back_project(query_grad_low, unpack_query)
    )
    mem_part = back_project(query_grad_mem, pack_query)
    tok_total, mem_total = lax.psum((tok_part, mem_part), "head")
    grad_tokens = (tok_total + grad_mixsum).astype(jnp.bfloat16)
    grad_memory = (mem_total + grad_memsum).astype(jnp.bfloat16)
    reduced = (
        lax.psum_scatter(grad_pack_query, "seq", scatter_dimension=0, tiled=True),
        lax.psum_scatter(grad_pack_key, "seq", scatter_dimension=0, tiled=True),
        lax.psum_scatter(grad_pack_value, "seq", scatter_dimension=0, tiled=True),
        lax.psum_scatter(grad_pack_out, "seq", scatter_dimension=0, tiled=True),
        lax.psum_scatter(grad_unpack_query, "seq", scatter_dimension=0, tiled=True),
        lax.psum_scatter(grad_unpack_key, "seq", scatter_dimension=0, tiled=True),
        lax.psum_scatter(grad_unpack_value, "seq", scatter_dimension=0, tiled=True),
        lax.psum_scatter(grad_unpack_out, "seq", scatter_dimension=0, tiled=True),
        lax.psum_scatter(grad_ffn_in, "seq", scatter_dimension=0, tiled=True),
        lax.psum_scatter(grad_ffn_in_bias, "seq", scatter_dimension=0, tiled=True),
        lax.psum_scatter(grad_ffn_out, "seq", scatter_dimension=0, tiled=True),
        lax.psum_scatter(grad_ffn_out_bias, "seq", scatter_dimension=0, tiled=True),
        lax.psum_scatter(grad_mem_gain, "seq", scatter_dimension=0, tiled=True),
        lax.psum_scatter(grad_mem_bias, "seq", scatter_dimension=0, tiled=True),
        lax.psum_scatter(grad_attn_gain, "seq", scatter_dimension=0, tiled=True),
        lax.psum_scatter(grad_attn_bias, "seq", scatter_dimension=0, tiled=True),
        lax.psum_scatter(grad_out_gain, "seq", scatter_dimension=0, tiled=True),
        lax.psum_scatter(grad_out_bias, "seq", scatter_dimension=0, tiled=True),
    )
    return (
        out_result.astype(jnp.bfloat16),
        mem_result.astype(jnp.bfloat16),
        grad_tokens,
        grad_memory,
        reduced[0],
        reduced[1],
        reduced[2],
        reduced[3],
        reduced[4],
        reduced[5],
        reduced[6],
        reduced[7],
        reduced[8],
        reduced[9],
        reduced[10],
        reduced[11],
        reduced[12],
        reduced[13],
        reduced[14],
        reduced[15],
        reduced[16],
        reduced[17],
    )


def solution(mesh):
    in_specs = (
        P(None, "seq", None),
        P(None, "seq", None),
        P(),
        P(None, "head"),
        P(None, "head"),
        P(None, "head"),
        P("head", None),
        P(None, "head"),
        P(None, "head"),
        P(None, "head"),
        P("head", None),
        P(None, "head"),
        P("head"),
        P("head", None),
        P(),
        P(),
        P(),
        P(),
        P(),
        P(),
        P(),
        P(None, "seq", None),
        P(None, "seq", None),
    )
    out_specs = (
        P(None, "seq", None),
        P(None, "seq", None),
        P(None, "seq", None),
        P(None, "seq", None),
        P("seq", "head"),
        P("seq", "head"),
        P("seq", "head"),
        P(("head", "seq"), None),
        P("seq", "head"),
        P("seq", "head"),
        P("seq", "head"),
        P(("head", "seq"), None),
        P("seq", "head"),
        P(("head", "seq")),
        P(("head", "seq"), None),
        P("seq"),
        P("seq"),
        P("seq"),
        P("seq"),
        P("seq"),
        P("seq"),
        P("seq"),
    )
    return jax.shard_map(local, mesh=mesh, in_specs=in_specs, out_specs=out_specs, check_vma=False)
```

profile of v0, /device:TPU:0, one launch (start us, length us, event | category | flops | bytes accessed | tf_op | source)
XLA Modules:
  0.0 2039.7 jit_solution(4025998374962779870)
XLA Ops:
  47.8 23.9 %pmax.7 = f32[4,4,256,3]{2,3,1,0:T(4,128)S(1)} all-reduce(f32[4,4,256,3]{2,3,1,0:T(4,128)S(1)} %copy.76), channel_id=1, replica_groups=mesh['seq'=8,'head'=4] {'seq'}, use_global_device_ids=true, to_apply=%region_3.5 | all-reduce | flops 12288 | bytes 98304 | tf_op jit(solution)/shard_map/pmax | solution.py:129
  96.6 21.3 %reduce-scatter.46.cloned.1.call-done = f32[128,12]{1,0:T(8,128)} async-done(((f32[1024,12]{1,0:T(8,128)}), f32[128,12]{1,0:T(8,128)}) %reduce-scatter.46.cloned.1.call-update) | async-done | bytes 6160
  119.0 49.5 %reduce-scatter.26.cloned.1.call-done = f32[4,128,192]{1,2,0:T(8,128)} async-done(((f32[4,1024,192]{1,2,0:T(8,128)}), f32[4,128,192]{1,2,0:T(8,128)}) %reduce-scatter.26.cloned.1.call-update) | async-done | bytes 393232 | tf_op jit(solution)/shard_map/reduce_scatter | solution.py:142
  171.9 69.2 %all-reduce.17.cloned.1.call-done = f32[4,128,768]{2,1,0:T(8,128)} async-done(((f32[4,128,768]{2,1,0:T(8,128)}), f32[4,128,768]{2,1,0:T(8,128)}) %all-reduce.17.cloned.1.call-update) | async-done | bytes 1572880 | tf_op jit(solution)/shard_map/psum | solution.py:152
  276.9 22.6 %all-gather.7.cloned.1.call-done = bf16[4,1024,192]{1,2,0:T(8,128)(2,1)} async-done(((bf16[4,128,192]{1,2,0:T(8,128)(2,1)}), bf16[4,1024,192]{1,2,0:T(8,128)(2,1)}) %all-gather.7.cloned.1.call-update) | async-done | bytes 1572880 | tf_op jit(solution)/shard_map/all_gather | solution.py:75
  317.8 223.0 %all-reduce.19.cloned.1.call-done = f32[4,512,768]{2,1,0:T(8,128)} async-done(((f32[4,512,768]{2,1,0:T(8,128)}), f32[4,512,768]{2,1,0:T(8,128)}) %all-reduce.19.cloned.1.call-update) | async-done | bytes 6291472 | tf_op jit(solution)/shard_map/psum | solution.py:183
  559.7 221.5 %all-reduce.21.cloned.1.call-done = f32[4,512,768]{2,1,0:T(8,128)} async-done(((f32[4,512,768]{2,1,0:T(8,128)}), f32[4,512,768]{2,1,0:T(8,128)}) %all-reduce.21.cloned.1.call-update) | async-done | bytes 6291472 | tf_op jit(solution)/shard_map/psum | solution.py:189
  811.3 221.7 %all-reduce.23.cloned.1.call-done = f32[4,512,768]{2,1,0:T(8,128)} async-done(((f32[4,512,768]{2,1,0:T(8,128)}), f32[4,512,768]{2,1,0:T(8,128)}) %all-reduce.23.cloned.1.call-update) | async-done | bytes 6291472 | tf_op jit(solution)/shard_map/psum | solution.py:202
  1085.9 44.5 %reduce-scatter.28.cloned.1.call-done = f32[4,128,192]{1,2,0:T(8,128)} async-done(((f32[4,1024,192]{1,2,0:T(8,128)}), f32[4,128,192]{1,2,0:T(8,128)}) %reduce-scatter.28.cloned.1.call-update) | async-done | bytes 393232 | tf_op jit(solution)/shard_map/reduce_scatter | solution.py:251
  1133.0 48.0 %reduce-scatter.30.cloned.1.call-done = f32[4,128,192]{1,2,0:T(8,128)} async-done(((f32[4,1024,192]{1,2,0:T(8,128)}), f32[4,128,192]{1,2,0:T(8,128)}) %reduce-scatter.30.cloned.1.call-update) | async-done | bytes 393232 | tf_op jit(solution)/shard_map/reduce_scatter | solution.py:254
  1186.4 67.0 %all-reduce.25.cloned.1.call-done = f32[4,128,768]{2,1,0:T(8,128)} async-done(((f32[4,128,768]{2,1,0:T(8,128)}), f32[4,128,768]{2,1,0:T(8,128)}) %all-reduce.25.cloned.1.call-update) | async-done | bytes 1572880 | tf_op jit(solution)/shard_map/psum | solution.py:267
  1323.5 29.6 %reduce-scatter.32.cloned.1.call-done = f32[4,128,192]{1,2,0:T(8,128)} async-done(((f32[4,1024,192]{1,2,0:T(8,128)}), f32[4,128,192]{1,2,0:T(8,128)}) %reduce-scatter.32.cloned.1.call-update) | async-done | bytes 393232 | tf_op jit(solution)/shard_map/reduce_scatter | solution.py:312
  1404.7 26.4 %all-reduce.8 = (f32[768]{0:T(1024)}, f32[768]{0:T(1024)}, f32[768]{0:T(1024)}, f32[768]{0:T(1024)}, f32[768]{0:T(1024)}, /*index=5*/f32[768]{0:T(1024)}, f32[768]{0:T(1024)}, f32[768]{0:T(1024)}) all-reduce(f32[768]{0:T(1024)} %get-tuple-element.139, f32[768]{0:T(1024)} %get-tuple-element.112, ...), channel_id=16, replica_groups=mesh['seq'=8,'head'=4] {'seq'}, use_global_device_ids=true, to_apply=%region_43.46.clone | all-reduce | flops 6144 | bytes 49152
  1444.6 185.5 %all-reduce.27.cloned.1.call-done = (f32[4,512,768]{2,1,0:T(8,128)}, f32[4,128,768]{2,1,0:T(8,128)}) async-done(((f32[4,512,768]{2,1,0:T(8,128)}, f32[4,128,768]{2,1,0:T(8,128)}), (f32[4,512,768]{2,1,0:T(8,128)}, f32[4,128,768]{2,1,0:T(8,128)})) %all-reduce.27.cloned.1.call-update) | async-done | bytes 7864336 | tf_op jit(solution)/shard_map/psum | solution.py:324
  1640.4 35.3 %reduce-scatter.44.cloned.1.call-done = f32[96,768]{1,0:T(8,128)} async-done(((f32[768,768]{1,0:T(8,128)}), f32[96,768]{1,0:T(8,128)}) %reduce-scatter.44.cloned.1.call-update) | async-done | bytes 294928 | tf_op jit(solution)/shard_map/reduce_scatter | solution.py:338
  1675.7 46.3 %reduce-scatter.42.cloned.1.call-done = f32[96,768]{1,0:T(8,128)} async-done(((f32[768,768]{1,0:T(8,128)}), f32[96,768]{1,0:T(8,128)}) %reduce-scatter.42.cloned.1.call-update) | async-done | bytes 294928 | tf_op jit(solution)/shard_map/reduce_scatter | solution.py:336
  1722.0 38.3 %reduce-scatter.40.cloned.1.call-done = f32[24,768]{1,0:T(8,128)} async-done(((f32[192,768]{1,0:T(8,128)}), f32[24,768]{1,0:T(8,128)}) %reduce-scatter.40.cloned.1.call-update) | async-done | bytes 73744 | tf_op jit(solution)/shard_map/reduce_scatter | solution.py:335
  1760.3 39.0 %reduce-scatter.54.cloned.1.call-done = f32[96,192]{1,0:T(8,128)} async-done(((f32[768,192]{1,0:T(8,128)}), f32[96,192]{1,0:T(8,128)}) %reduce-scatter.54.cloned.1.call-update) | async-done | bytes 73744
  1799.3 38.9 %reduce-scatter.38.cloned.1.call-done = f32[96,192]{1,0:T(8,128)} async-done(((f32[768,192]{1,0:T(8,128)}), f32[96,192]{1,0:T(8,128)}) %reduce-scatter.38.cloned.1.call-update) | async-done | bytes 73744 | tf_op jit(solution)/shard_map/reduce_scatter | solution.py:334
  1838.2 39.0 %reduce-scatter.36.cloned.1.call-done = f32[96,192]{1,0:T(8,128)} async-done(((f32[768,192]{1,0:T(8,128)}), f32[96,192]{1,0:T(8,128)}) %reduce-scatter.36.cloned.1.call-update) | async-done | bytes 73744 | tf_op jit(solution)/shard_map/reduce_scatter | solution.py:333
  1877.3 38.4 %reduce-scatter.34.cloned.1.call-done = f32[24,768]{1,0:T(8,128)} async-done(((f32[192,768]{1,0:T(8,128)}), f32[24,768]{1,0:T(8,128)}) %reduce-scatter.34.cloned.1.call-update) | async-done | bytes 73744 | tf_op jit(solution)/shard_map/reduce_scatter | solution.py:331
  1915.7 39.1 %reduce-scatter.50.cloned.1.call-done = f32[96,192]{1,0:T(8,128)} async-done(((f32[768,192]{1,0:T(8,128)}), f32[96,192]{1,0:T(8,128)}) %reduce-scatter.50.cloned.1.call-update) | async-done | bytes 73744
  1954.7 38.9 %reduce-scatter.52.cloned.1.call-done = f32[96,192]{1,0:T(8,128)} async-done(((f32[768,192]{1,0:T(8,128)}), f32[96,192]{1,0:T(8,128)}) %reduce-scatter.52.cloned.1.call-update) | async-done | bytes 73744
  1993.6 39.1 %reduce-scatter.48.cloned.1.call-done = f32[96,192]{1,0:T(8,128)} async-done(((f32[768,192]{1,0:T(8,128)}), f32[96,192]{1,0:T(8,128)}) %reduce-scatter.48.cloned.1.call-update) | async-done | bytes 73744
  (382 shorter events, 377.1 us)
Async XLA Ops:
  9.7 108.2 %reduce-scatter.46.cloned.1.call-start = ((), (), s32[]{:S(2)}) async-start(), calls=%async_computation.34 | async-start | bytes 589824
  83.6 84.9 %reduce-scatter.26.cloned.1.call-start = ((), (), s32[]{:S(2)}) async-start(), calls=%async_computation.16 | async-start | bytes 3538944 | tf_op jit(solution)/shard_map/reduce_scatter | solution.py:142
  96.5 144.5 %all-reduce.17.cloned.1.call-start = ((), (), s32[]{:S(2)}) async-start(), calls=%async_computation.17 | async-start | bytes 3145728 | tf_op jit(solution)/shard_map/psum | solution.py:152
  171.8 99.6 %all-gather.9.cloned.1.call-start = ((), (), s32[]{:S(2)}) async-start(), calls=%async_computation.19 | async-start | bytes 1769472 | tf_op jit(solution)/shard_map/all_gather | solution.py:74
  246.3 53.3 %all-gather.7.cloned.1.call-start = ((), (), s32[]{:S(2)}) async-start(), calls=%async_computation.18 | async-start | bytes 1769472 | tf_op jit(solution)/shard_map/all_gather | solution.py:75
  248.4 292.3 %all-reduce.19.cloned.1.call-start = ((), (), s32[]{:S(2)}) async-start(), calls=%async_computation.20 | async-start | bytes 12582912 | tf_op jit(solution)/shard_map/psum | solution.py:183
  317.7 463.4 %all-reduce.21.cloned.1.call-start = ((), (), s32[]{:S(2)}) async-start(), calls=%async_computation.21 | async-start | bytes 12582912 | tf_op jit(solution)/shard_map/psum | solution.py:189
  559.2 473.8 %all-reduce.23.cloned.1.call-start = ((), (), s32[]{:S(2)}) async-start(), calls=%async_computation.22 | async-start | bytes 12582912 | tf_op jit(solution)/shard_map/psum | solution.py:202
  811.1 319.3 %reduce-scatter.28.cloned.1.call-start = ((), (), s32[]{:S(2)}) async-start(), calls=%async_computation.23 | async-start | bytes 3538944 | tf_op jit(solution)/shard_map/reduce_scatter | solution.py:251
  1085.1 95.9 %reduce-scatter.30.cloned.1.call-start = ((), (), s32[]{:S(2)}) async-start(), calls=%async_computation.24 | async-start | bytes 3538944 | tf_op jit(solution)/shard_map/reduce_scatter | solution.py:254
  1085.8 167.5 %all-reduce.25.cloned.1.call-start = ((), (), s32[]{:S(2)}) async-start(), calls=%async_computation.25 | async-start | bytes 3145728 | tf_op jit(solution)/shard_map/psum | solution.py:267
  1184.1 98.9 %all-gather.11.cloned.1.call-start = ((), (), s32[]{:S(2)}) async-start(), calls=%async_computation.26 | async-start | bytes 1769472 | tf_op jit(solution)/shard_map/all_gather | solution.py:273
  1257.9 95.2 %reduce-scatter.32.cloned.1.call-start = ((), (), s32[]{:S(2)}) async-start(), calls=%async_computation.27 | async-start | bytes 3538944 | tf_op jit(solution)/shard_map/reduce_scatter | solution.py:312
  1306.5 323.6 %all-reduce.27.cloned.1.call-start = ((), (), s32[]{:S(2)}) async-start(), calls=%async_computation.39 | async-start | bytes 15728640 | tf_op jit(solution)/shard_map/psum | solution.py:324
  1355.7 320.1 %reduce-scatter.44.cloned.1.call-start = ((), (), s32[]{:S(2)}) async-start(), calls=%async_computation.33 | async-start | bytes 2654208 | tf_op jit(solution)/shard_map/reduce_scatter | solution.py:338
  1364.6 357.4 %reduce-scatter.42.cloned.1.call-start = ((), (), s32[]{:S(2)}) async-start(), calls=%async_computation.32 | async-start | bytes 2654208 | tf_op jit(solution)/shard_map/reduce_scatter | solution.py:336
  1373.1 387.2 %reduce-scatter.40.cloned.1.call-start = ((), (), s32[]{:S(2)}) async-start(), calls=%async_computation.31 | async-start | bytes 663552 | tf_op jit(solution)/shard_map/reduce_scatter | solution.py:335
  1377.6 421.8 %reduce-scatter.54.cloned.1.call-start = ((), (), s32[]{:S(2)}) async-start(), calls=%async_computation.38 | async-start | bytes 884736
  1383.5 454.7 %reduce-scatter.38.cloned.1.call-start = ((), (), s32[]{:S(2)}) async-start(), calls=%async_computation.30 | async-start | bytes 884736 | tf_op jit(solution)/shard_map/reduce_scatter | solution.py:334
  1385.9 491.3 %reduce-scatter.36.cloned.1.call-start = ((), (), s32[]{:S(2)}) async-start(), calls=%async_computation.29 | async-start | bytes 884736 | tf_op jit(solution)/shard_map/reduce_scatter | solution.py:333
  1388.3 527.3 %reduce-scatter.34.cloned.1.call-start = ((), (), s32[]{:S(2)}) async-start(), calls=%async_computation.28 | async-start | bytes 663552 | tf_op jit(solution)/shard_map/reduce_scatter | solution.py:331
  1390.8 564.0 %reduce-scatter.50.cloned.1.call-start = ((), (), s32[]{:S(2)}) async-start(), calls=%async_computation.36 | async-start | bytes 884736
  1396.7 596.9 %reduce-scatter.52.cloned.1.call-start = ((), (), s32[]{:S(2)}) async-start(), calls=%async_computation.37 | async-start | bytes 884736
  1402.7 629.9 %reduce-scatter.48.cloned.1.call-start = ((), (), s32[]{:S(2)}) async-start(), calls=%async_computation.35 | async-start | bytes 884736
  (94 other events, 5847.5 us)
Sparse Core Ops, SparseCore 0:
  10.5 28.5 all-gather.4
  83.8 34.1 reduce-scatter.45
  122.2 46.2 reduce-scatter.25
  171.9 69.1 all-reduce.16
  273.7 25.8 all-gather.6
  317.8 222.8 all-reduce.18
  559.3 221.7 all-reduce.20
  811.2 221.7 all-reduce.22
  1085.2 45.1 reduce-scatter.27
  1134.7 46.2 reduce-scatter.29
  1184.2 69.1 all-reduce.24
  1258.0 24.9 all-gather.10
  1306.7 46.3 reduce-scatter.31
  1356.0 274.0 all-reduce.26
  1634.3 41.3 reduce-scatter.43
  1679.5 42.4 reduce-scatter.41
  1725.9 34.3 reduce-scatter.39
  1764.3 34.9 reduce-scatter.53
  1803.2 34.9 reduce-scatter.37
  1842.3 34.9 reduce-scatter.35
  1881.2 34.3 reduce-scatter.33
  1919.7 34.9 reduce-scatter.49
  1958.6 34.9 reduce-scatter.51
  1997.6 34.9 reduce-scatter.47
  (1 shorter events, 24.9 us)
where the time goes:
time: 2050 us; the launch traced here: 2040 us
  waiting for transfers between devices  1650 us (80%)
  matrix products  138 us (7%)
  local copies, waits for them, and re-layouts  94.2 us (5%)
  other arithmetic  83.3 us (4%)
  blocking collectives  59.5 us (3%)
    psum x1, waiting for transfers between devices, local(): attn_mix = lax.psum(project(tok_ctx_low, unpack_out), 'head')  223 us
    psum x1, waiting for transfers between devices, local(): grad_attn = grad_sum + lax.psum(back_project(grad_hidden, ffn_in), 'head')  222 us
    psum x1, waiting for transfers between devices, local(): ffn_mix = lax.psum(project(gelu_low, ffn_out), 'head') + ffn_out_bias  221 us
    psum x1, waiting for transfers between devices, local(): tok_total, mem_total = lax.psum((tok_part, mem_part), 'head')  186 us
    unnamed x30, waiting for transfers between devices  178 us
    psum x1, waiting for transfers between devices, local(): mem_mix = lax.psum(project(pack_ctx_low, pack_out), 'head')  69.2 us
    psum x1, waiting for transfers between devices, local(): lax.psum(mix_part, 'head')  67 us
    reduce_scatter x1, waiting for transfers between devices, local(): lax.psum_scatter(spread_slot(num_part, block_slot, 0.0), 'seq', scatter_d...  49.5 us
  transfers between devices with their start and end apart: 25, of which 25 were waited for; matrix products, arithmetic and copies ran while one was open for 6% of the time, Pallas kernels for 0%

commit v1 on v0

v1 whole, which is shorter than its diff:
```python
import math

import jax
import jax.numpy as jnp
from jax import lax
from jax.sharding import PartitionSpec as P

HD = 64
MEM = 256
SLOTS = 4
EPSILON = 1e-05
NEG_FILL = -1e30
BF = jnp.bfloat16
F32 = jnp.float32


def norm_forward(summed, gain_vec, bias_vec):
    centre = summed - jnp.mean(summed, axis=-1, keepdims=True)
    inv_std = lax.rsqrt(jnp.mean(centre * centre, axis=-1, keepdims=True) + EPSILON)
    normed = centre * inv_std
    return (normed * gain_vec + bias_vec, normed, inv_std)


def norm_backward(upstream, normed, inv_std, gain_vec):
    scaled = upstream * gain_vec
    centred_grad = (
        scaled
        - jnp.mean(scaled, axis=-1, keepdims=True)
        - normed * jnp.mean(scaled * normed, axis=-1, keepdims=True)
    )
    return (inv_std * centred_grad, jnp.sum(upstream * normed, axis=0), jnp.sum(upstream, axis=0))


def mm(left, right):
    return jnp.dot(left, right, preferred_element_type=F32)


def mm_t(left, right):
    return lax.dot_general(left, right, (((1,), (1,)), ((), ())), preferred_element_type=F32)


def t_mm(left, right):
    return lax.dot_general(left, right, (((0,), (0,)), ((), ())), preferred_element_type=F32)


def ein(pattern, left, right):
    return jnp.einsum(pattern, left, right, preferred_element_type=F32)


def heads_of(values):
    return values.reshape(values.shape[0], -1, HD)


def flat(values):
    return values.reshape(values.shape[0], -1)


def wide(per_head):
    rows, heads = per_head.shape
    return jnp.broadcast_to(per_head[:, :, None], (rows, heads, HD)).reshape(rows, heads * HD)


def parts_of(value):
    first = lax.reduce_precision(value, 8, 7)
    rest = value - first
    second = lax.reduce_precision(rest, 8, 7)
    return [first.astype(BF), second.astype(BF), (rest - second).astype(BF)]


def joined(parts):
    heads = parts.shape[1] // 3
    wide_parts = parts.astype(F32)
    return (
        wide_parts[:, :heads]
        + wide_parts[:, heads : 2 * heads]
        + wide_parts[:, 2 * heads :]
    )


def make_local(axis_seq, axis_head):
    unit = axis_seq // SLOTS

    def swap(value, step):
        return lax.ppermute(value, "seq", [(i, i ^ step) for i in range(axis_seq)])

    def local(
        tokens,
        memory,
        seq_lengths,
        pack_query,
        pack_key,
        pack_value,
        pack_out,
        unpack_query,
        unpack_key,
        unpack_value,
        unpack_out,
        ffn_in,
        ffn_in_bias,
        ffn_out,
        ffn_out_bias,
        mem_gain,
        mem_bias,
        attn_gain,
        attn_bias,
        out_gain,
        out_bias,
        cot_tokens,
        cot_memory,
    ):
        seq_index = lax.axis_index("seq")
        head_index = lax.axis_index("head")
        block_len = tokens.shape[1]
        width = tokens.shape[2]
        heads = width // HD
        scale = 1.0 / math.sqrt(HD)
        my_unit, my_lane = seq_index // unit, seq_index % unit

        def mine(value):
            return lax.dynamic_index_in_dim(value, head_index, 0, keepdims=False)

        def seq_rows(value):
            size = value.shape[0] // axis_seq
            return lax.dynamic_slice_in_dim(value, seq_index * size, size, 0)

        columns = jnp.concatenate(
            [
                seq_rows(w)
                for w in (
                    pack_query,
                    pack_key,
                    pack_value,
                    unpack_query,
                    unpack_key,
                    unpack_value,
                )
            ],
            axis=1,
        )
        columns = lax.all_gather(columns, ("seq", "head"), axis=0)
        columns = columns.reshape(axis_seq, axis_head, -1, 6, width // axis_head)
        columns = columns.transpose(3, 0, 2, 1, 4).reshape(6, width, width)
        w_pq, w_pk, w_pv, w_uq, w_uk, w_uv = [columns[i] for i in range(6)]
        outs = jnp.stack([seq_rows(pack_out), seq_rows(unpack_out)])
        outs = lax.all_gather(outs, ("head", "seq"), axis=0)
        outs = outs.transpose(1, 0, 2, 3).reshape(2, width, width)
        w_po, w_uo = outs[0], outs[1]
        w_fi = lax.all_gather(seq_rows(ffn_in), ("head", "seq"), axis=0)
        w_fi = w_fi.reshape(axis_head, width, -1).transpose(1, 0, 2).reshape(width, -1)
        w_fo = lax.all_gather(seq_rows(ffn_out), ("head", "seq"), axis=0, tiled=True)
        b_fi = lax.all_gather(ffn_in_bias, "head", axis=0, tiled=True)

        tok = mine(tokens)
        mem = mine(memory)
        cot_tok = mine(cot_tokens).astype(F32)
        cot_mem = mine(cot_memory).astype(F32)
        tok_f32 = tok.astype(F32)
        mem_f32 = mem.astype(F32)
        seq_ends = jnp.cumsum(mine(seq_lengths))
        slot = jnp.sum((seq_ends <= seq_index * block_len).astype(jnp.int32))

        def gather_unit(value):
            step = 1
            while step < unit:
                other = swap(value, step)
                low = (my_lane // step) % 2 == 0
                value = jnp.concatenate(
                    [jnp.where(low, value, other), jnp.where(low, other, value)], axis=0
                )
                step *= 2
            return value

        def scatter_unit(value, add):
            step = unit // 2
            while step >= 1:
                half = value.shape[0] // 2
                low = (my_lane // step) % 2 == 0
                keep = jnp.where(low, value[:half], value[half:])
                send = jnp.where(low, value[half:], value[:half])
                value = add([keep, swap(send, step)])
                step //= 2
            return value

        def fetch(value):
            picked = value
            for j in range(1, SLOTS):
                other = swap(value, j * unit)
                picked = jnp.where(slot == (my_unit ^ j), other, picked)
            return gather_unit(picked)

        def deliver(value, empty, add):
            value = scatter_unit(value, add)
            got = [jnp.where(slot == my_unit, value, empty)]
            for j in range(1, SLOTS):
                got.append(swap(jnp.where(slot == (my_unit ^ j), value, empty), j * unit))
            return add(got)

        def sum_rows(values):
            total = values[0].astype(F32)
            for value in values[1:]:
                total = total + value.astype(F32)
            return total.astype(BF)

        lane_pad = -(heads * 3) % 128

        def with_scalars(rows, scalars):
            cols = [rows]
            for scalar in scalars:
                cols += parts_of(scalar)
            pad = -sum(c.shape[1] for c in cols[1:]) % 128
            cols.append(jnp.zeros((rows.shape[0], pad), BF))
            return jnp.concatenate(cols, axis=1)

        def scalars_in(packed, which):
            start = width + which * 3 * heads
            return joined(packed[:, start : start + 3 * heads])

        def blend(values):
            lses = [scalars_in(v, 0) for v in values]
            top = lses[0]
            for lse in lses[1:]:
                top = jnp.maximum(top, lse)
            shares = [jnp.exp(lse - top) for lse in lses]
            total = shares[0]
            for share in shares[1:]:
                total = total + share
            inv = 1.0 / total
            ctx = wide(shares[0] * inv) * values[0][:, :width].astype(F32)
            for share, value in zip(shares[1:], values[1:]):
                ctx = ctx + wide(share * inv) * value[:, :width].astype(F32)
            return with_scalars(ctx.astype(BF), [top + jnp.log(total)])

        mem_slot = fetch(mem)

        q_pack = mm(mem_slot, w_pq).astype(BF)
        k_pack = mm(tok, w_pk).astype(BF)
        v_pack = mm(tok, w_pv).astype(BF)

        def pack_scores():
            return ein("rhd,thd->hrt", heads_of(q_pack), heads_of(k_pack)) * scale

        scores = pack_scores()
        top = jnp.max(scores, axis=2, keepdims=True)
        weights = jnp.exp(scores - top)
        den = jnp.sum(weights, axis=2)
        num = flat(ein("hrt,thd->rhd", weights.astype(BF), heads_of(v_pack)))
        ctx_here = (num * wide(1.0 / den.T)).astype(BF)
        lse_here = (top[:, :, 0] + jnp.log(den)).T
        empty = jnp.concatenate(
            [
                jnp.zeros((1, width), BF),
                jnp.full((1, heads), NEG_FILL, BF),
                jnp.zeros((1, 2 * heads + lane_pad), BF),
            ],
            axis=1,
        )
        blended = deliver(with_scalars(ctx_here, [lse_here]), empty, blend)
        pack_ctx = blended[:, :width]
        pack_lse = scalars_in(blended, 0)
        mem_mix = mm(pack_ctx, w_po)
        mem_result, mem_normed, mem_inv = norm_forward(mem_mix + mem_f32, mem_gain, mem_bias)
        mix_low = mem_mix.astype(BF)
        mix_slot = fetch(mix_low)

        k_un = mm(mix_slot, w_uk).astype(BF)
        v_un = mm(mix_slot, w_uv).astype(BF)
        q_un = mm(tok, w_uq).astype(BF)
        tok_scores = ein("thd,rhd->htr", heads_of(q_un), heads_of(k_un)) * scale
        tok_top = jnp.max(tok_scores, axis=2, keepdims=True)
        tok_weights = jnp.exp(tok_scores - tok_top)
        tok_inv = (1.0 / jnp.sum(tok_weights, axis=2)).T
        tok_num = flat(ein("htr,rhd->thd", tok_weights.astype(BF), heads_of(v_un)))
        tok_ctx = tok_num * wide(tok_inv)
        tok_ctx_low = tok_ctx.astype(BF)
        attn_mix = mm(tok_ctx_low, w_uo)
        attn_result, attn_normed, attn_inv = norm_forward(attn_mix + tok_f32, attn_gain, attn_bias)

        attn_low = attn_result.astype(BF)
        hidden = mm(attn_low, w_fi) + b_fi
        gelu_out, gelu_pull = jax.vjp(lambda pre: jax.nn.gelu(pre, approximate=True), hidden)
        gelu_low = gelu_out.astype(BF)
        ffn_mix = mm(gelu_low, w_fo) + ffn_out_bias
        out_result, out_normed, out_inv = norm_forward(ffn_mix + attn_result, out_gain, out_bias)
        out_tokens = lax.all_gather(out_result.astype(BF), "head", axis=0)
        out_memory = lax.all_gather(mem_result.astype(BF), "head", axis=0)

        grad_sum, grad_out_gain, grad_out_bias = norm_backward(
            cot_tok, out_normed, out_inv, out_gain
        )
        ffn_grad = grad_sum.astype(BF)
        grad_ffn_out_bias = jnp.sum(ffn_grad.astype(F32), axis=0)
        grad_ffn_out = t_mm(gelu_low, ffn_grad).astype(BF)
        grad_hidden = gelu_pull(mm_t(ffn_grad, w_fo))[0].astype(BF)
        grad_ffn_in_bias = jnp.sum(grad_hidden.astype(F32), axis=0)
        grad_ffn_in = t_mm(attn_low, grad_hidden).astype(BF)
        grad_attn = grad_sum + mm_t(grad_hidden, w_fi)
        grad_mixsum, grad_attn_gain, grad_attn_bias = norm_backward(
            grad_attn, attn_normed, attn_inv, attn_gain
        )

        mix_grad = grad_mixsum.astype(BF)
        grad_unpack_out = t_mm(tok_ctx_low, mix_grad).astype(BF)
        ctx_grad = mm_t(mix_grad, w_uo)
        num_grad = (ctx_grad * wide(tok_inv)).astype(BF)
        den_grad = -tok_inv * jnp.sum(heads_of(ctx_grad * tok_ctx), axis=2)
        tok_dweights = ein("thd,rhd->htr", heads_of(num_grad), heads_of(v_un)) + den_grad.T[:, :, None]
        tok_dscores = (tok_weights * tok_dweights).astype(BF)
        uq_grad = flat(ein("htr,rhd->thd", tok_dscores, heads_of(k_un)) * scale).astype(BF)
        uk_part = flat(ein("htr,thd->rhd", tok_dscores, heads_of(q_un)) * scale).astype(BF)
        uv_part = flat(ein("htr,thd->rhd", tok_weights.astype(BF), heads_of(num_grad))).astype(BF)
        mix_part = (mm_t(uk_part, w_uk) + mm_t(uv_part, w_uv)).astype(BF)
        mix_total = deliver(mix_part, jnp.zeros((), BF), sum_rows)
        grad_unpack_query = t_mm(tok, uq_grad).astype(BF)
        grad_unpack_key = t_mm(mix_slot, uk_part).astype(BF)
        grad_unpack_value = t_mm(mix_slot, uv_part).astype(BF)

        grad_memsum, grad_mem_gain, grad_mem_bias = norm_backward(
            cot_mem, mem_normed, mem_inv, mem_gain
        )
        mem_mix_grad = (grad_memsum + mix_total.astype(F32)).astype(BF)
        grad_pack_out = t_mm(pack_ctx, mem_mix_grad).astype(BF)
        pctx_grad = mm_t(mem_mix_grad, w_po)
        delta = jnp.sum(heads_of(pctx_grad * pack_ctx.astype(F32)), axis=2)
        back = fetch(with_scalars(pctx_grad.astype(BF), [pack_lse, delta]))
        pctx_slot = back[:, :width]
        lse_slot = scalars_in(back, 0).T[:, :, None]
        delta_slot = scalars_in(back, 1).T[:, :, None]

        weights_back = jnp.exp(pack_scores() - lse_slot)
        dweights = ein("rhd,thd->hrt", heads_of(pctx_slot), heads_of(v_pack)) - delta_slot
        dscores = (weights_back * dweights).astype(BF)
        pq_part = flat(ein("hrt,thd->rhd", dscores, heads_of(k_pack)) * scale).astype(BF)
        pk_grad = flat(ein("hrt,rhd->thd", dscores, heads_of(q_pack)) * scale).astype(BF)
        pv_grad = flat(ein("hrt,rhd->thd", weights_back.astype(BF), heads_of(pctx_slot))).astype(BF)
        tok_part = mm_t(pk_grad, w_pk) + mm_t(pv_grad, w_pv) + mm_t(uq_grad, w_uq)
        grad_tokens = (tok_part + grad_mixsum).astype(BF)
        grad_tokens = lax.all_gather(grad_tokens, "head", axis=0)
        mem_part = deliver(mm_t(pq_part, w_pq).astype(BF), jnp.zeros((), BF), sum_rows)
        grad_memory = (mem_part.astype(F32) + grad_memsum).astype(BF)
        grad_memory = lax.all_gather(grad_memory, "head", axis=0)
        grad_pack_query = t_mm(mem_slot, pq_part).astype(BF)
        grad_pack_key = t_mm(tok, pk_grad).astype(BF)
        grad_pack_value = t_mm(tok, pv_grad).astype(BF)

        def scatter(value, axis, dim):
            return lax.psum_scatter(value, axis, scatter_dimension=dim, tiled=True)

        col_grads = jnp.stack(
            [
                grad_pack_query,
                grad_pack_key,
                grad_pack_value,
                grad_unpack_query,
                grad_unpack_key,
                grad_unpack_value,
            ]
        )
        col_grads = scatter(col_grads, "seq", 1)
        col_grads = col_grads.reshape(6, -1, axis_head, width // axis_head).transpose(2, 0, 1, 3)
        col_grads = scatter(col_grads, "head", 0)[0].astype(F32)
        out_grads = jnp.stack([grad_pack_out, grad_unpack_out]).reshape(2, axis_head, -1, width)
        out_grads = scatter(scatter(out_grads, "seq", 2), "head", 1)[:, 0].astype(F32)
        fi_grad = scatter(grad_ffn_in, "seq", 0).reshape(-1, axis_head, ffn_in.shape[1])
        fi_grad = scatter(fi_grad.transpose(1, 0, 2), "head", 0)[0].astype(F32)
        fo_grad = scatter(grad_ffn_out.reshape(axis_head, -1, width), "seq", 1)
        fo_grad = scatter(fo_grad, "head", 0)[0].astype(F32)

        small = jnp.concatenate(
            [
                grad_ffn_out_bias,
                grad_mem_gain,
                grad_mem_bias,
                grad_attn_gain,
                grad_attn_bias,
                grad_out_gain,
                grad_out_bias,
                grad_ffn_in_bias,
            ]
        ).reshape(-1, width)
        small = lax.psum(small, ("seq", "head"))
        share = width // axis_seq
        vectors = lax.dynamic_slice_in_dim(small[:7], seq_index * share, share, 1)
        fib = mine(small[7:].reshape(axis_head, -1))
        fib = lax.dynamic_slice_in_dim(fib, seq_index * share, share, 0)
        return (
            out_tokens,
            out_memory,
            grad_tokens,
            grad_memory,
            col_grads[0],
            col_grads[1],
            col_grads[2],
            out_grads[0],
            col_grads[3],
            col_grads[4],
            col_grads[5],
            out_grads[1],
            fi_grad,
            fib,
            fo_grad,
            vectors[0],
            vectors[1],
            vectors[2],
            vectors[3],
            vectors[4],
            vectors[5],
            vectors[6],
        )

    return local


def solution(mesh):
    rows = P(None, "seq", None)
    by_col, by_row, both = P(None, "head"), P("head", None), P("seq", "head")
    wide_rows = P(("head", "seq"), None)
    in_specs = (
        (rows, rows, P())
        + (by_col, by_col, by_col, by_row)
        + (by_col, by_col, by_col, by_row)
        + (by_col, P("head"), by_row)
        + (P(),) * 7
        + (rows, rows)
    )
    out_specs = (
        (rows,) * 4
        + (both, both, both, wide_rows)
        + (both, both, both, wide_rows)
        + (both, P(("head", "seq")), wide_rows)
        + (P("seq"),) * 7
    )
    local = make_local(mesh.shape["seq"], mesh.shape["head"])
    return jax.shard_map(local, mesh=mesh, in_specs=in_specs, out_specs=out_specs, check_vma=False)
```

time: 2050 us -> 895 us (0.44)
  waiting for transfers between devices: 1650 us -> 457 us
  local copies, waits for them, and re-layouts: 94.2 us -> 145 us
  other arithmetic: 83.3 us -> 34.9 us
  blocking collectives: 59.5 us -> 98.2 us
  matrix products: 138 us -> 105 us
  starting transfers between devices: 2.08 us -> 24.4 us
    psum x6 -> x0, waiting for transfers between devices: 988 us -> none  [the longest x1 223 us: local(): attn_mix = lax.psum(project(tok_ctx_low, unpack_out), 'head')]
    reduce_scatter x10 -> x6, waiting for transfers between devices: 408 us -> 198 us  [scatter(): return lax.psum_scatter(value, axis, scatter_dimension=dim, tiled=True)]
    unnamed x30 -> x16, waiting for transfers between devices: 178 us -> 0.77 us
    all_gather x4 -> x6, waiting for transfers between devices: 72.4 us -> 212 us  [the longest x1 64.3 us: local(): grad_tokens = lax.all_gather(grad_tokens, 'head', axis=0)]
    all_gather x1 -> x3, blocking collectives: 9.09 us -> 58 us  [the longest x1 22.7 us: local(): out_memory = lax.all_gather(mem_result.astype(BF), 'head', axis=0)]
    ppermute x0 -> x24, waiting for transfers between devices: none -> 46.1 us  [swap(): return lax.ppermute(value, 'seq', [(i, i ^ step) for i in range(axis_seq)])]
    psum x0 -> x1, blocking collectives: none -> 40.2 us  [local(): small = lax.psum(small, ('seq', 'head'))]
    dot_general x42, matrix products: 138 us -> 105 us  [the longest x10 28.3 us: mm(): return jnp.dot(left, right, preferred_element_type=F32)]
  transfers between devices with their start and end apart: 25 -> 38, of which waited for: 25 -> 23; matrix products, arithmetic and copies ran while one was open for 6% -> 22% of each run, Pallas kernels for 0% -> 0%
where the time goes in v1:
time: 895 us; the launch traced here: 883 us
  waiting for transfers between devices  457 us (51%)
  local copies, waits for them, and re-layouts  145 us (16%)
  matrix products  105 us (12%)
  blocking collectives  98.2 us (11%)
  other arithmetic  34.9 us (4%)
  starting transfers between devices  24.4 us (3%)
  between operations  18.8 us (2%)
    reduce_scatter x6, waiting for transfers between devices, scatter(): return lax.psum_scatter(value, axis, scatter_dimension=dim, tiled=True)  198 us
    all_gather x1, waiting for transfers between devices, local(): grad_tokens = lax.all_gather(grad_tokens, 'head', axis=0)  64.3 us
    all_gather x1, waiting for transfers between devices, local(): out_tokens = lax.all_gather(out_result.astype(BF), 'head', axis=0)  56.2 us
    all_gather x1, waiting for transfers between devices, local(): w_fi = lax.all_gather(seq_rows(ffn_in), ('head', 'seq'), axis=0)  49.1 us
    ppermute x24, waiting for transfers between devices, swap(): return lax.ppermute(value, 'seq', [(i, i ^ step) for i in range(axis_seq)])  46.1 us
    all_gather x1, waiting for transfers between devices, local(): columns = lax.all_gather(columns, ('seq', 'head'), axis=0)  42.1 us
    psum x1, blocking collectives, local(): small = lax.psum(small, ('seq', 'head'))  40.2 us
    unnamed x243, local copies, waits for them, and re-layouts  33.2 us
  transfers between devices with their start and end apart: 38, of which 23 were waited for; matrix products, arithmetic and copies ran while one was open for 22% of the time, Pallas kernels for 0%

profile of v1, /device:TPU:0, one launch (start us, length us, event | category | flops | bytes accessed | tf_op | source)
XLA Modules:
  0.0 882.5 jit_solution(11208089255602697907)
XLA Ops:
  31.8 14.0 %all-gather.7 = f32[4,1,768]{2,1,0:T(1,128)} all-gather(f32[1,1,768]{2,1,0:T(1,128)S(1)} %reshape.349), channel_id=1, replica_groups=mesh['seq'=8,'head'=4] {'head'}, dimensions={0}, use_global_device_ids=true | all-gather | bytes 15360 | tf_op jit(solution)/shard_map/all_gather | solution.py:151
  46.7 42.1 %all-gather.17.cloned.1.call-done = bf16[3072,1152]{1,0:T(8,128)(2,1)} async-done(((bf16[96,1152]{1,0:T(8,128)(2,1)}), bf16[3072,1152]{1,0:T(8,128)(2,1)}) %all-gather.17.cloned.1.call-update) | async-done | bytes 7077904 | tf_op jit(solution)/shard_map/all_gather | solution.py:140
  88.8 10.3 %copy.320 = bf16[3072,1152]{0,1:T(8,128)(2,1)} copy(bf16[3072,1152]{1,0:T(8,128)(2,1)} %all-gather.17.cloned.1.call-done) | data formatting | bytes 14155776 | tf_op jit(solution)/shard_map/all_gather | solution.py:140
  99.1 18.2 %reshape.313 = bf16[8,4,96,6,192]{2,1,0,4,3:T(4,128)(2,1)} reshape(bf16[3072,1152]{0,1:T(8,128)(2,1)} %copy.320) | data formatting | bytes 14155776 | tf_op jit(solution)/shard_map/reshape | solution.py:141
  117.3 7.0 fusion.133
  165.0 49.1 %all-gather.21.cloned.1.call-done = bf16[3072,768]{1,0:T(8,128)(2,1)} async-done(((bf16[96,768]{1,0:T(8,128)(2,1)}), bf16[3072,768]{1,0:T(8,128)(2,1)}) %all-gather.21.cloned.1.call-update) | async-done | bytes 4718608 | tf_op jit(solution)/shard_map/all_gather | solution.py:148
  214.1 6.7 copy.334
  294.0 7.8 fusion.136
  305.2 7.2 convert_reduce_fusion
  357.5 6.8 collective-permute-done.14
  374.1 6.4 convolution_convert_fusion.1
  382.1 9.0 %convolution_convert_fusion = bf16[3072,768]{1,0:T(8,128)(2,1)} fusion(f32[512,768]{1,0:T(8,128)S(1)} %copy-done.45, f32[512,3072]{1,0:T(8,128)} %fusion.129, f32[3072]{0:T(1024)S(1)} %bitcast.406), kind=kOutput, calls=%fused_computation.20 | convolution fusion | flops 2434400256 | bytes 12595200 | tf_op jit(solution)/shard_map/dot_general | solution.py:43
  400.5 7.8 collective-permute-done.16
  442.5 39.3 %reduce-scatter.15.cloned.1.call-done = bf16[96,3072]{1,0:T(8,128)(2,1)} async-done(((bf16[768,3072]{1,0:T(8,128)(2,1)}), bf16[96,3072]{1,0:T(8,128)(2,1)}) %reduce-scatter.15.cloned.1.call-update) | async-done | bytes 589840 | tf_op jit(solution)/shard_map/reduce_scatter | solution.py:346
  485.8 53.3 %reduce-scatter.19.cloned.1.call-done = bf16[4,96,768]{2,1,0:T(8,128)(2,1)} async-done(((bf16[4,768,768]{2,1,0:T(8,128)(2,1)}), bf16[4,96,768]{2,1,0:T(8,128)(2,1)}) %reduce-scatter.19.cloned.1.call-update) | async-done | bytes 589840 | tf_op jit(solution)/shard_map/reduce_scatter | solution.py:346
  539.9 40.2 %psum.7 = f32[11,768]{1,0:T(8,128)S(1)} all-reduce(f32[11,768]{1,0:T(8,128)S(1)} %reshape.336), channel_id=1, replica_groups=mesh['seq'=8,'head'=4] {'seq','head'}, use_global_device_ids=true, to_apply=%region_34.35 | all-reduce | flops 8448 | bytes 67584 | tf_op jit(solution)/shard_map/psum | solution.py:380
  584.8 32.6 %reduce-scatter.11.cloned.1.call-done = bf16[6,96,768]{2,1,0:T(8,128)(2,1)} async-done(((bf16[6,768,768]{2,1,0:T(8,128)(2,1)}), bf16[6,96,768]{2,1,0:T(8,128)(2,1)}) %reduce-scatter.11.cloned.1.call-update) | async-done | bytes 884752 | tf_op jit(solution)/shard_map/reduce_scatter | solution.py:346
  623.4 22.7 %all-gather.4 = bf16[512,768]{1,0:T(8,128)(2,1)S(1)} all-gather(bf16[128,768]{1,0:T(8,128)(2,1)S(1)} %get-tuple-element.76), channel_id=6, replica_groups=mesh['seq'=8,'head'=4] {'head'}, dimensions={0}, use_global_device_ids=true | all-gather | bytes 983040 | tf_op jit(solution)/shard_map/all_gather | solution.py:285
  646.1 21.2 %all-gather.6 = bf16[512,768]{1,0:T(8,128)(2,1)S(1)} all-gather(bf16[128,768]{1,0:T(8,128)(2,1)S(1)} %get-tuple-element.75), channel_id=8, replica_groups=mesh['seq'=8,'head'=4] {'head'}, dimensions={0}, use_global_device_ids=true | all-gather | bytes 983040 | tf_op jit(solution)/shard_map/all_gather | solution.py:340
  669.5 56.2 %all-gather.23.cloned.1.call-done = bf16[2048,768]{1,0:T(8,128)(2,1)} async-done(((bf16[512,768]{1,0:T(8,128)(2,1)}), bf16[2048,768]{1,0:T(8,128)(2,1)}) %all-gather.23.cloned.1.call-update) | async-done | bytes 3145744 | tf_op jit(solution)/shard_map/all_gather | solution.py:284
  725.7 64.3 %all-gather.25.cloned.1.call-done = bf16[2048,768]{1,0:T(8,128)(2,1)} async-done(((bf16[512,768]{1,0:T(8,128)(2,1)}), bf16[2048,768]{1,0:T(8,128)(2,1)}) %all-gather.25.cloned.1.call-update) | async-done | bytes 3145744 | tf_op jit(solution)/shard_map/all_gather | solution.py:337
  790.0 23.3 %reduce-scatter.17.cloned.1.call-done = bf16[1,96,768]{2,1,0:T(8,128)(2,1)} async-done(((bf16[4,96,768]{2,1,0:T(8,128)(2,1)}), bf16[1,96,768]{2,1,0:T(8,128)(2,1)}) %reduce-scatter.17.cloned.1.call-update) | async-done | bytes 147472 | tf_op jit(solution)/shard_map/reduce_scatter | solution.py:346
  815.0 21.0 %reduce-scatter.21.cloned.1.call-done = bf16[1,96,768]{2,1,0:T(8,128)(2,1)} async-done(((bf16[4,96,768]{2,1,0:T(8,128)(2,1)}), bf16[1,96,768]{2,1,0:T(8,128)(2,1)}) %reduce-scatter.21.cloned.1.call-update) | async-done | bytes 147472 | tf_op jit(solution)/shard_map/reduce_scatter | solution.py:346
  837.7 28.7 %reduce-scatter.13.cloned.1.call-done = bf16[1,6,96,192]{3,2,1,0:T(8,128)(2,1)} async-done(((bf16[4,6,96,192]{3,2,1,0:T(8,128)(2,1)}), bf16[1,6,96,192]{3,2,1,0:T(8,128)(2,1)}) %reduce-scatter.13.cloned.1.call-update) | async-done | bytes 221200 | tf_op jit(solution)/shard_map/reduce_scatter | solution.py:346
  (487 shorter events, 268.4 us)
Async XLA Ops:
  7.2 81.5 %all-gather.17.cloned.1.call-start = ((), (), s32[]{:S(2)}) async-start(), calls=%async_computation.14 | async-start | bytes 7299072 | tf_op jit(solution)/shard_map/all_gather | solution.py:140
  12.0 150.1 %all-gather.19.cloned.1.call-start = ((), (), s32[]{:S(2)}) async-start(), calls=%async_computation.15 | async-start | bytes 2433024 | tf_op jit(solution)/shard_map/all_gather | solution.py:145
  13.6 200.5 %all-gather.21.cloned.1.call-start = ((), (), s32[]{:S(2)}) async-start(), calls=%async_computation.16 | async-start | bytes 4866048 | tf_op jit(solution)/shard_map/all_gather | solution.py:148
  14.3 279.6 %all-gather.15.cloned.1.call-start = ((), (), s32[]{:S(2)}) async-start(), calls=%async_computation.7 | async-start | bytes 4866048 | tf_op jit(solution)/shard_map/all_gather | solution.py:150
  29.4 16.5 %collective-permute-start.3 = (bf16[128,768]{1,0:T(8,128)(2,1)S(1)}, bf16[128,768]{1,0:T(8,128)(2,1)S(1)}, u32[]{:S(2)}, u32[]{:S(2)}) collective-permute-start(bf16[128,768]{1,0:T(8,128)(2,1)S(1)} %select_select_fusion.2), channel_id=1, source_target_pairs={{0,4},{4,0},{8,12},{12,8},{16,20},{20,16},{24,28},{28,24},{1,5},{5... | collective-permute-start | bytes 589832 | tf_op jit(solution)/shard_map/ppermute | solution.py:84
  31.1 402.7 %reduce-scatter.23.cloned.1.call-start = ((), (), s32[]{:S(2)}) async-start(), calls=%async_computation.19 | async-start | bytes 2654208
  161.9 65.5 %collective-permute-start.4 = (bf16[128,896]{0,1:T(8,128)(2,1)S(1)}, bf16[128,896]{0,1:T(8,128)(2,1)}, u32[]{:S(2)}, u32[]{:S(2)}) collective-permute-start(bf16[128,896]{0,1:T(8,128)(2,1)S(1)} %get-tuple-element.74), channel_id=1, source_target_pairs={{0,4},{4,0},{8,12},{12,8},{16,20},{20,16},{24,28},{28,24},{1,5},{5... | collective-permute-start | bytes 688136 | tf_op jit(solution)/shard_map/ppermute | solution.py:84
  230.7 17.5 %collective-permute-start.7 = (bf16[128,896]{0,1:T(8,128)(2,1)}, bf16[128,896]{0,1:T(8,128)(2,1)}, u32[]{:S(2)}, u32[]{:S(2)}) collective-permute-start(bf16[128,896]{0,1:T(8,128)(2,1)} %get-tuple-element.85), channel_id=1, source_target_pairs={{0,24},{4,28},{8,16},{12,20},{16,8},{20,12},{24,0},{28,4},{1,25},{... | collective-permute-start | bytes 688136 | tf_op jit(solution)/shard_map/ppermute | solution.py:84
  258.3 16.4 %collective-permute-start.8 = (bf16[128,768]{1,0:T(8,128)(2,1)S(1)}, bf16[128,768]{1,0:T(8,128)(2,1)S(1)}, u32[]{:S(2)}, u32[]{:S(2)}) collective-permute-start(bf16[128,768]{1,0:T(8,128)(2,1)S(1)} %get-tuple-element.79), channel_id=1, source_target_pairs={{0,24},{4,28},{8,16},{12,20},{16,8},{20,12},{24,0},{28,4},{1,25},{... | collective-permute-start | bytes 589832 | tf_op jit(solution)/shard_map/ppermute | solution.py:84
  259.7 15.0 %collective-permute-start.9 = (bf16[128,768]{1,0:T(8,128)(2,1)S(1)}, bf16[128,768]{1,0:T(8,128)(2,1)S(1)}, u32[]{:S(2)}, u32[]{:S(2)}) collective-permute-start(bf16[128,768]{1,0:T(8,128)(2,1)S(1)} %get-tuple-element.79), channel_id=1, source_target_pairs={{0,16},{4,20},{8,24},{12,28},{16,0},{20,4},{24,8},{28,12},{1,17},{... | collective-permute-start | bytes 589832 | tf_op jit(solution)/shard_map/ppermute | solution.py:84
  372.8 109.0 %reduce-scatter.15.cloned.1.call-start = ((), (), s32[]{:S(2)}) async-start(), calls=%async_computation.10 | async-start | bytes 5308416 | tf_op jit(solution)/shard_map/reduce_scatter | solution.py:346
  380.6 158.5 %reduce-scatter.19.cloned.1.call-start = ((), (), s32[]{:S(2)}) async-start(), calls=%async_computation.12 | async-start | bytes 5308416 | tf_op jit(solution)/shard_map/reduce_scatter | solution.py:346
  391.1 226.3 %reduce-scatter.11.cloned.1.call-start = ((), (), s32[]{:S(2)}) async-start(), calls=%async_computation.8 | async-start | bytes 7962624 | tf_op jit(solution)/shard_map/reduce_scatter | solution.py:346
  399.4 12.4 %collective-permute-start.17 = (bf16[128,896]{0,1:T(8,128)(2,1)S(1)}, bf16[128,896]{0,1:T(8,128)(2,1)S(1)}, u32[]{:S(2)}, u32[]{:S(2)}) collective-permute-start(bf16[128,896]{0,1:T(8,128)(2,1)S(1)} %concatenate.34), channel_id=1, source_target_pairs={{0,16},{4,20},{8,24},{12,28},{16,0},{20,4},{24,8},{28,12},{1,17},{... | collective-permute-start | bytes 688136 | tf_op jit(solution)/shard_map/ppermute | solution.py:84
  433.8 233.5 %all-reduce.3.cloned.1.call-start = ((), (), s32[]{:S(2)}) async-start(), calls=%async_computation.20 | async-start | bytes 589824
  435.9 289.8 %all-gather.23.cloned.1.call-start = ((), (), s32[]{:S(2)}) async-start(), calls=%async_computation.17 | async-start | bytes 3932160 | tf_op jit(solution)/shard_map/all_gather | solution.py:284
  436.5 353.5 %all-gather.25.cloned.1.call-start = ((), (), s32[]{:S(2)}) async-start(), calls=%async_computation.18 | async-start | bytes 3932160 | tf_op jit(solution)/shard_map/all_gather | solution.py:337
  442.4 370.9 %reduce-scatter.17.cloned.1.call-start = ((), (), s32[]{:S(2)}) async-start(), calls=%async_computation.11 | async-start | bytes 737280 | tf_op jit(solution)/shard_map/reduce_scatter | solution.py:346
  483.7 352.3 %reduce-scatter.21.cloned.1.call-start = ((), (), s32[]{:S(2)}) async-start(), calls=%async_computation.13 | async-start | bytes 737280 | tf_op jit(solution)/shard_map/reduce_scatter | solution.py:346
  539.1 327.2 %reduce-scatter.13.cloned.1.call-start = ((), (), s32[]{:S(2)}) async-start(), calls=%async_computation.9 | async-start | bytes 1474560 | tf_op jit(solution)/shard_map/reduce_scatter | solution.py:346
  539.8 40.4 %collective-permute-start.20 = (bf16[128,768]{1,0:T(8,128)(2,1)S(1)}, bf16[128,768]{1,0:T(8,128)(2,1)S(1)}, u32[]{:S(2)}, u32[]{:S(2)}) collective-permute-start(bf16[128,768]{1,0:T(8,128)(2,1)S(1)} %broadcast_select_fusion.14), channel_id=1, source_target_pairs={{0,4},{4,0},{8,12},{12,8},{16,20},{20,16},{24,28},{28,24},{1,5},{5... | collective-permute-start | bytes 589832 | tf_op jit(solution)/shard_map/ppermute | solution.py:84
  580.3 41.8 %collective-permute-start.22 = (bf16[128,768]{1,0:T(8,128)(2,1)S(1)}, bf16[128,768]{1,0:T(8,128)(2,1)S(1)}, u32[]{:S(2)}, u32[]{:S(2)}) collective-permute-start(bf16[128,768]{1,0:T(8,128)(2,1)S(1)} %get-tuple-element.88), channel_id=1, source_target_pairs={{0,16},{4,20},{8,24},{12,28},{16,0},{20,4},{24,8},{28,12},{1,17},{... | collective-permute-start | bytes 589832 | tf_op jit(solution)/shard_map/ppermute | solution.py:84
  582.7 39.4 %collective-permute-start.23 = (bf16[128,768]{1,0:T(8,128)(2,1)S(1)}, bf16[128,768]{1,0:T(8,128)(2,1)S(1)}, u32[]{:S(2)}, u32[]{:S(2)}) collective-permute-start(bf16[128,768]{1,0:T(8,128)(2,1)S(1)} %get-tuple-element.89), channel_id=1, source_target_pairs={{0,24},{4,28},{8,16},{12,20},{16,8},{20,12},{24,0},{28,4},{1,25},{... | collective-permute-start | bytes 589832 | tf_op jit(solution)/shard_map/ppermute | solution.py:84
  584.1 38.0 %collective-permute-start.21 = (bf16[128,768]{1,0:T(8,128)(2,1)S(1)}, bf16[128,768]{1,0:T(8,128)(2,1)}, u32[]{:S(2)}, u32[]{:S(2)}) collective-permute-start(bf16[128,768]{1,0:T(8,128)(2,1)S(1)} %get-tuple-element.34), channel_id=1, source_target_pairs={{0,8},{4,12},{8,0},{12,4},{16,24},{20,28},{24,16},{28,20},{1,9},{5... | collective-permute-start | bytes 589832 | tf_op jit(solution)/shard_map/ppermute | solution.py:84
  (124 other events, 1319.9 us)
Sparse Core Ops, SparseCore 0:
  12.2 76.5 all-gather.16
  92.2 55.7 all-gather.18
  151.5 62.4 all-gather.20
  216.8 70.3 all-gather.14
  372.9 51.1 reduce-scatter.22
  427.8 53.9 reduce-scatter.14
  485.2 53.8 reduce-scatter.18
  543.0 74.3 reduce-scatter.10
  620.3 40.4 all-reduce.2
  662.8 62.8 all-gather.22
  727.8 62.1 all-gather.24
  792.7 20.5 reduce-scatter.16
  815.6 20.3 reduce-scatter.20
  838.8 27.5 reduce-scatter.12

commit v2 on v1

--- a/solution.py
+++ b/solution.py
@@ -123,32 +123,71 @@
             size = value.shape[0] // axis_seq
             return lax.dynamic_slice_in_dim(value, seq_index * size, size, 0)
 
-        columns = jnp.concatenate(
-            [
-                seq_rows(w)
-                for w in (
-                    pack_query,
-                    pack_key,
-                    pack_value,
-                    unpack_query,
-                    unpack_key,
-                    unpack_value,
+        role = seq_index % 2
+        quad = (seq_index // 2) % 4
+        first_step = jnp.where(role == 0, 1, 2)
+        second_step = 3 - first_step
+
+        def cross(value, order):
+            pairs = [(i, i ^ (2 * ((1, 2) if i % 2 == order else (2, 1))[0])) for i in range(axis_seq)]
+            return lax.ppermute(value, "seq", pairs)
+
+        def from_planes(value):
+            got = [value]
+            for j in range(1, axis_head):
+                pairs = [(i, (i - j) % axis_head) for i in range(axis_head)]
+                got.append(lax.ppermute(value, "head", pairs))
+            stacked = jnp.stack(got)
+            return jnp.roll(stacked, head_index, axis=0)
+
+        def by_role(zero, one):
+            return jnp.where(role == 0, zero, one)
+
+        def quad_rows(value):
+            size = value.shape[0] // 4
+            return lax.dynamic_slice_in_dim(value, quad * size, size, 0)
+
+        def spread_weights(piece):
+            first = cross(piece, 0)
+            second = cross(piece, 1)
+            third = cross(first, 1)
+            mine_set = [piece, first, second, third]
+            steps = [0, first_step, second_step, 3]
+            mats, rows, cols = piece.shape
+            buffer = jnp.zeros((2, mats, 4, rows, cols), piece.dtype)
+            for part, step in zip(mine_set, steps):
+                buffer = lax.dynamic_update_slice(
+                    buffer, part[None, :, None], (role, 0, quad ^ step, 0, 0)
                 )
-            ],
-            axis=1,
-        )
-        columns = lax.all_gather(columns, ("seq", "head"), axis=0)
-        columns = columns.reshape(axis_seq, axis_head, -1, 6, width // axis_head)
-        columns = columns.transpose(3, 0, 2, 1, 4).reshape(6, width, width)
-        w_pq, w_pk, w_pv, w_uq, w_uk, w_uv = [columns[i] for i in range(6)]
-        outs = jnp.stack([seq_rows(pack_out), seq_rows(unpack_out)])
-        outs = lax.all_gather(outs, ("head", "seq"), axis=0)
-        outs = outs.transpose(1, 0, 2, 3).reshape(2, width, width)
-        w_po, w_uo = outs[0], outs[1]
-        w_fi = lax.all_gather(seq_rows(ffn_in), ("head", "seq"), axis=0)
-        w_fi = w_fi.reshape(axis_head, width, -1).transpose(1, 0, 2).reshape(width, -1)
-        w_fo = lax.all_gather(seq_rows(ffn_out), ("head", "seq"), axis=0, tiled=True)
-        b_fi = lax.all_gather(ffn_in_bias, "head", axis=0, tiled=True)
+            for part, step in zip(mine_set, [0, second_step, first_step, 3]):
+                buffer = lax.dynamic_update_slice(
+                    buffer, swap(part, 1)[None, :, None], (1 - role, 0, quad ^ step, 0, 0)
+                )
+            return buffer.reshape(2, mats, 4 * rows, cols)
+
+        def attention_piece(key_w, value_w, query_w, out_w):
+            size = out_w.shape[1] // 4
+            out_t = lax.dynamic_slice_in_dim(out_w, quad * size, size, 1).T
+            zero = jnp.concatenate([quad_rows(key_w), quad_rows(value_w)], axis=1)
+            one = jnp.concatenate([quad_rows(query_w), out_t], axis=1)
+            planes = from_planes(by_role(zero, one))
+            rows = planes.shape[1]
+            planes = planes.reshape(axis_head, rows, 2, -1)
+            return planes.transpose(2, 1, 0, 3).reshape(2, rows, -1)
+
+        w_pack = spread_weights(attention_piece(pack_key, pack_value, pack_query, pack_out))
+        w_un = spread_weights(attention_piece(unpack_key, unpack_value, unpack_query, unpack_out))
+        bias_rows = jnp.stack(parts_of(ffn_in_bias) + [jnp.zeros(ffn_in_bias.shape, BF)] * 13)
+        ffn_piece = by_role(quad_rows(ffn_in), quad_rows(ffn_out))
+        ffn_piece = from_planes(jnp.concatenate([ffn_piece, bias_rows]))
+        split = ffn_piece.shape[1] - 16
+        bias_all = ffn_piece[:, split : split + 3].astype(F32)
+        b_fi = (bias_all[:, 0] + bias_all[:, 1] + bias_all[:, 2]).reshape(-1)
+        w_ffn = spread_weights(ffn_piece[:, :split])
+        w_pk, w_pv, w_pq, w_po = w_pack[0, 0], w_pack[0, 1], w_pack[1, 0], w_pack[1, 1]
+        w_uk, w_uv, w_uq, w_uo = w_un[0, 0], w_un[0, 1], w_un[1, 0], w_un[1, 1]
+        w_fi = w_ffn[0].transpose(1, 0, 2).reshape(width, -1)
+        w_fo = w_ffn[1].reshape(-1, width)
 
         tok = mine(tokens)
         mem = mine(memory)
@@ -257,7 +296,7 @@
         blended = deliver(with_scalars(ctx_here, [lse_here]), empty, blend)
         pack_ctx = blended[:, :width]
         pack_lse = scalars_in(blended, 0)
-        mem_mix = mm(pack_ctx, w_po)
+        mem_mix = mm_t(pack_ctx, w_po)
         mem_result, mem_normed, mem_inv = norm_forward(mem_mix + mem_f32, mem_gain, mem_bias)
         mix_low = mem_mix.astype(BF)
         mix_slot = fetch(mix_low)
@@ -272,7 +311,7 @@
         tok_num = flat(ein("htr,rhd->thd", tok_weights.astype(BF), heads_of(v_un)))
         tok_ctx = tok_num * wide(tok_inv)
         tok_ctx_low = tok_ctx.astype(BF)
-        attn_mix = mm(tok_ctx_low, w_uo)
+        attn_mix = mm_t(tok_ctx_low, w_uo)
         attn_result, attn_normed, attn_inv = norm_forward(attn_mix + tok_f32, attn_gain, attn_bias)
 
         attn_low = attn_result.astype(BF)
@@ -281,8 +320,9 @@
         gelu_low = gelu_out.astype(BF)
         ffn_mix = mm(gelu_low, w_fo) + ffn_out_bias
         out_result, out_normed, out_inv = norm_forward(ffn_mix + attn_result, out_gain, out_bias)
-        out_tokens = lax.all_gather(out_result.astype(BF), "head", axis=0)
-        out_memory = lax.all_gather(mem_result.astype(BF), "head", axis=0)
+        outs = jnp.concatenate([out_result.astype(BF), mem_result.astype(BF)])
+        outs = lax.all_gather(outs, "head", axis=0)
+        out_tokens, out_memory = outs[:, :block_len], outs[:, block_len:]
 
         grad_sum, grad_out_gain, grad_out_bias = norm_backward(
             cot_tok, out_normed, out_inv, out_gain
@@ -300,7 +340,7 @@
 
         mix_grad = grad_mixsum.astype(BF)
         grad_unpack_out = t_mm(tok_ctx_low, mix_grad).astype(BF)
-        ctx_grad = mm_t(mix_grad, w_uo)
+        ctx_grad = mm(mix_grad, w_uo)
         num_grad = (ctx_grad * wide(tok_inv)).astype(BF)
         den_grad = -tok_inv * jnp.sum(heads_of(ctx_grad * tok_ctx), axis=2)
         tok_dweights = ein("thd,rhd->htr", heads_of(num_grad), heads_of(v_un)) + den_grad.T[:, :, None]
@@ -319,7 +359,7 @@
         )
         mem_mix_grad = (grad_memsum + mix_total.astype(F32)).astype(BF)
         grad_pack_out = t_mm(pack_ctx, mem_mix_grad).astype(BF)
-        pctx_grad = mm_t(mem_mix_grad, w_po)
+        pctx_grad = mm(mem_mix_grad, w_po)
         delta = jnp.sum(heads_of(pctx_grad * pack_ctx.astype(F32)), axis=2)
         back = fetch(with_scalars(pctx_grad.astype(BF), [pack_lse, delta]))
         pctx_slot = back[:, :width]
@@ -334,37 +374,89 @@
         pv_grad = flat(ein("hrt,rhd->thd", weights_back.astype(BF), heads_of(pctx_slot))).astype(BF)
         tok_part = mm_t(pk_grad, w_pk) + mm_t(pv_grad, w_pv) + mm_t(uq_grad, w_uq)
         grad_tokens = (tok_part + grad_mixsum).astype(BF)
-        grad_tokens = lax.all_gather(grad_tokens, "head", axis=0)
         mem_part = deliver(mm_t(pq_part, w_pq).astype(BF), jnp.zeros((), BF), sum_rows)
         grad_memory = (mem_part.astype(F32) + grad_memsum).astype(BF)
-        grad_memory = lax.all_gather(grad_memory, "head", axis=0)
+        grads = jnp.concatenate([grad_tokens, grad_memory])
+        grads = lax.all_gather(grads, "head", axis=0)
+        grad_tokens, grad_memory = grads[:, :block_len], grads[:, block_len:]
         grad_pack_query = t_mm(mem_slot, pq_part).astype(BF)
         grad_pack_key = t_mm(tok, pk_grad).astype(BF)
         grad_pack_value = t_mm(tok, pv_grad).astype(BF)
 
-        def scatter(value, axis, dim):
-            return lax.psum_scatter(value, axis, scatter_dimension=dim, tiled=True)
-
-        col_grads = jnp.stack(
-            [
-                grad_pack_query,
-                grad_pack_key,
-                grad_pack_value,
-                grad_unpack_query,
-                grad_unpack_key,
-                grad_unpack_value,
-            ]
+        def pick(value, index):
+            return lax.dynamic_index_in_dim(value, index, 0, keepdims=False)
+
+        def plane_sum(grads):
+            keep, send = pick(grads, role), pick(grads, 1 - role)
+            total = sum_rows([keep, swap(send, 1)])
+            mats, rows, cols = total.shape
+            blocks = total.reshape(mats, 4, rows // 4, cols).transpose(1, 0, 2, 3)
+            low, high = quad % 2, quad // 2
+
+            def pair(bit):
+                zero = by_role(bit, 2 * bit)
+                one = by_role(2 + bit, 2 * bit + 1)
+                return jnp.stack([pick(blocks, zero), pick(blocks, one)])
+
+            bit = by_role(low, high)
+            blocks = sum_rows([pair(bit), cross(pair(1 - bit), 0)])
+            bit = by_role(high, low)
+            return sum_rows([pick(blocks, bit), cross(pick(blocks, 1 - bit), 1)])
+
+        def head_sum(blocks):
+            total = mine(blocks).astype(F32)
+            for j in range(1, axis_head):
+                pairs = [(i, (i + j) % axis_head) for i in range(axis_head)]
+                block = pick(blocks, (head_index + j) % axis_head)
+                total = total + lax.ppermute(block, "head", pairs).astype(F32)
+            return total
+
+        def own_rows(total):
+            half = total.shape[1] // 2
+            keep = lax.dynamic_slice_in_dim(total, role * half, half, 1)
+            send = lax.dynamic_slice_in_dim(total, (1 - role) * half, half, 1)
+            other = swap(send, 1)
+            return by_role(keep, other), by_role(other, keep)
+
+        head_cols = width // axis_head
+
+        groups = axis_seq // 8
+        peers = [[g * 8 + low for g in range(groups)] for low in range(8)]
+
+        def group_sum(value):
+            if groups == 1:
+                return value[0]
+            return lax.psum_scatter(
+                value, "seq", scatter_dimension=0, tiled=False, axis_index_groups=peers
+            )
+
+        def out_rows(grad):
+            blocks = grad.reshape(axis_head, groups * 4, -1, width)
+            return blocks.transpose(1, 0, 2, 3).reshape(width, width)
+
+        def attention_grads(key_g, value_g, query_g, out_g):
+            grads = jnp.stack([key_g, value_g, query_g, out_rows(out_g)])
+            grads = grads.reshape(2, 2, groups, -1, width).transpose(2, 0, 1, 3, 4)
+            total = plane_sum(group_sum(grads))
+            rows = total.shape[1]
+            by_cols = total.reshape(2, rows, axis_head, head_cols).transpose(2, 0, 1, 3)
+            as_rows = total[1].reshape(axis_head, rows, head_cols)
+            second = by_role(by_cols[:, 1], as_rows)
+            total = head_sum(jnp.stack([by_cols[:, 0], second], axis=1))
+            zero, one = own_rows(total)
+            return zero[0], zero[1], one[0], one[1].reshape(-1, width)
+
+        un_grads = attention_grads(
+            grad_unpack_key, grad_unpack_value, grad_unpack_query, grad_unpack_out
         )
-        col_grads = scatter(col_grads, "seq", 1)
-        col_grads = col_grads.reshape(6, -1, axis_head, width // axis_head).transpose(2, 0, 1, 3)
-        col_grads = scatter(col_grads, "head", 0)[0].astype(F32)
-        out_grads = jnp.stack([grad_pack_out, grad_unpack_out]).reshape(2, axis_head, -1, width)
-        out_grads = scatter(scatter(out_grads, "seq", 2), "head", 1)[:, 0].astype(F32)
-        fi_grad = scatter(grad_ffn_in, "seq", 0).reshape(-1, axis_head, ffn_in.shape[1])
-        fi_grad = scatter(fi_grad.transpose(1, 0, 2), "head", 0)[0].astype(F32)
-        fo_grad = scatter(grad_ffn_out.reshape(axis_head, -1, width), "seq", 1)
-        fo_grad = scatter(fo_grad, "head", 0)[0].astype(F32)
-
+        pack_grads = attention_grads(grad_pack_key, grad_pack_value, grad_pack_query, grad_pack_out)
+        fi_blocks = grad_ffn_in.reshape(width, axis_head, -1).transpose(1, 0, 2)
+        fo_blocks = grad_ffn_out.reshape(axis_head, -1, width)
+        ffn_blocks = jnp.stack([fi_blocks, fo_blocks])
+        ffn_blocks = ffn_blocks.reshape(2, axis_head, groups, -1, ffn_in.shape[1])
+        ffn_total = head_sum(plane_sum(group_sum(ffn_blocks.transpose(2, 0, 1, 3, 4))))
+        fi_grad, fo_grad = own_rows(ffn_total[None])
+        fi_grad, fo_grad = fi_grad[0], fo_grad[0]
         small = jnp.concatenate(
             [
                 grad_ffn_out_bias,
@@ -377,7 +469,15 @@
                 grad_ffn_in_bias,
             ]
         ).reshape(-1, width)
-        small = lax.psum(small, ("seq", "head"))
+        step = 1
+        while step < axis_seq:
+            small = small + swap(small, step)
+            step *= 2
+        vector_total = small
+        for j in range(1, axis_head):
+            pairs = [(i, (i + j) % axis_head) for i in range(axis_head)]
+            vector_total = vector_total + lax.ppermute(small, "head", pairs)
+        small = vector_total
         share = width // axis_seq
         vectors = lax.dynamic_slice_in_dim(small[:7], seq_index * share, share, 1)
         fib = mine(small[7:].reshape(axis_head, -1))
@@ -387,14 +487,14 @@
             out_memory,
             grad_tokens,
             grad_memory,
-            col_grads[0],
-            col_grads[1],
-            col_grads[2],
-            out_grads[0],
-            col_grads[3],
-            col_grads[4],
-            col_grads[5],
-            out_grads[1],
+            pack_grads[2],
+            pack_grads[0],
+            pack_grads[1],
+            pack_grads[3],
+            un_grads[2],
+            un_grads[0],
+            un_grads[1],
+            un_grads[3],
             fi_grad,
             fib,
             fo_grad,

time: 895 us -> 619 us (0.69)
  the two profiles are of different devices: /device:TPU:0 before, /device:TPU:11 now
where the time goes in v2:
time: 619 us; the launch traced here: 609 us
  local copies, waits for them, and re-layouts  161 us (26%)
  waiting for transfers between devices  143 us (23%)
  starting transfers between devices  111 us (18%)
  matrix products  106 us (17%)
  other arithmetic  69.4 us (11%)
  between operations  19.4 us (3%)
    ppermute x9, waiting for transfers between devices, head_sum(): total = total + lax.ppermute(block, 'head', pairs).astype(F32)  75.1 us
    ppermute x45, starting transfers between devices, swap(): return lax.ppermute(value, 'seq', [(i, i ^ step) for i in range(axis_seq)])  67 us
    ppermute x45, waiting for transfers between devices, swap(): return lax.ppermute(value, 'seq', [(i, i ^ step) for i in range(axis_seq)])  39.7 us
    dot_general x10, matrix products, mm(): return jnp.dot(left, right, preferred_element_type=F32)  31 us
    dot_general x12, matrix products, ein(): return jnp.einsum(pattern, left, right, preferred_element_type=F32)  29.2 us
    dot_general x10, matrix products, mm_t(): lax.dot_general(left, right, (((1,), (1,)), ((), ())), preferred_element_...  27.9 us
    ppermute x15, waiting for transfers between devices, cross(): return lax.ppermute(value, 'seq', pairs)  22.1 us
    convert_element_type x9, other arithmetic, sum_rows(): return total.astype(BF)  19.1 us
  transfers between devices with their start and end apart: 83, of which 28 were waited for; matrix products, arithmetic and copies ran while one was open for 38% of the time, Pallas kernels for 0%

profile of v2, /device:TPU:11, one launch (start us, length us, event | category | flops | bytes accessed | tf_op | source)
XLA Modules:
  0.0 609.4 jit_solution(14186952733117907251)
XLA Ops:
  36.2 5.6 collective-permute-done.23
  66.4 5.2 collective-permute-start.6
  80.1 4.6 broadcast_in_dim.213
  101.4 8.9 %collective-permute-done.5 = bf16[2,192,768]{2,1,0:T(8,128)(2,1)S(1)} collective-permute-done((bf16[2,192,768]{2,1,0:T(8,128)(2,1)S(1)}, bf16[2,192,768]{2,1,0:T(8,128)(2,1)S(1)}, u32[]{:S(2)}, u32[]{:S(2)}) %collective-permute-start.5) | collective-permute-done | bytes 589856 | tf_op jit(solution)/shard_map/ppermute | solution.py:133
  191.9 5.0 collective-permute-done.20
  228.1 8.4 %fusion.179 = (bf16[1,4,4,192,768]{4,3,2,1,0:T(8,128)(2,1)}, bf16[1,4,4,192,768]{4,3,2,1,0:T(8,128)(2,1)}) fusion(bf16[2,4,4,192,768]{4,3,2,1,0:T(8,128)(2,1)} %bitcast_dynamic-update-slice_fusion.7), kind=kLoop, calls=%fused_computation.521 | loop fusion | bytes 18874368 | tf_op jit(solution)/shard_map/slice | solution.py:189
  236.5 6.6 %copy.434 = bf16[768,4,768]{0,2,1:T(8,128)(2,1)} copy(bf16[768,4,768]{2,0,1:T(8,128)(2,1)} %bitcast.572) | data formatting | bytes 9437184 | tf_op jit(solution)/shard_map/transpose | solution.py:189
  243.2 5.8 fusion.175
  256.1 6.7 %convert_reduce_fusion = (f32[3072]{0:T(1024)S(1)}, bf16[512,3072]{1,0:T(8,128)(2,1)S(1)}) fusion(f32[512,3072]{1,0:T(8,128)S(1)} %fusion.175, f32[3072]{0:T(1024)S(1)} %bitcast.646, bf16[3072,768]{1,0:T(8,128)(2,1)S(1)} %bitcast.600, f32[512,768]{1,0:T(8,128)S(1)} %get-tuple-element.34), kind=kOutput, calls=%fused_computation.15 | convolution fusion | flops 2452485120 | bytes 15753216 | tf_op jit(solution)/shard_map/dot_general | solution.py:39
  277.1 4.7 multiply_convert_fusion.1
  292.0 5.6 convolution_convert_fusion
  303.7 7.6 %concatenate.137 = bf16[128,896]{0,1:T(8,128)(2,1)} concatenate(bf16[128,768]{0,1:T(8,128)(2,1)S(1)} %get-tuple-element.101, bf16[128,12]{0,1:T(8,128)(2,1)S(1)} %get-tuple-element.144, bf16[128,12]{0,1:T(8,128)(2,1)S(1)} %get-tuple-element.143, bf16[128,12]{0,1:T(8,128)(2,1)S(1)} %get-tuple-element.37, bf16[128,12]{0,1:T(8,128)(2,1)S(1)} %get-tuple-element.142, ...), dimensions={1} | concatenate | bytes 458752 | tf_op jit(solution)/shard_map/concatenate | solution.py:251
  314.0 6.5 %convolution_convert_fusion.1 = bf16[768,3072]{1,0:T(8,128)(2,1)} fusion(bf16[512,3072]{1,0:T(8,128)(2,1)} %copy-done.81, f32[512,768]{1,0:T(8,128)S(1)} %copy-done.23, f32[768]{0:T(1024)S(1)} %copy-done.79, f32[768]{0:T(1024)S(1)} %copy-done.75, f32[512]{0:T(512)S(1)} %add_rsqrt_fusion.1, f32[512]{0:T(512)S(1)} %broadcast_multiply_fusion.5), kind=kOutput, calls=%fused_computation.27 | convolution fusion | flops 2420244480 | bytes 9447424 | tf_op jit(solution)/shard_map/dot_general | solution.py:43
  320.5 8.1 %copy.459 = bf16[1,4,768,768]{3,1,2,0:T(4,128)(2,1)} copy(bf16[1,4,768,768]{3,2,1,0:T(8,128)(2,1)} %bitcast.590) | data formatting | bytes 9437184 | tf_op jit(solution)/shard_map/stack;reshape | solution.py:455
  328.6 9.9 %reshape.490 = bf16[768,4,768]{2,1,0:T(4,128)(2,1)} reshape(bf16[768,3072]{1,0:T(8,128)(2,1)} %convolution_convert_fusion.1) | data formatting | bytes 9437184 | tf_op jit(solution)/shard_map/reshape | solution.py:453
  364.9 5.5 collective-permute-done.52
  374.4 10.5 %fusion.12 = bf16[4,768,768]{2,0,1:T(4,128)(2,1)} fusion(s32[]{:T(128)S(6)} %select_n.558, bf16[1,4,768,768]{3,1,2,0:T(4,128)(2,1)} %bitcast.563, bf16[1,4,768,768]{3,1,2,0:T(4,128)(2,1)} %copy.459), kind=kLoop, calls=%fused_computation.30 | loop fusion | flops 2359296 | bytes 14155780 | tf_op jit(solution)/shard_map/jit(dynamic_index_in_dim)/squeeze | solution.py:387
  416.8 8.9 %collective-permute-done.77 = f32[11,768]{1,0:T(8,128)S(1)} collective-permute-done((f32[11,768]{1,0:T(8,128)S(1)}, f32[11,768]{1,0:T(8,128)S(1)}, u32[]{:S(2)}, u32[]{:S(2)}) %collective-permute-start.77) | collective-permute-done | bytes 33824 | tf_op jit(solution)/shard_map/ppermute | solution.py:84
  441.4 7.7 %fusion = bf16[4,768,768]{2,0,1:T(4,128)(2,1)S(1)} fusion(bf16[4,768,768]{2,0,1:T(4,128)(2,1)} %collective-permute-done.68, s32[]{:T(128)S(6)} %select_n.552, bf16[1,4,768,768]{3,1,2,0:T(4,128)(2,1)S(1)} %bitcast.566, bf16[1,4,768,768]{3,1,2,0:T(4,128)(2,1)S(1)} %bitcast.562), kind=kLoop, calls=%fused_computation.5 | loop fusion | flops 11796480 | bytes 18874372 | tf_op jit(solution)/shard_map/convert_element_type | solution.py:241
  463.6 15.5 %collective-permute-done.65 = bf16[2,192,192]{2,1,0:T(8,128)(2,1)S(1)} collective-permute-done((bf16[2,192,192]{2,1,0:T(8,128)(2,1)S(1)}, bf16[2,192,192]{2,1,0:T(8,128)(2,1)S(1)}, u32[]{:S(2)}, u32[]{:S(2)}) %collective-permute-start.65) | collective-permute-done | bytes 147488 | tf_op jit(solution)/shard_map/ppermute | solution.py:411
  484.9 20.0 %collective-permute-start.67 = (f32[2,96,192]{2,1,0:T(8,128)S(1)}, f32[2,96,192]{2,1,0:T(8,128)S(1)}, u32[]{:S(2)}, u32[]{:S(2)}) collective-permute-start(f32[2,96,192]{2,1,0:T(8,128)S(1)} %constant_dynamic-slice_fusion.6), channel_id=1, source_target_pairs={{0,4},{4,0},{8,12},{12,8},{16,20},{20,16},{24,28},{28,24},{1,5},{5... | collective-permute-start | bytes 442376 | tf_op jit(solution)/shard_map/ppermute | solution.py:84
  522.7 6.6 %collective-permute-done.57 = bf16[2,192,192]{2,1,0:T(8,128)(2,1)S(1)} collective-permute-done((bf16[2,192,192]{2,1,0:T(8,128)(2,1)S(1)}, bf16[2,192,192]{2,1,0:T(8,128)(2,1)S(1)}, u32[]{:S(2)}, u32[]{:S(2)}) %collective-permute-start.57) | collective-permute-done | bytes 147488 | tf_op jit(solution)/shard_map/ppermute | solution.py:411
  529.3 21.6 %collective-permute-done.58 = bf16[2,192,192]{2,1,0:T(8,128)(2,1)S(1)} collective-permute-done((bf16[2,192,192]{2,1,0:T(8,128)(2,1)S(1)}, bf16[2,192,192]{2,1,0:T(8,128)(2,1)S(1)}, u32[]{:S(2)}, u32[]{:S(2)}) %collective-permute-start.58) | collective-permute-done | bytes 147488 | tf_op jit(solution)/shard_map/ppermute | solution.py:411
  566.5 17.0 %collective-permute-done.72 = bf16[192,768]{1,0:T(8,128)(2,1)} collective-permute-done((bf16[192,768]{1,0:T(8,128)(2,1)S(1)}, bf16[192,768]{1,0:T(8,128)(2,1)}, u32[]{:S(2)}, u32[]{:S(2)}) %collective-permute-start.72) | collective-permute-done | bytes 294944 | tf_op jit(solution)/shard_map/ppermute | solution.py:411
  (617 shorter events, 377.6 us)
Async XLA Ops:
  7.2 582.3 %all-gather.7.cloned.1.call-start = ((), (), s32[]{:S(2)}) async-start(), calls=%async_computation.1 | async-start | bytes 4915200 | tf_op jit(solution)/shard_map/all_gather | solution.py:380
  15.3 45.2 %collective-permute-start.10 = (bf16[128,768]{1,0:T(8,128)(2,1)S(1)}, bf16[128,768]{1,0:T(8,128)(2,1)}, u32[]{:S(2)}, u32[]{:S(2)}) collective-permute-start(bf16[128,768]{1,0:T(8,128)(2,1)S(1)} %dynamic-slice_bitcast_fusion.17), channel_id=1, source_target_pairs={{0,24},{4,28},{8,16},{12,20},{16,8},{20,12},{24,0},{28,4},{1,25},{... | collective-permute-start | bytes 589832 | tf_op jit(solution)/shard_map/ppermute | solution.py:84
  16.6 46.3 %collective-permute-start.11 = (bf16[128,768]{1,0:T(8,128)(2,1)S(1)}, bf16[128,768]{1,0:T(8,128)(2,1)}, u32[]{:S(2)}, u32[]{:S(2)}) collective-permute-start(bf16[128,768]{1,0:T(8,128)(2,1)S(1)} %dynamic-slice_bitcast_fusion.17), channel_id=1, source_target_pairs={{0,16},{4,20},{8,24},{12,28},{16,0},{20,4},{24,8},{28,12},{1,17},{... | collective-permute-start | bytes 589832 | tf_op jit(solution)/shard_map/ppermute | solution.py:84
  35.0 29.2 %collective-permute-start.12 = (bf16[128,768]{1,0:T(8,128)(2,1)S(1)}, bf16[128,768]{1,0:T(8,128)(2,1)S(1)}, u32[]{:S(2)}, u32[]{:S(2)}) collective-permute-start(bf16[128,768]{1,0:T(8,128)(2,1)S(1)} %dynamic-slice_bitcast_fusion.17), channel_id=1, source_target_pairs={{0,8},{4,12},{8,0},{12,4},{16,24},{20,28},{24,16},{28,20},{1,9},{5... | collective-permute-start | bytes 589832 | tf_op jit(solution)/shard_map/ppermute | solution.py:84
  66.4 47.6 %collective-permute-start.6 = (bf16[2,192,768]{2,1,0:T(8,128)(2,1)}, bf16[2,192,768]{2,1,0:T(8,128)(2,1)S(1)}, u32[]{:S(2)}, u32[]{:S(2)}) collective-permute-start(bf16[2,192,768]{2,1,0:T(8,128)(2,1)} %reshape.460), channel_id=1, source_target_pairs={{0,4},{4,0},{8,12},{12,8},{16,20},{20,16},{24,28},{28,24},{1,5},{5... | collective-permute-start | bytes 1769480 | tf_op jit(solution)/shard_map/ppermute | solution.py:84
  88.8 37.1 %collective-permute-start.28 = (bf16[2,192,768]{2,1,0:T(8,128)(2,1)S(1)}, bf16[2,192,768]{2,1,0:T(8,128)(2,1)S(1)}, u32[]{:S(2)}, u32[]{:S(2)}) collective-permute-start(bf16[2,192,768]{2,1,0:T(8,128)(2,1)S(1)} %reshape.472), channel_id=1, source_target_pairs={{0,4},{4,0},{8,12},{12,8},{16,20},{20,16},{24,28},{28,24},{1,5},{5... | collective-permute-start | bytes 1769480 | tf_op jit(solution)/shard_map/ppermute | solution.py:84
  91.6 37.5 %collective-permute-start.35 = (bf16[4,192,768]{2,1,0:T(8,128)(2,1)}, bf16[4,192,768]{2,1,0:T(8,128)(2,1)S(1)}, u32[]{:S(2)}, u32[]{:S(2)}) collective-permute-start(bf16[4,192,768]{2,1,0:T(8,128)(2,1)} %get-tuple-element.49), channel_id=1, source_target_pairs={{0,8},{4,20},{8,0},{12,28},{16,24},{20,4},{24,16},{28,12},{1,9},{5... | collective-permute-start | bytes 3538952 | tf_op jit(solution)/shard_map/ppermute | solution.py:133
  125.9 75.3 %collective-permute-start.38 = (bf16[4,192,768]{2,1,0:T(8,128)(2,1)}, bf16[4,192,768]{2,1,0:T(8,128)(2,1)}, u32[]{:S(2)}, u32[]{:S(2)}) collective-permute-start(bf16[4,192,768]{2,1,0:T(8,128)(2,1)} %get-tuple-element.49), channel_id=1, source_target_pairs={{0,4},{4,0},{8,12},{12,8},{16,20},{20,16},{24,28},{28,24},{1,5},{5... | collective-permute-start | bytes 3538952 | tf_op jit(solution)/shard_map/ppermute | solution.py:84
  128.2 30.7 %collective-permute-start.31 = (bf16[2,192,768]{2,1,0:T(8,128)(2,1)}, bf16[2,192,768]{2,1,0:T(8,128)(2,1)}, u32[]{:S(2)}, u32[]{:S(2)}) collective-permute-start(bf16[2,192,768]{2,1,0:T(8,128)(2,1)} %collective-permute-done.27), channel_id=1, source_target_pairs={{0,4},{4,0},{8,12},{12,8},{16,20},{20,16},{24,28},{28,24},{1,5},{5... | collective-permute-start | bytes 1769480 | tf_op jit(solution)/shard_map/ppermute | solution.py:84
  129.2 69.7 %collective-permute-start.37 = (bf16[4,192,768]{2,1,0:T(8,128)(2,1)S(1)}, bf16[4,192,768]{2,1,0:T(8,128)(2,1)}, u32[]{:S(2)}, u32[]{:S(2)}) collective-permute-start(bf16[4,192,768]{2,1,0:T(8,128)(2,1)S(1)} %collective-permute-done.35), channel_id=1, source_target_pairs={{0,16},{4,12},{8,24},{12,4},{16,0},{20,28},{24,8},{28,20},{1,17},{... | collective-permute-start | bytes 3538952 | tf_op jit(solution)/shard_map/ppermute | solution.py:133
  135.7 67.9 %collective-permute-start.39 = (bf16[4,192,768]{2,1,0:T(8,128)(2,1)S(1)}, bf16[4,192,768]{2,1,0:T(8,128)(2,1)}, u32[]{:S(2)}, u32[]{:S(2)}) collective-permute-start(bf16[4,192,768]{2,1,0:T(8,128)(2,1)S(1)} %collective-permute-done.35), channel_id=1, source_target_pairs={{0,4},{4,0},{8,12},{12,8},{16,20},{20,16},{24,28},{28,24},{1,5},{5... | collective-permute-start | bytes 3538952 | tf_op jit(solution)/shard_map/ppermute | solution.py:84
  311.3 27.2 %collective-permute-start.46 = (bf16[128,896]{0,1:T(8,128)(2,1)}, bf16[128,896]{0,1:T(8,128)(2,1)}, u32[]{:S(2)}, u32[]{:S(2)}) collective-permute-start(bf16[128,896]{0,1:T(8,128)(2,1)} %concatenate.137), channel_id=1, source_target_pairs={{0,24},{4,28},{8,16},{12,20},{16,8},{20,12},{24,0},{28,4},{1,25},{... | collective-permute-start | bytes 688136 | tf_op jit(solution)/shard_map/ppermute | solution.py:84
  374.3 221.0 %all-gather.5.cloned.1.call-start = ((), (), s32[]{:S(2)}) async-start(), calls=%async_computation | async-start | bytes 4915200 | tf_op jit(solution)/shard_map/all_gather | solution.py:324
  384.9 56.0 %collective-permute-start.68 = (bf16[4,768,768]{2,0,1:T(4,128)(2,1)}, bf16[4,768,768]{2,0,1:T(4,128)(2,1)}, u32[]{:S(2)}, u32[]{:S(2)}) collective-permute-start(bf16[4,768,768]{2,0,1:T(4,128)(2,1)} %fusion.12), channel_id=1, source_target_pairs={{0,4},{4,0},{8,12},{12,8},{16,20},{20,16},{24,28},{28,24},{1,5},{5... | collective-permute-start | bytes 14155784 | tf_op jit(solution)/shard_map/ppermute | solution.py:84
  401.7 31.6 %collective-permute-start.54 = (bf16[2,768,768]{2,1,0:T(8,128)(2,1)}, bf16[2,768,768]{2,1,0:T(8,128)(2,1)S(1)}, u32[]{:S(2)}, u32[]{:S(2)}) collective-permute-start(bf16[2,768,768]{2,1,0:T(8,128)(2,1)} %dynamic-slice_bitcast_fusion.1), channel_id=1, source_target_pairs={{0,4},{4,0},{8,12},{12,8},{16,20},{20,16},{24,28},{28,24},{1,5},{5... | collective-permute-start | bytes 7077896 | tf_op jit(solution)/shard_map/ppermute | solution.py:84
  409.5 28.6 %collective-permute-start.62 = (bf16[2,2,192,768]{3,2,1,0:T(8,128)(2,1)}, bf16[2,2,192,768]{3,2,1,0:T(8,128)(2,1)}, u32[]{:S(2)}, u32[]{:S(2)}) collective-permute-start(bf16[2,2,192,768]{3,2,1,0:T(8,128)(2,1)} %pad_maximum_fusion.4), channel_id=1, source_target_pairs={{0,8},{4,20},{8,0},{12,28},{16,24},{20,4},{24,16},{28,12},{1,9},{5... | collective-permute-start | bytes 3538952 | tf_op jit(solution)/shard_map/ppermute | solution.py:133
  425.7 33.3 %collective-permute-start.78 = (f32[11,768]{1,0:T(8,128)S(1)}, f32[11,768]{1,0:T(8,128)S(1)}, u32[]{:S(2)}, u32[]{:S(2)}) collective-permute-start(f32[11,768]{1,0:T(8,128)S(1)} %add.697), channel_id=1, source_target_pairs={{0,1},{1,2},{2,3},{3,0},{4,5},{5,6},{6,7},{7,4},{8,9},{9,10},{10,1... | collective-permute-start | bytes 101384 | tf_op jit(solution)/shard_map/ppermute | solution.py:479
  428.2 32.4 %collective-permute-start.79 = (f32[11,768]{1,0:T(8,128)S(1)}, f32[11,768]{1,0:T(8,128)}, u32[]{:S(2)}, u32[]{:S(2)}) collective-permute-start(f32[11,768]{1,0:T(8,128)S(1)} %add.697), channel_id=1, source_target_pairs={{0,2},{1,3},{2,0},{3,1},{4,6},{5,7},{6,4},{7,5},{8,10},{9,11},{10,... | collective-permute-start | bytes 101384 | tf_op jit(solution)/shard_map/ppermute | solution.py:479
  433.3 29.0 %collective-permute-start.80 = (f32[11,768]{1,0:T(8,128)S(1)}, f32[11,768]{1,0:T(8,128)}, u32[]{:S(2)}, u32[]{:S(2)}) collective-permute-start(f32[11,768]{1,0:T(8,128)S(1)} %add.697), channel_id=1, source_target_pairs={{0,3},{1,0},{2,1},{3,2},{4,7},{5,4},{6,5},{7,6},{8,11},{9,8},{10,9... | collective-permute-start | bytes 101384 | tf_op jit(solution)/shard_map/ppermute | solution.py:479
  438.1 45.0 %collective-permute-start.55 = (bf16[2,2,192,768]{3,2,1,0:T(8,128)(2,1)}, bf16[2,2,192,768]{3,2,1,0:T(8,128)(2,1)}, u32[]{:S(2)}, u32[]{:S(2)}) collective-permute-start(bf16[2,2,192,768]{3,2,1,0:T(8,128)(2,1)} %pad_maximum_fusion.3), channel_id=1, source_target_pairs={{0,8},{4,20},{8,0},{12,28},{16,24},{20,4},{24,16},{28,12},{1,9},{5... | collective-permute-start | bytes 3538952 | tf_op jit(solution)/shard_map/ppermute | solution.py:133
  452.6 57.6 %collective-permute-start.69 = (bf16[2,4,192,768]{3,2,1,0:T(8,128)(2,1)}, bf16[2,4,192,768]{3,2,1,0:T(8,128)(2,1)}, u32[]{:S(2)}, u32[]{:S(2)}) collective-permute-start(bf16[2,4,192,768]{3,2,1,0:T(8,128)(2,1)} %pad_maximum_fusion.2), channel_id=1, source_target_pairs={{0,8},{4,20},{8,0},{12,28},{16,24},{20,4},{24,16},{28,12},{1,9},{5... | collective-permute-start | bytes 7077896 | tf_op jit(solution)/shard_map/ppermute | solution.py:133
  512.5 44.9 %collective-permute-start.70 = (bf16[4,192,768]{2,1,0:T(8,128)(2,1)S(1)}, bf16[4,192,768]{2,1,0:T(8,128)(2,1)S(1)}, u32[]{:S(2)}, u32[]{:S(2)}) collective-permute-start(bf16[4,192,768]{2,1,0:T(8,128)(2,1)S(1)} %dynamic-slice_bitcast_fusion.2), channel_id=1, source_target_pairs={{0,16},{4,12},{8,24},{12,4},{16,0},{20,28},{24,8},{28,20},{1,17},{... | collective-permute-start | bytes 3538952 | tf_op jit(solution)/shard_map/ppermute | solution.py:133
  516.9 33.9 %collective-permute-start.58 = (bf16[2,192,192]{2,1,0:T(8,128)(2,1)S(1)}, bf16[2,192,192]{2,1,0:T(8,128)(2,1)S(1)}, u32[]{:S(2)}, u32[]{:S(2)}) collective-permute-start(bf16[2,192,192]{2,1,0:T(8,128)(2,1)S(1)} %bitcast.639), channel_id=1, source_target_pairs={{0,2},{1,3},{2,0},{3,1},{4,6},{5,7},{6,4},{7,5},{8,10},{9,11},{10,... | collective-permute-start | bytes 442376 | tf_op jit(solution)/shard_map/ppermute | solution.py:411
  520.5 33.8 %collective-permute-start.59 = (bf16[2,192,192]{2,1,0:T(8,128)(2,1)S(1)}, bf16[2,192,192]{2,1,0:T(8,128)(2,1)S(1)}, u32[]{:S(2)}, u32[]{:S(2)}) collective-permute-start(bf16[2,192,192]{2,1,0:T(8,128)(2,1)S(1)} %bitcast.640), channel_id=1, source_target_pairs={{0,3},{1,0},{2,1},{3,2},{4,7},{5,4},{6,5},{7,6},{8,11},{9,8},{10,9... | collective-permute-start | bytes 442376 | tf_op jit(solution)/shard_map/ppermute | solution.py:411
  (151 other events, 1575.5 us)
Sparse Core Ops, SparseCore 0:
  374.5 80.4 all-gather.6
  456.5 101.7 all-gather.4

commit v3 on v1

v3 whole, which is shorter than its diff:
```python
import functools
import math

import jax
import jax.numpy as jnp
import numpy as np
from jax import lax
from jax.experimental import pallas as pl
from jax.experimental.pallas import tpu as pltpu
from jax.sharding import PartitionSpec as P

HD = 64
SLOTS = 4
EPSILON = 1e-05
NEG_FILL = -1e30
BF = jnp.bfloat16
F32 = jnp.float32


def dot(left, right):
    return jnp.dot(left, right, preferred_element_type=F32)


def dot_nt(left, right):
    return lax.dot_general(left, right, (((1,), (1,)), ((), ())), preferred_element_type=F32)


def dot_tn(left, right):
    return lax.dot_general(left, right, (((0,), (0,)), ((), ())), preferred_element_type=F32)


TILE = 2 * HD
PARTS = 3
MIB = 1024 * 1024
SMALL = pl.CostEstimate(flops=1, bytes_accessed=1, transcendentals=0)


ROLE, WALK, OTHER_WALK, PLANE, SLOT, UNIT, HALF, BIT, OTHER_BIT, INFO = 0, 1, 5, 9, 10, 11, 12, 13, 14, 16


def call(kernel, name, operands, outs, anys=0, scratch=(), flops=0, vmem=None, out_any=0, after=(), smem=1):
    def body(*refs):
        kernel(*refs[: len(operands)], *refs[len(operands) + len(after) :])

    if vmem is None:
        vmem = 60 if anys or name == "attention_weight_grad" else 16
    vm, anywhere = pl.BlockSpec(memory_space=pltpu.VMEM), pl.BlockSpec(memory_space=pl.ANY)
    specs = [pl.BlockSpec(memory_space=pltpu.SMEM)] * smem
    specs += [vm] * (len(operands) - smem - anys) + [anywhere] * (anys + len(after))
    return pl.pallas_call(
        body,
        out_shape=[jax.ShapeDtypeStruct(s, d) for s, d in outs],
        in_specs=specs,
        out_specs=[vm] * (len(outs) - out_any) + [anywhere] * out_any,
        scratch_shapes=list(scratch),
        compiler_params=pltpu.CompilerParams(vmem_limit_bytes=vmem * MIB),
        cost_estimate=SMALL,
        name=name,
    )(*operands, *after)


def info_kernel(places, lengths, info, unit, block_len):
    seq, head = places[0], places[1]
    role, quad = lax.rem(seq, 2), lax.rem(seq // 2, 4)
    first, second = 1 + role, 2 - role
    info[ROLE] = role
    for at, step in enumerate((0, first, second, 3)):
        info[WALK + at] = quad ^ step
    for at, step in enumerate((0, second, first, 3)):
        info[OTHER_WALK + at] = quad ^ step
    info[PLANE] = head
    end = 0
    slot = 0
    for at in range(SLOTS):
        end = end + lengths[head, at]
        slot = slot + (end <= seq * block_len).astype(jnp.int32)
    info[SLOT] = slot
    info[UNIT] = seq // unit
    info[HALF] = lax.rem(seq, unit) // (unit // 2)
    info[BIT] = jnp.where(role == 0, lax.rem(quad, 2), quad // 2)
    info[OTHER_BIT] = jnp.where(role == 0, quad // 2, lax.rem(quad, 2))
    info[INFO - 1] = 0


def planes_kernel(info, first, second, third, fourth, *outs):
    for at, ref in enumerate((first, second, third, fourth)):
        for mat in range(4):
            out = outs[mat // 2]
            out[mat % 2, info[PLANE] ^ at] = ref[mat]


def first_pieces_kernel(places, lengths, memory, *refs, unit, block_len):
    weights, (info, piece, mem, sems) = refs[:8], refs[8:]
    info_kernel(places, lengths, info, unit, block_len)
    copy_mem = pltpu.make_async_copy(memory.at[places[1]], mem, sems.at[4])
    copy_mem.start()
    rows = piece.shape[1]
    at = pl.ds(pl.multiple_of(info[WALK] * rows, rows), rows)
    for role, chosen in enumerate(((0, 1, 4, 5), (2, 3, 6, 7))):

        @pl.when(info[ROLE] == role)
        def _(chosen=chosen):
            copies = [
                pltpu.make_async_copy(weights[which].at[at], piece.at[mat], sems.at[mat])
                for mat, which in enumerate(chosen)
            ]
            for copy in copies:
                copy.start()
            for copy in copies:
                copy.wait()

    copy_mem.wait()


def other_pieces_kernel(info, bias, *refs):
    ffn_in, ffn_out, tokens, cot_tok, cot_mem = refs[:5]
    ffn, tok, cot_t, cot_m, sems = refs[5:]
    plane = info[PLANE]
    copies = []
    for at, (source, to) in enumerate(((tokens, tok), (cot_tok, cot_t), (cot_mem, cot_m))):
        copies.append(pltpu.make_async_copy(source.at[plane], to, sems.at[2 + at]))
    for copy in copies:
        copy.start()
    rows = ffn.shape[0] - 16
    for role, source in enumerate((ffn_in, ffn_out)):

        @pl.when(info[ROLE] == role)
        def _(source=source):
            copy = pltpu.make_async_copy(source, ffn.at[pl.ds(0, rows)], sems.at[5])
            copy.start()
            copy.wait()

    value = bias[...][None]
    parts = []
    for part in range(PARTS):
        low = value.astype(BF).astype(F32)
        parts.append(low)
        value = value - low
    parts.append(jnp.zeros((16 - PARTS, bias.shape[0]), F32))
    ffn[rows:] = jnp.concatenate(parts, axis=0).astype(BF)
    for copy in copies:
        copy.wait()


def vectors_kernel(info, mem_vectors, out_vectors, attn_vectors, hid_vec, out):
    out[...] = jnp.zeros(out.shape, F32)
    out[0:1] = out_vectors[0:1]
    out[1:3] = mem_vectors[0:2]
    out[3:5] = attn_vectors[0:2]
    out[5:7] = out_vectors[1:3]
    for plane in range(hid_vec.shape[0]):
        out[7 + plane : 8 + plane] = hid_vec[plane]


def total_kernel(info, *refs):
    total = refs[0][...]
    for ref in refs[1:-1]:
        total = total + ref[...]
    refs[-1][...] = total


def plane_vectors_kernel(info, first, second, third, fourth, out, held):
    planes = held.shape[0]
    for at, ref in enumerate((first, second, third, fourth)):
        held[info[PLANE] ^ at] = ref[...]
    total = held[0]
    for plane in range(1, planes):
        total = total + held[plane]
    out[...] = total


def memory_total_kernel(info, base, first, second, third, fourth, out):
    total = base[...]
    for ref in (first, second, third, fourth):
        total = total + ref[...].astype(F32)
    out[...] = total.astype(BF)


def pick_kernel(info, first, second, third, fourth, out):
    for at, ref in enumerate((first, second, third, fourth)):

        @pl.when(info[SLOT] == (info[UNIT] ^ at))
        def _(ref=ref):
            out[...] = ref[...]


def tie(value, *after):
    anywhere = pl.BlockSpec(memory_space=pl.ANY)
    return pl.pallas_call(
        lambda *refs: None,
        out_shape=jax.ShapeDtypeStruct(value.shape, value.dtype),
        in_specs=[anywhere] * (1 + len(after)),
        out_specs=anywhere,
        input_output_aliases={0: 0},
        compiler_params=pltpu.CompilerParams(vmem_limit_bytes=16 * MIB),
        cost_estimate=SMALL,
        name="tie",
    )(value, *after)


def stack_kernel(info, first, second, third, fourth, out):
    for at, ref in enumerate((first, second, third, fourth)):
        out[info[PLANE] ^ at] = ref[...]


def put_halves(info, keep, send, value):
    size = keep.shape[0]

    @pl.when(info[HALF] == 0)
    def _():
        keep[...] = value[:size]
        send[...] = value[size:]

    @pl.when(info[HALF] == 1)
    def _():
        keep[...] = value[size:]
        send[...] = value[:size]


def put_slots(info, outs, value, empty):
    for at, out in enumerate(outs):
        here = info[SLOT] == (info[UNIT] ^ at)

        @pl.when(here)
        def _(out=out):
            out[...] = value

        @pl.when(jnp.logical_not(here))
        def _(out=out):
            out[...] = empty


def blend_values(given, sel, width):
    lses = [dot(c[:, width:], sel[0]) for c in given]
    top = lses[0]
    for lse in lses[1:]:
        top = jnp.maximum(top, lse)
    shares = [jnp.exp(lse - top) for lse in lses]
    total = shares[0]
    for share in shares[1:]:
        total = total + share
    inv = 1.0 / total
    low = lax.broadcasted_iota(jnp.int32, (1, TILE), 1) < HD
    tiles = []
    for pair in range(width // TILE):
        cols = slice(pair * TILE, (pair + 1) * TILE)
        ctx = None
        for share, c in zip(shares, given):
            share = share * inv
            weight = jnp.where(
                low, share[:, 2 * pair : 2 * pair + 1], share[:, 2 * pair + 1 : 2 * pair + 2]
            )
            term = weight * c[:, cols].astype(F32)
            ctx = term if ctx is None else ctx + term
        tiles.append(ctx.astype(BF))
    return tiles, top + jnp.log(total)


def blend_kernel(info, keep, got, sel, *outs):
    outs, value = outs[:SLOTS], outs[SLOTS]
    width = value.shape[1] - TILE
    heads = width // HD
    tiles, lse = blend_values((keep, got), sel, width)
    for pair, tile in enumerate(tiles):
        value[:, pair * TILE : (pair + 1) * TILE] = tile
    value[:, width:] = as_parts(lse, heads).astype(BF)
    col = lax.broadcasted_iota(jnp.int32, value.shape, 1)
    fill = jnp.where((col >= width) & (col < width + heads), NEG_FILL, 0.0)
    put_slots(info, outs, value[...], fill.astype(BF))


def sum_kernel(info, keep, got, *outs):
    total = (keep[...].astype(F32) + got[...].astype(F32)).astype(BF)
    put_slots(info, outs, total, jnp.zeros(total.shape, BF))


def start_weights(info, pieces, held, sems, mats=(0, 1)):
    planes = held.shape[2]
    for mat in mats:
        for j in range(4):
            mine = (info[ROLE], info[WALK + j], pieces[j])
            theirs = (1 - info[ROLE], info[OTHER_WALK + j], pieces[4 + j])
            for role, unit, piece in (mine, theirs):
                for plane in range(planes):
                    pltpu.make_async_copy(
                        piece.at[mat, plane],
                        held.at[role, mat, plane, unit],
                        sems.at[role, mat, j * planes + plane],
                    ).start()


def weight(held, sems, pieces, role, mat):
    planes = held.shape[2]
    for j in range(4):
        for plane in range(planes):
            pltpu.make_async_copy(
                pieces[j].at[mat, plane],
                held.at[role, mat, plane, j],
                sems.at[role, mat, j * planes + plane],
            ).wait()
    return matrix(held, role, mat)


def matrix(held, *index):
    block = held[index]
    return block.reshape(-1, block.shape[-1])


def half_masks():
    lane = lax.broadcasted_iota(jnp.int32, (1, TILE), 1)
    low = (lane < HD).astype(F32).astype(BF)
    return low, (lane >= HD).astype(F32).astype(BF)


def put_scalars(rows):
    count = len(rows)
    stack = jnp.concatenate(rows * PARTS, axis=0)
    extra = TILE - stack.shape[0]
    stack = jnp.concatenate([stack, jnp.zeros((extra, stack.shape[1]), F32)], axis=0)
    return stack.T


def as_parts(wide, heads, offset=0):
    first = wide.astype(BF).astype(F32)
    rest = wide - first
    second = rest.astype(BF).astype(F32)
    third = rest - second
    lane = lax.broadcasted_iota(jnp.int32, wide.shape, 1) - offset
    return jnp.where(
        lane < 0,
        0.0,
        jnp.where(
            lane < heads,
            first,
            jnp.where(lane < 2 * heads, second, jnp.where(lane < 3 * heads, third, 0.0)),
        ),
    )


def norm_stats(summed):
    centre = summed - jnp.mean(summed, axis=-1, keepdims=True)
    inv = lax.rsqrt(jnp.mean(centre * centre, axis=-1, keepdims=True) + EPSILON)
    return centre * inv, inv


def norm_pull(upstream, normed, inv, gain):
    scaled = upstream * gain
    return inv * (
        scaled
        - jnp.mean(scaled, axis=-1, keepdims=True)
        - normed * jnp.mean(scaled * normed, axis=-1, keepdims=True)
    )


def head_forward(q_tile, k_tile, v_tile, masks):
    parts, rows = [], []
    for side in range(2):
        scores = dot_nt(k_tile * masks[side], q_tile)
        top = jnp.max(scores, axis=0, keepdims=True)
        weights = jnp.exp(scores - top)
        den = jnp.sum(weights, axis=0, keepdims=True)
        num = dot_tn(v_tile, weights.astype(BF))[side * HD : (side + 1) * HD]
        parts.append(num * (1.0 / den))
        rows.append(top + jnp.log(den))
    return jnp.concatenate(parts, axis=0), rows


def head_backward(q_tile, k_tile, v_tile, g_tile, lses, deltas, masks):
    dq, dk, dv = [], None, None
    for side in range(2):
        q_side, g_side = q_tile * masks[side], g_tile * masks[side]
        weights = jnp.exp(dot_nt(k_tile, q_side) - lses[side])
        dscores = (weights * (dot_nt(v_tile, g_side) - deltas[side])).astype(BF)
        weights = weights.astype(BF)
        dq.append(dot_tn(k_tile, dscores)[side * HD : (side + 1) * HD])
        dk_side, dv_side = dot(dscores, q_side), dot(weights, g_side)
        dk = dk_side if dk is None else dk + dk_side
        dv = dv_side if dv is None else dv + dv_side
    return jnp.concatenate(dq, axis=0), dk, dv


def pack_forward_kernel(
    info, tok, mem, *refs
):
    pieces, (k_out, v_out, q_out, keep, send, packed, held, sems) = refs[:8], refs[8:]
    width = tok.shape[1]
    heads = width // HD
    start_weights(info, pieces, held, sems)
    k_out[...] = dot_nt(tok[...], weight(held, sems, pieces, 0, 0)).astype(BF)
    v_out[...] = dot_nt(tok[...], weight(held, sems, pieces, 0, 1)).astype(BF)
    q_out[...] = dot_nt(mem[...], weight(held, sems, pieces, 1, 0)).astype(BF) * BF(HD**-0.5)
    masks = half_masks()
    rows = []
    for pair in range(heads // 2):
        cols = slice(pair * TILE, (pair + 1) * TILE)
        ctx, pair_rows = head_forward(q_out[:, cols], k_out[:, cols], v_out[:, cols], masks)
        packed[:, cols] = ctx.T.astype(BF)
        rows += pair_rows
    packed[:, width:] = as_parts(put_scalars(rows), heads).astype(BF)
    put_halves(info, keep, send, packed)
    weight(held, sems, pieces, 1, 1)


def start_out_matrix(info, pieces, held, sems):
    planes = held.shape[0]
    for j in range(4):
        for role, piece, unit in ((1, pieces[j], WALK + j), (0, pieces[4 + j], OTHER_WALK + j)):

            @pl.when(info[ROLE] == role)
            def _(piece=piece, unit=unit, j=j):
                for plane in range(planes):
                    pltpu.make_async_copy(
                        piece.at[1, plane], held.at[plane, info[unit]], sems.at[j * planes + plane]
                    ).start()


def out_matrix(pieces, held, sems):
    planes = held.shape[0]
    for j in range(4):
        for plane in range(planes):
            pltpu.make_async_copy(
                pieces[j].at[1, plane], held.at[plane, j], sems.at[j * planes + plane]
            ).wait()
    return matrix(held, Ellipsis)


def memory_kernel(info, c0, c1, c2, c3, sel, mem, cot, gain, bias, *refs):
    pieces, outs = refs[:8], refs[8:]
    result, mix_low, ctx_out, lse_out, grad_sum, vectors, held, sems = outs
    width = mem.shape[1]
    heads = width // HD
    start_out_matrix(info, pieces, held, sems)
    tiles, lse = blend_values((c0, c1, c2, c3), sel, width)
    lse_out[...] = lse
    for pair, tile in enumerate(tiles):
        ctx_out[:, pair * TILE : (pair + 1) * TILE] = tile
    mix = dot(ctx_out[...], out_matrix(pieces, held, sems))
    mix_low[...] = mix.astype(BF)
    normed, inv_std = norm_stats(mix + mem[...].astype(F32))
    gain_row = gain[...][None]
    result[...] = (normed * gain_row + bias[...][None]).astype(BF)
    upstream = cot[...].astype(F32)
    grad_sum[...] = norm_pull(upstream, normed, inv_std, gain_row)
    vectors[0:1] = jnp.sum(upstream * normed, axis=0, keepdims=True)
    vectors[1:2] = jnp.sum(upstream, axis=0, keepdims=True)


def unpack_forward_kernel(info, tok, mix, *refs):
    pieces, outs = refs[:8], refs[8:]
    k_out, v_out, q_out, ctx_out, lse_out, normed_out, inv_out, held, sems = outs
    width = tok.shape[1]
    heads = width // HD
    start_weights(info, pieces, held, sems)
    k_out[...] = dot_nt(mix[...], weight(held, sems, pieces, 0, 0)).astype(BF)
    v_out[...] = dot_nt(mix[...], weight(held, sems, pieces, 0, 1)).astype(BF)
    q_out[...] = dot_nt(tok[...], weight(held, sems, pieces, 1, 0)).astype(BF) * BF(HD**-0.5)
    masks = half_masks()
    for pair in range(heads // 2):
        cols = slice(pair * TILE, (pair + 1) * TILE)
        ctx, rows = head_forward(q_out[:, cols], k_out[:, cols], v_out[:, cols], masks)
        ctx_out[:, cols] = ctx.T.astype(BF)
        lse_out[2 * pair : 2 * pair + 1] = rows[0]
        lse_out[2 * pair + 1 : 2 * pair + 2] = rows[1]
    summed = dot(ctx_out[...], weight(held, sems, pieces, 1, 1)) + tok[...].astype(F32)
    normed, inv = norm_stats(summed)
    normed_out[...] = normed
    inv_out[...] = inv


GELU_A = math.sqrt(2.0 / math.pi)
GELU_B = 0.044715


def start_ffn(info, pieces, held, sems):
    planes, rows = held.shape[1], held.shape[2]
    quarter = rows // 4
    for plane in range(planes):
        for j, role in enumerate((info[ROLE], 1 - info[ROLE])):
            for part in range(4):
                at = pl.ds(part * quarter, quarter)
                pltpu.make_async_copy(
                    pieces[j].at[plane, at], held.at[role, plane, at], sems.at[plane, 4 * j + part]
                ).start()


def wait_ffn(pieces, held, sems, plane):
    rows = held.shape[2]
    quarter = rows // 4
    for j in range(2):
        for part in range(4):
            at = pl.ds(part * quarter, quarter)
            pltpu.make_async_copy(
                pieces[j].at[0, at], held.at[j, plane, at], sems.at[plane, 4 * j + part]
            ).wait()


def ffn_forward_kernel(info, normed_in, cot, mem_result, *refs):
    rows, refs = [r[...][None] for r in refs[:5]], refs[5:]
    attn_gain, attn_bias, out_gain, out_bias, ffn_bias = rows
    pieces, outs = refs[:2], refs[2:]
    out, attn_low, gelu_out, slope, grad_sum, vectors = outs[:6]
    held, bias, total, sems, bias_sem = outs[6:]
    planes = held.shape[1]
    bias_at = pl.ds(held.shape[2], 16)
    bias_copies = [
        pltpu.make_async_copy(pieces[0].at[plane, bias_at], bias.at[plane], bias_sem.at[plane])
        for plane in range(planes)
    ]
    for copy in bias_copies:
        copy.start()
    start_ffn(info, pieces, held, sems)
    attn = normed_in[...] * attn_gain + attn_bias
    attn_low[...] = attn.astype(BF)
    total[...] = attn + ffn_bias
    for copy in bias_copies:
        copy.wait()

    def forward(plane, carry):
        wait_ffn(pieces, held, sems, plane)
        parts = bias[plane].astype(F32)
        hidden = dot(attn_low[...], held[0, plane])
        hidden = hidden + (parts[0:1] + parts[1:2] + parts[2:3])
        square = hidden * hidden
        curve = jnp.tanh(GELU_A * hidden * (1.0 + GELU_B * square))
        half = 0.5 + 0.5 * curve
        gelu_out[plane] = (hidden * half).astype(BF)
        slope[plane] = (
            half
            + 0.5 * hidden * (1.0 - curve * curve) * (GELU_A + 3.0 * GELU_A * GELU_B * square)
        ).astype(BF)
        total[...] += dot(gelu_out[plane], held[1, plane])
        return carry

    lax.fori_loop(0, planes, forward, 0)
    out_normed, out_inv = norm_stats(total[...])
    rows = normed_in.shape[0]
    out[:rows] = (out_normed * out_gain + out_bias).astype(BF)
    out[rows:] = mem_result[...]
    upstream = cot[...].astype(F32)
    grad = norm_pull(upstream, out_normed, out_inv, out_gain)
    vectors[0:1] = jnp.sum(grad.astype(BF).astype(F32), axis=0, keepdims=True)
    vectors[1:2] = jnp.sum(upstream * out_normed, axis=0, keepdims=True)
    vectors[2:3] = jnp.sum(upstream, axis=0, keepdims=True)
    grad_sum[...] = grad


def ffn_backward_kernel(info, grad_sum, normed_in, inv_in, slope, attn_gain, *refs):
    pieces, outs = refs[:2], refs[2:]
    hid_grad, ffn_grad, mix_grad, mix_sum, vectors, hid_vec = outs[:6]
    held, total, sems = outs[6:]
    planes = held.shape[1]
    start_ffn(info, pieces, held, sems)
    grad = grad_sum[...]
    ffn_grad[...] = grad.astype(BF)
    total[...] = grad

    def backward(plane, carry):
        wait_ffn(pieces, held, sems, plane)
        pulled = dot_nt(ffn_grad[...], held[1, plane]) * slope[plane].astype(F32)
        low = pulled.astype(BF)
        hid_grad[plane] = low
        hid_vec[plane] = jnp.sum(low.astype(F32), axis=0, keepdims=True)
        total[...] += dot_nt(low, held[0, plane])
        return carry

    lax.fori_loop(0, planes, backward, 0)
    upstream = total[...]
    normed = normed_in[...]
    vectors[0:1] = jnp.sum(upstream * normed, axis=0, keepdims=True)
    vectors[1:2] = jnp.sum(upstream, axis=0, keepdims=True)
    grad = norm_pull(upstream, normed, inv_in[...], attn_gain[...][None])
    mix_sum[...] = grad
    mix_grad[...] = grad.astype(BF)


def unpack_backward_kernel(info, q_in, k_in, v_in, ctx, lse, mix_grad, mix_sum, *refs):
    pieces, outs = refs[:8], refs[8:]
    uq, uk, uv, keep, send, tok_part, held, sems = outs
    width = q_in.shape[1]
    heads = width // HD
    start_weights(info, pieces, held, sems, (1, 0))
    masks = half_masks()
    ctx_grad = dot_nt(mix_grad[...], weight(held, sems, pieces, 1, 1))
    ctx_low = ctx_grad.astype(BF)
    for pair in range(heads // 2):
        cols = slice(pair * TILE, (pair + 1) * TILE)
        product = ctx_grad[:, cols] * ctx[:, cols].astype(F32)
        first = product.astype(BF)
        second = (product - first.astype(F32)).astype(BF)
        deltas = []
        for side in range(2):
            picker = jnp.broadcast_to(masks[side], (16, TILE))
            deltas.append((dot_nt(picker, first) + dot_nt(picker, second))[0:1])
        lses = [lse[2 * pair : 2 * pair + 1], lse[2 * pair + 1 : 2 * pair + 2]]
        dq, dk, dv = head_backward(
            q_in[:, cols], k_in[:, cols], v_in[:, cols], ctx_low[:, cols], lses, deltas, masks
        )
        uq[:, cols] = (dq.T * (HD**-0.5)).astype(BF)
        uk[:, cols] = dk.astype(BF)
        uv[:, cols] = dv.astype(BF)
    mix_part = dot(uk[...], weight(held, sems, pieces, 0, 0))
    mix_part = mix_part + dot(uv[...], weight(held, sems, pieces, 0, 1))
    put_halves(info, keep, send, mix_part.astype(BF))
    tok_part[...] = mix_sum[...] + dot(uq[...], weight(held, sems, pieces, 1, 0))


def memory_back_kernel(info, c0, c1, c2, c3, sel, grad_sum, ctx, lse, *refs):
    pieces, outs = refs[:8], refs[8:]
    mix_grad, packed, held, sems = outs
    width = ctx.shape[1]
    heads = width // HD
    start_out_matrix(info, pieces, held, sems)
    total = grad_sum[...]
    for c in (c0, c1, c2, c3):
        total = total + c[...].astype(F32)
    mix_grad[...] = total.astype(BF)
    pulled = dot_nt(mix_grad[...], out_matrix(pieces, held, sems))
    packed[:, :width] = pulled.astype(BF)
    delta = jnp.zeros(lse.shape, F32)
    for pair in range(heads // 2):
        cols = slice(pair * TILE, (pair + 1) * TILE)
        product = pulled[:, cols] * ctx[:, cols].astype(F32)
        first = product.astype(BF)
        second = (product - first.astype(F32)).astype(BF)
        delta = delta + dot(first, sel[2 + pair]) + dot(second, sel[2 + pair])
    scalars = as_parts(lse[...], heads) + as_parts(delta, heads, PARTS * heads)
    packed[:, width:] = scalars.astype(BF)


def pack_backward_kernel(info, back, sel, q_in, k_in, v_in, tok_part, *refs):
    pieces, outs = refs[:8], refs[8:]
    pq, pk, pv, tok_grad, keep, send, held, sems = outs
    width = q_in.shape[1]
    heads = width // HD
    start_weights(info, pieces, held, sems)
    masks = half_masks()
    lse = dot(back[:, width:], sel[0]).T
    delta = dot(back[:, width:], sel[1]).T
    for pair in range(heads // 2):
        cols = slice(pair * TILE, (pair + 1) * TILE)
        lses = [lse[2 * pair : 2 * pair + 1], lse[2 * pair + 1 : 2 * pair + 2]]
        deltas = [delta[2 * pair : 2 * pair + 1], delta[2 * pair + 1 : 2 * pair + 2]]
        dq, dk, dv = head_backward(
            q_in[:, cols], k_in[:, cols], v_in[:, cols], back[:, cols], lses, deltas, masks
        )
        pq[:, cols] = (dq.T * (HD**-0.5)).astype(BF)
        pk[:, cols] = dk.astype(BF)
        pv[:, cols] = dv.astype(BF)
    total = dot(pk[...], weight(held, sems, pieces, 0, 0))
    total = total + dot(pv[...], weight(held, sems, pieces, 0, 1))
    tok_grad[...] = (total + tok_part[...]).astype(BF)
    put_halves(info, keep, send, dot(pq[...], weight(held, sems, pieces, 1, 0)).astype(BF))
    weight(held, sems, pieces, 1, 1)


def selectors(width):
    heads = width // HD
    lane = np.arange(TILE)
    inside = lane < PARTS * heads
    first = inside[:, None] & inside[None, :] & (lane[:, None] % heads == lane[None, :] % heads)
    shifted = lane - PARTS * heads
    second = (shifted >= 0) & (shifted < PARTS * heads)
    second = second[:, None] & inside[None, :] & (shifted[:, None] % heads == lane[None, :] % heads)
    rows = [first, second]
    target = (shifted >= 0) & (shifted < PARTS * heads)
    for pair in range(heads // 2):
        head = 2 * pair + (lane >= HD)
        rows.append(target[None, :] & (head[:, None] == (shifted % heads)[None, :]))
    return jnp.asarray(np.stack(rows).astype(np.float32), BF)


def pair_units(info):
    role, quad = info[ROLE], info[WALK]
    bit = jnp.where(role == 0, lax.rem(quad, 2), quad // 2)
    step, scale = jnp.where(role == 0, 2, 1), jnp.where(role == 0, 1, 2)
    keep = [bit * scale + at * step for at in range(2)]
    send = [(1 - bit) * scale + at * step for at in range(2)]
    return keep, send


def split_pairs(info, value, keep, send, rows):
    for units, out in zip(pair_units(info), (keep, send)):
        for at, unit in enumerate(units):
            out[at, 0] = value[pl.ds(pl.multiple_of(unit * rows, rows), rows)]


def ffn_weight_grad(info, role, operands, added, after=()):
    attn_low, hid_grad, gelu_out, ffn_grad = operands
    planes, rows, cols = hid_grad.shape
    width = attn_low.shape[1]
    quarter = width // 4

    def kernel(info, which, attn_ref, hid_ref, gelu_ref, grad_ref, *refs):
        plane = pl.program_id(0)
        refs = refs[:1] * (added is not None) + refs[(added is not None) + len(after) :]

        def put(value):
            if added is None:
                refs[0][0] = value.astype(BF)
            else:
                recv, held = refs[0], refs[5]
                held[...] = (value + recv[0].astype(F32)).astype(BF)
                for side, (keep, send) in enumerate((refs[1:3], refs[3:5])):

                    @pl.when(plane // (planes // 2) == side)
                    def _(keep=keep, send=send):
                        split_pairs(info, held, keep, send, quarter)

        @pl.when(which[0] == 0)
        def _():
            put(dot_tn(attn_ref[...], hid_ref[plane]))

        @pl.when(which[0] == 1)
        def _():
            put(dot_tn(gelu_ref[plane], grad_ref[...]))

    vm, sm = pl.BlockSpec(memory_space=pltpu.VMEM), pl.BlockSpec(memory_space=pltpu.SMEM)
    block = pl.BlockSpec((1, width, cols), lambda i: (i, 0, 0))
    half = planes // 2
    pairs = [
        pl.BlockSpec((2, 1, quarter, cols), lambda i: (0, jnp.minimum(i, half - 1), 0, 0)),
        pl.BlockSpec((2, 1, quarter, cols), lambda i: (0, jnp.maximum(i - half, 0), 0, 0)),
    ]
    pair_shape = jax.ShapeDtypeStruct((2, half, quarter, cols), BF)
    args, specs = [info, role, attn_low, hid_grad, gelu_out, ffn_grad], [sm, sm] + [vm] * 4
    if added is not None:
        args.append(added)
        specs.append(block)
    return pl.pallas_call(
        kernel,
        grid=(planes,),
        out_shape=(
            jax.ShapeDtypeStruct((planes, width, cols), BF)
            if added is None
            else [pair_shape] * 4
        ),
        in_specs=specs + [pl.BlockSpec(memory_space=pl.ANY)] * len(after),
        out_specs=block if added is None else [pairs[0], pairs[0], pairs[1], pairs[1]],
        scratch_shapes=[] if added is None else [pltpu.VMEM((width, cols), BF)],
        compiler_params=pltpu.CompilerParams(vmem_limit_bytes=60 * MIB),
        cost_estimate=SMALL,
        name="ffn_weight_grad",
    )(*args, *after)


def attention_weight_grad(info, role, operands, planes, added, after=()):
    width = operands[0].shape[1]
    quarter = width // 4
    size = quarter // planes

    def kernel(info, which, kv, dk, dv, q_rows, dq, left, right, *refs):
        def put(mat, value, by_plane=False):
            if added is None:
                out, value = refs[0].at[mat], value.astype(BF)
            else:
                out = refs[3].at[mat]
            if by_plane:
                for plane in range(planes):
                    for quad in range(4):
                        at, to = (plane * 4 + quad) * size, (quad * planes + plane) * size
                        piece = value[at : at + size]
                        if added is not None:
                            piece = piece + refs[0][mat, to : to + size].astype(F32)
                        out[to : to + size] = piece.astype(BF)
            else:
                if added is not None:
                    value = value + refs[0][mat].astype(F32)
                out[...] = value.astype(BF)

        @pl.when(which[0] == 0)
        def _():
            put(0, dot_tn(kv[...], dk[...]))
            put(1, dot_tn(kv[...], dv[...]))

        @pl.when(which[0] == 1)
        def _():
            put(0, dot_tn(q_rows[...], dq[...]))
            put(1, dot_tn(left[...], right[...]), True)

        if added is not None:
            for mat in range(2):
                keep, send = refs[1].at[:, mat : mat + 1], refs[2].at[:, mat : mat + 1]
                split_pairs(info, refs[3].at[mat], keep, send, quarter)

    rows = operands[0].shape[0] + operands[3].shape[0]
    operands = [info, role] + list(operands)
    outs = [((2, width, width), BF)]
    scratch = []
    if added is not None:
        operands.append(added)
        outs = [((2, 2, quarter, width), BF)] * 2
        scratch = [pltpu.VMEM((2, width, width), BF)]
    result = call(
        kernel,
        "attention_weight_grad",
        operands,
        outs,
        scratch=scratch,
        flops=2 * rows * width * width,
        smem=2,
        after=after,
    )
    return result[0] if added is None else result


def add_pairs(info, kept, got, after=()):
    _, mats, rows, cols = kept.shape

    def kernel(info, kept_ref, got_ref, *refs):
        keep, send = refs[len(after) :]
        quad = info[WALK]
        at = jnp.where(info[ROLE] == 0, quad // 2, lax.rem(quad, 2))
        for index, out in ((at, keep), (1 - at, send)):
            out[0] = (kept_ref[index, 0].astype(F32) + got_ref[index, 0].astype(F32)).astype(BF)

    pairs = pl.BlockSpec((2, 1, rows, cols), lambda i: (0, i, 0, 0))
    one = pl.BlockSpec((1, rows, cols), lambda i: (i, 0, 0))
    return pl.pallas_call(
        kernel,
        grid=(mats,),
        out_shape=[jax.ShapeDtypeStruct((mats, rows, cols), BF)] * 2,
        in_specs=[pl.BlockSpec(memory_space=pltpu.SMEM), pairs, pairs]
        + [pl.BlockSpec(memory_space=pl.ANY)] * len(after),
        out_specs=[one, one],
        compiler_params=pltpu.CompilerParams(vmem_limit_bytes=16 * MIB),
        cost_estimate=SMALL,
        name="add_pairs",
    )(info, kept, got, *after)


def put_planes(info, held, keep, send):
    kind = lax.rem(info[PLANE], 2)
    for at in range(held.shape[0] // 2):
        keep[at] = held[2 * at + kind].astype(keep.dtype)
        send[at] = held[2 * at + 1 - kind].astype(send.dtype)


def ffn_blocks_kernel(info, kept_low, got_low, kept_high, got_high, keep, send):
    kind = lax.rem(info[PLANE], 2)
    for at, (kept, got) in enumerate(((kept_low, got_low), (kept_high, got_high))):
        for plane, out in ((kind, keep), (1 - kind, send)):
            out[at] = (kept[plane].astype(F32) + got[plane].astype(F32)).astype(out.dtype)


def attention_blocks_kernel(info, kept, got, keep, send, total, held):
    planes, _, rows, cols = held.shape
    size = rows // planes
    total[...] = kept[...].astype(F32) + got[...].astype(F32)
    for plane in range(planes):
        held[plane, 0] = total[0, :, plane * cols : (plane + 1) * cols]

    @pl.when(info[ROLE] == 0)
    def _():
        for plane in range(planes):
            held[plane, 1] = total[1, :, plane * cols : (plane + 1) * cols]

    @pl.when(info[ROLE] == 1)
    def _():
        for plane in range(planes):
            for at in range(planes):
                held[plane, 1, at * size : (at + 1) * size] = total[
                    1, plane * size : (plane + 1) * size, at * cols : (at + 1) * cols
                ]

    put_planes(info, held, keep, send)


def middle_kernel(info, kept, got, keep, send):
    mine = info[PLANE] // 2
    keep[...] = kept[mine] + got[mine].astype(F32)
    send[...] = (kept[1 - mine] + got[1 - mine].astype(F32)).astype(BF)


def ffn_total_kernel(info, own, other, keep, send, total):
    total[...] = own[...] + other[...].astype(F32)
    half = keep.shape[0]
    for index, out in ((info[ROLE], keep), (1 - info[ROLE], send)):
        out[...] = total[pl.ds(pl.multiple_of(index * half, half), half)]


def attention_total_kernel(info, own, other, keep, send, total, planes):
    total[...] = own[...] + other[...].astype(F32)
    half = keep.shape[1]
    for index, out in ((info[ROLE], keep), (1 - info[ROLE], send)):
        at = pl.ds(pl.multiple_of(index * half, half), half)
        out[0] = total[0, at]

        @pl.when(info[ROLE] == 0)
        def _(out=out, at=at):
            out[1] = total[1, at]

        @pl.when(info[ROLE] == 1)
        def _(out=out, index=index):
            size = half // planes
            for chunk in range(planes):
                start = pl.multiple_of(2 * chunk * size + index * size, size)
                out[1, chunk * size : (chunk + 1) * size] = total[1, pl.ds(start, size)]


def attention_final_kernel(info, kept, got, key_g, value_g, query_g, out_g, planes):
    def put(zero, one):
        key_g[...] = zero[0]
        value_g[...] = zero[1]
        query_g[...] = one[0]
        size = out_g.shape[0]
        chunks = [one[1, at * size : (at + 1) * size] for at in range(planes)]
        out_g[...] = jnp.concatenate(chunks, axis=1)

    @pl.when(info[ROLE] == 0)
    def _():
        put(kept, got)

    @pl.when(info[ROLE] == 1)
    def _():
        put(got, kept)


def ffn_final_kernel(info, kept, got, in_g, out_g):
    @pl.when(info[ROLE] == 0)
    def _():
        in_g[...] = kept[...]
        out_g[...] = got[...]

    @pl.when(info[ROLE] == 1)
    def _():
        in_g[...] = got[...]
        out_g[...] = kept[...]


def empty_row(width):
    heads = width // HD
    row = np.zeros((1, width + TILE), np.float32)
    row[:, width : width + heads] = NEG_FILL
    return jnp.asarray(row)


def blend_two_kernel(info, keep, got, sel, value):
    width = value.shape[1] - TILE
    tiles, lse = blend_values((keep, got), sel, width)
    for pair, tile in enumerate(tiles):
        value[:, pair * TILE : (pair + 1) * TILE] = tile
    value[:, width:] = as_parts(lse, width // HD).astype(BF)


def first_pieces(places, lengths, memory, weights, unit, block_len):
    sm, vm = pl.BlockSpec(memory_space=pltpu.SMEM), pl.BlockSpec(memory_space=pltpu.VMEM)
    rows, width = weights[0].shape
    return pl.pallas_call(
        functools.partial(first_pieces_kernel, unit=unit, block_len=block_len),
        out_shape=[
            jax.ShapeDtypeStruct((INFO,), jnp.int32),
            jax.ShapeDtypeStruct((4, rows // 4, width), BF),
            jax.ShapeDtypeStruct(memory.shape[1:], BF),
        ],
        in_specs=[sm, sm] + [pl.BlockSpec(memory_space=pl.ANY)] * 9,
        out_specs=[sm, vm, vm],
        scratch_shapes=[pltpu.SemaphoreType.DMA((5,))],
        compiler_params=pltpu.CompilerParams(vmem_limit_bytes=60 * MIB),
        cost_estimate=SMALL,
        name="first_pieces",
    )(places, lengths, memory, *weights)


def make_local(axis_seq, axis_head):
    unit = axis_seq // SLOTS
    fast = axis_seq == 8

    def swap(value, step):
        return lax.ppermute(value, "seq", [(i, i ^ step) for i in range(axis_seq)])

    def cross(value, order):
        steps = (2, 4) if order == 0 else (4, 2)
        return lax.ppermute(value, "seq", [(i, i ^ steps[i % 2]) for i in range(axis_seq)])

    def over(value, step):
        return lax.ppermute(value, "head", [(i, i ^ step) for i in range(axis_head)])

    def from_planes(value):
        got = [value]
        step = 1
        while step < axis_head:
            got += [over(value, step) if part is value else over(part, step) for part in got]
            step *= 2
        return got

    def direct_planes(value):
        return [value] + [over(value, step) for step in range(1, axis_head)]

    def local(
        tokens,
        memory,
        seq_lengths,
        pack_query,
        pack_key,
        pack_value,
        pack_out,
        unpack_query,
        unpack_key,
        unpack_value,
        unpack_out,
        ffn_in,
        ffn_in_bias,
        ffn_out,
        ffn_out_bias,
        mem_gain,
        mem_bias,
        attn_gain,
        attn_bias,
        out_gain,
        out_bias,
        cot_tokens,
        cot_memory,
    ):
        seq_index = lax.axis_index("seq")
        head_index = lax.axis_index("head")
        _, block_len, width = tokens.shape
        hidden_width = ffn_in.shape[1]
        my_lane, role = seq_index % unit, seq_index % 2
        quarter, head_cols = width // 4, width // axis_head
        info, pieces, mem = first_pieces(
            jnp.stack([seq_index, head_index]),
            seq_lengths,
            memory,
            [pack_key.T, pack_value.T, pack_query.T, pack_out]
            + [unpack_key.T, unpack_value.T, unpack_query.T, unpack_out],
            unit,
            block_len,
        )
        last = []

        def run(kernel, name, operands, outs, also=(), **more):
            after = list(last) + list(also)
            result = call(kernel, name, [info] + operands, outs, after=after, **more)
            last[:] = [result[0]]
            return result

        def run_grid(function, *operands):
            result = function(info, *operands, after=list(last))
            last[:] = [result[0] if isinstance(result, (list, tuple)) else result]
            return result

        def mine(value):
            return lax.dynamic_index_in_dim(value, head_index, 0, keepdims=False)

        def gather_unit(value):
            step = 1
            while step < unit:
                other = swap(value, step)
                low = (my_lane // step) % 2 == 0
                value = jnp.concatenate(
                    [jnp.where(low, value, other), jnp.where(low, other, value)], axis=0
                )
                step *= 2
            return value

        def scatter_unit(value, add, step):
            while step >= 1:
                half = value.shape[0] // 2
                low = (my_lane // step) % 2 == 0
                keep = jnp.where(low, value[:half], value[half:])
                send = jnp.where(low, value[half:], value[:half])
                value = add([keep, swap(send, step)])
                step //= 2
            return value

        def fetch_start(value):
            return [value] + [swap(value, j * unit) for j in range(1, SLOTS)]

        def fetch_finish(parts, also=()):
            return run(pick_kernel, "pick_slot", parts, [(parts[0].shape, BF)], also=also)[0]

        def sum_rows(values):
            total = values[0].astype(F32)
            for value in values[1:]:
                total = total + value.astype(F32)
            return total.astype(BF)

        packed_width = width + TILE
        row_count = memory.shape[1]
        slot_count = unit * row_count
        half_rows = slot_count // 2
        sel = selectors(width)
        deep = [((row_count, packed_width), BF)] * SLOTS
        flat = [((row_count, width), BF)] * SLOTS

        def blend_two(values):
            return run(blend_two_kernel, "blend", values + [sel], [(values[0].shape, BF)])[0]

        def to_slots(keep, got, kernel, extra, outs, add, empty, also=()):
            if unit > 2:
                keep = scatter_unit(add([keep, got]), add, unit // 4)
                got = jnp.broadcast_to(empty, keep.shape).astype(BF)
            scratch = [pltpu.VMEM(keep.shape, BF)] if extra else []
            parts = run(kernel, "to_slots", [keep, got] + extra, outs, scratch=scratch, also=also)
            return [parts[0]] + [swap(parts[j], j * unit) for j in range(1, SLOTS)]

        def spread(piece, first, second, third):
            parts = [piece, first, second, third]
            return parts + [swap(part, 1) for part in parts]

        def all_planes(pieces):
            return run(
                stack_kernel, "all_planes", pieces, [((axis_head,) + pieces[0].shape, BF)]
            )[0]

        held_out = pltpu.VMEM((axis_head, 4, head_cols // 4, width), BF)
        held_pair = pltpu.VMEM((2, 2) + held_out.shape, BF)
        pair_sems = pltpu.SemaphoreType.DMA((2, 2, 4 * axis_head))
        out_sems = pltpu.SemaphoreType.DMA((4 * axis_head,))
        ffn_sems = pltpu.SemaphoreType.DMA((axis_head, 8))
        tok_low, slot_low = ((block_len, width), BF), ((slot_count, width), BF)
        row_low, half_low = ((row_count, width), BF), ((half_rows, width), BF)
        tok_f32 = ((block_len, width), F32)

        mem_parts = fetch_start(mem)
        planes = from_planes(pieces)
        piece_ffn, tok, cot_tok, cot_mem = run(
            other_pieces_kernel,
            "other_pieces",
            [ffn_in_bias, ffn_in, ffn_out, tokens, cot_tokens, cot_memory],
            [((width + 16, hidden_width), BF), tok_low, tok_low, row_low],
            anys=5,
            scratch=[pltpu.SemaphoreType.DMA((6,))],
        )
        mem_picked = fetch_finish(mem_parts)
        shape = (2, axis_head) + pieces.shape[1:]
        rows_pack, rows_un = run(planes_kernel, "weight_planes", planes, [(shape, BF)] * 2)

        pack_first, pack_second = cross(rows_pack, 0), cross(rows_pack, 1)
        pack_third = cross(pack_first, 1)
        w_pack = spread(rows_pack, pack_first, pack_second, pack_third)
        rows_un = tie(rows_un, pack_third)
        un_first, un_second = cross(rows_un, 0), cross(rows_un, 1)
        ffn_rows = lax.all_gather(tie(piece_ffn, rows_pack), "head", axis=0)
        mem_slot = gather_unit(mem_picked)
        k_pack, v_pack, q_pack, keep, send = run(
            pack_forward_kernel,
            "pack_forward",
            [tok, mem_slot] + w_pack,
            [tok_low, tok_low, slot_low] + [((half_rows, packed_width), BF)] * 2,
            anys=8,
            scratch=[pltpu.VMEM((slot_count, packed_width), BF), held_pair, pair_sems],
        )
        got = swap(send, unit // 2)
        un_first = tie(un_first, keep)
        w_un = spread(rows_un, un_first, un_second, cross(un_first, 1))
        parts = to_slots(keep, got, blend_kernel, [sel], deep, blend_two, empty_row(width), [un_second])
        mem_result, mix_low, pack_ctx, pack_lse, grad_memsum, mem_vectors = run(
            memory_kernel,
            "memory_rows",
            parts + [sel, mem, cot_mem, mem_gain, mem_bias] + w_pack,
            [row_low, row_low, row_low]
            + [((row_count, TILE), F32), ((row_count, width), F32), ((8, width), F32)],
            anys=8,
            scratch=[held_out, out_sems],
            also=[w_un[3]],
        )
        mix_parts = fetch_start(mix_low)
        mix_picked = fetch_finish(mix_parts, w_un)
        ffn_rows = tie(ffn_rows, mix_picked)
        ffn_parts = [ffn_rows, swap(ffn_rows, 1)]
        mix_slot = gather_unit(mix_picked)
        k_un, v_un, q_un, tok_ctx, tok_lse, attn_normed, attn_inv = run(
            unpack_forward_kernel,
            "unpack_forward",
            [tok, mix_slot] + w_un,
            [slot_low, slot_low, tok_low, tok_low]
            + [((16, block_len), F32), tok_f32, ((block_len, 1), F32)],
            anys=8,
            scratch=[held_pair, pair_sems],
        )
        by_plane = (axis_head, block_len, hidden_width)
        held_ffn = pltpu.VMEM((2, axis_head, width, hidden_width), BF)
        out_result, attn_low, gelu_out, slope, grad_sum, out_vectors = run(
            ffn_forward_kernel,
            "ffn_forward",
            [attn_normed, cot_tok, mem_result]
            + [attn_gain, attn_bias, out_gain, out_bias, ffn_out_bias]
            + ffn_parts,
            [((block_len + row_count, width), BF)]
            + [tok_low, (by_plane, BF), (by_plane, BF), tok_f32, ((8, width), F32)],
            anys=2,
            scratch=[
                held_ffn,
                pltpu.VMEM((axis_head, 16, hidden_width), BF),
                pltpu.VMEM((block_len, width), F32),
                ffn_sems,
                pltpu.SemaphoreType.DMA((axis_head,)),
            ],
        )
        out_rows = lax.all_gather(out_result, "head", axis=0)
        out_tokens, out_memory = out_rows[:, :block_len], out_rows[:, block_len:]
        hid_grad, ffn_grad, mix_grad, mix_sum, attn_vectors, hid_vec = run(
            ffn_backward_kernel,
            "ffn_backward",
            [grad_sum, attn_normed, attn_inv, slope, attn_gain] + ffn_parts,
            [(by_plane, BF), tok_low, tok_low, tok_f32, ((8, width), F32)]
            + [((axis_head, 1, hidden_width), F32)],
            anys=2,
            scratch=[held_ffn, pltpu.VMEM((block_len, width), F32), ffn_sems],
        )

        role_info, other_info = role[None], 1 - role[None]
        ffn_operands = (attn_low, hid_grad, gelu_out, ffn_grad)

        def vectors_step(value, other):
            return run(total_kernel, "vectors", [value, other], [(value.shape, F32)])[0]

        if fast:
            ffn_sent = run_grid(ffn_weight_grad, other_info, ffn_operands, None)
            ffn_got = swap(ffn_sent, 1)
        small = run(
            vectors_kernel,
            "vectors",
            [mem_vectors, out_vectors, attn_vectors, hid_vec],
            [((16, width), F32)],
        )[0]
        small_got = swap(small, 1)
        uq_grad, uk_part, uv_part, keep, send, tok_part = run(
            unpack_backward_kernel,
            "unpack_backward",
            [q_un, k_un, v_un, tok_ctx, tok_lse, mix_grad, mix_sum] + w_un,
            [tok_low, slot_low, slot_low, half_low, half_low, tok_f32],
            anys=8,
            scratch=[held_pair, pair_sems],
        )
        un_operands = (mix_slot, uk_part, uv_part, tok, uq_grad, tok_ctx, mix_grad)
        got = swap(send, unit // 2)
        small = vectors_step(small, small_got)
        parts = to_slots(keep, got, sum_kernel, [], flat, sum_rows, jnp.zeros((), BF))
        small_got = swap(small, 2)
        if fast:
            ffn_low, low_sent, ffn_high, high_sent = run_grid(
                ffn_weight_grad, role_info, ffn_operands, ffn_got
            )
        mem_mix_grad, packed = run(
            memory_back_kernel,
            "memory_rows_backward",
            parts + [sel, grad_memsum, pack_ctx, pack_lse] + w_pack,
            [row_low, ((row_count, packed_width), BF)],
            anys=8,
            scratch=[held_out, out_sems],
        )
        back_parts = fetch_start(packed)
        small = vectors_step(small, small_got)
        step = 4
        while step < axis_seq:
            small_got = swap(small, step)
            if fast:
                un_sent = run_grid(attention_weight_grad, other_info, un_operands, axis_head, None)
                un_kept, un_sent = run_grid(
                    attention_weight_grad, role_info, un_operands, axis_head, swap(un_sent, 1)
                )
            small = vectors_step(small, small_got)
            step *= 2
        back_picked = fetch_finish(back_parts)
        if fast:
            un_got = cross(tie(un_sent, back_picked), 0)
            low_got = cross(tie(low_sent, back_picked), 0)
        back = gather_unit(back_picked)
        pq_part, pk_grad, pv_grad, grad_tokens, keep, send = run(
            pack_backward_kernel,
            "pack_backward",
            [back, sel, q_pack, k_pack, v_pack, tok_part] + w_pack,
            [slot_low, tok_low, tok_low, tok_low, half_low, half_low],
            anys=8,
            scratch=[held_pair, pair_sems],
            also=[out_rows],
        )
        grad_tokens = lax.all_gather(grad_tokens, "head", axis=0)
        pack_operands = (tok, pk_grad, pv_grad, mem_slot, pq_part, pack_ctx, mem_mix_grad)
        got = swap(send, unit // 2)
        if fast:
            un_kept, un_sent = run_grid(add_pairs, un_kept, un_got)
            un_got = cross(un_sent, 1)
            ffn_low, low_sent = run_grid(add_pairs, ffn_low, low_got)
            high_got = cross(tie(high_sent, ffn_low), 0)
        if fast:
            pack_sent = run_grid(attention_weight_grad, other_info, pack_operands, axis_head, None)
            pack_got = swap(pack_sent, 1)
        parts = to_slots(keep, got, sum_kernel, [], flat, sum_rows, jnp.zeros((), BF))

        rows = (quarter, hidden_width)
        half = (quarter // 2, hidden_width)
        pair_rows = (2, quarter, head_cols)
        pair_half = (2, quarter // 2, head_cols)

        def pairs_of(shape):
            return [((2,) + shape, F32), ((2,) + shape, BF)]

        def middle(kept, got, shape):
            keep, send = run(
                middle_kernel, "plane_middle", [kept, got], [(shape, F32), (shape, BF)]
            )
            return keep, over(send, 2)

        def ffn_blocks(kept, got):
            operands = [kept[0], got[0], kept[1], got[1]]
            keep, send = run(ffn_blocks_kernel, "plane_blocks", operands, pairs_of(rows))
            return keep, over(send, 1)

        def ffn_total(kept, got):
            scratch = [pltpu.VMEM(rows, F32)]
            keep, send = run(
                ffn_total_kernel, "plane_total", [kept, got], [(half, F32)] * 2, scratch=scratch
            )
            return [keep, swap(send, 1)]

        def ffn_final(halves):
            return run(ffn_final_kernel, "weight_rows", halves, [(half, F32)] * 2)

        def attention_blocks(kept, got):
            keep, send = run(
                attention_blocks_kernel,
                "plane_blocks",
                [kept, got],
                pairs_of(pair_rows),
                scratch=[
                    pltpu.VMEM((2, quarter, width), F32),
                    pltpu.VMEM((axis_head,) + pair_rows, F32),
                ],
            )
            return keep, over(send, 1)

        def attention_total(kept, got):
            keep, send = run(
                functools.partial(attention_total_kernel, planes=axis_head),
                "plane_total",
                [kept, got],
                [(pair_half, F32)] * 2,
                scratch=[pltpu.VMEM(pair_rows, F32)],
            )
            return [keep, swap(send, 1)]

        def attention_final(halves):
            return run(
                functools.partial(attention_final_kernel, planes=axis_head),
                "weight_rows",
                halves,
                [(pair_half[1:], F32)] * 3 + [((quarter // 2 // axis_head, width), F32)],
            )

        def scatter(value, axis, dim):
            return lax.psum_scatter(value, axis, scatter_dimension=dim, tiled=True)

        def by_columns(grad):
            grad = scatter(grad, "seq", 0).reshape(-1, axis_head, head_cols)
            return scatter(grad.transpose(1, 0, 2), "head", 0)[0].astype(F32)

        def by_rows(grad):
            grad = scatter(grad.reshape(axis_head, -1, width), "seq", 1)
            return scatter(grad, "head", 0)[0].astype(F32)

        def product(left, right):
            return dot_tn(left, right).astype(BF)

        def attention_simple(operands):
            kv, dk, dv, q_rows, dq, left, right = operands
            first = [by_columns(product(a, b)) for a, b in ((kv, dk), (kv, dv), (q_rows, dq))]
            return first + [by_rows(product(left, right))]

        if fast:
            pack_kept, pack_sent = run_grid(
                attention_weight_grad, role_info, pack_operands, axis_head, pack_got
            )
            pack_got = cross(pack_sent, 0)
            ffn_high, high_sent = run_grid(add_pairs, ffn_high, high_got)
            low_got, high_got = cross(tie(low_sent, ffn_high), 1), cross(high_sent, 1)
            un_blocks = attention_blocks(un_kept, un_got)
        total = run(memory_total_kernel, "memory_total", [grad_memsum] + parts, [row_low])[0]
        grad_planes = from_planes(total)
        small_planes = direct_planes(tie(small, total))
        if fast:
            un_blocks = middle(*un_blocks, pair_rows)
            pack_kept, pack_sent = run_grid(add_pairs, pack_kept, pack_got)
            pack_got = cross(pack_sent, 1)
            blocks = ffn_blocks([ffn_low, ffn_high], [low_got, high_got])
            un_halves = attention_total(*un_blocks)
            pack_blocks = attention_blocks(pack_kept, pack_got)
            blocks = middle(*blocks, rows)
            un_grads = attention_final(un_halves)
            pack_blocks = middle(*pack_blocks, pair_rows)
            halves = ffn_total(*blocks)
            grad_memory = all_planes(grad_planes)
            pack_halves = attention_total(*pack_blocks)
            fi_grad, fo_grad = ffn_final(halves)
            pack_grads = attention_final(pack_halves)
        else:
            grad_memory = all_planes(grad_planes)
            un_grads = attention_simple(un_operands)
            pack_grads = attention_simple(pack_operands)
            fi_grad = jnp.stack([product(attn_low, hid_grad[p]) for p in range(axis_head)])
            fi_grad = scatter(scatter(fi_grad, "seq", 1), "head", 0)[0].astype(F32)
            fo_grad = jnp.stack([product(gelu_out[p], ffn_grad) for p in range(axis_head)])
            fo_grad = scatter(scatter(fo_grad, "seq", 1), "head", 0)[0].astype(F32)

        small = run(
            plane_vectors_kernel,
            "vectors",
            small_planes,
            [(small.shape, F32)],
            scratch=[pltpu.VMEM((axis_head,) + small.shape, F32)],
        )[0]
        share = width // axis_seq
        vectors = lax.dynamic_slice_in_dim(small[:7], seq_index * share, share, 1)
        fib = mine(small[7 : 7 + axis_head].reshape(axis_head, -1))
        fib = lax.dynamic_slice_in_dim(fib, seq_index * share, share, 0)
        return (
            out_tokens,
            out_memory,
            grad_tokens,
            grad_memory,
            pack_grads[2],
            pack_grads[0],
            pack_grads[1],
            pack_grads[3],
            un_grads[2],
            un_grads[0],
            un_grads[1],
            un_grads[3],
            fi_grad,
            fib,
            fo_grad,
            vectors[0],
            vectors[1],
            vectors[2],
            vectors[3],
            vectors[4],
            vectors[5],
            vectors[6],
        )

    return local


def solution(mesh):
    rows = P(None, "seq", None)
    by_col, by_row, both = P(None, "head"), P("head", None), P("seq", "head")
    wide_rows = P(("head", "seq"), None)
    in_specs = (
        (rows, rows, P())
        + (by_col, by_col, by_col, by_row)
        + (by_col, by_col, by_col, by_row)
        + (by_col, P("head"), by_row)
        + (P(),) * 7
        + (rows, rows)
    )
    out_specs = (
        (rows,) * 4
        + (both, both, both, wide_rows)
        + (both, both, both, wide_rows)
        + (both, P(("head", "seq")), wide_rows)
        + (P("seq"),) * 7
    )
    local = make_local(mesh.shape["seq"], mesh.shape["head"])
    return jax.shard_map(local, mesh=mesh, in_specs=in_specs, out_specs=out_specs, check_vma=False)
```

time: 895 us -> 475 us (0.53)
  waiting for transfers between devices: 457 us -> 173 us
  Pallas kernels: 0 us -> 165 us
  local copies, waits for them, and re-layouts: 145 us -> 36.3 us
  matrix products: 105 us -> 0 us
  blocking collectives: 98.2 us -> 0 us
  starting transfers between devices: 24.4 us -> 72.5 us
  other arithmetic: 34.9 us -> 3.1 us
    reduce_scatter x6 -> x0, waiting for transfers between devices: 198 us -> none  [scatter(): return lax.psum_scatter(value, axis, scatter_dimension=dim, tiled=True)]
    pallas_call x0 -> x55, Pallas kernels: none -> 165 us  [the longest x39 140 us: call(): pl.pallas_call(body, out_shape=[jax.ShapeDtypeStruct(s, d) for s, d in ou...]
    all_gather x5 -> x2, waiting for transfers between devices: 147 us -> 6.17 us  [the longest x1 5.92 us: local(): ffn_rows = lax.all_gather(tie(piece_ffn, rows_pack), 'head', axis=0)]
    dot_general x42 -> x0, matrix products: 105 us -> none  [the longest x10 28.3 us: mm(): return jnp.dot(left, right, preferred_element_type=F32)]
    ppermute x0 -> x29, waiting for transfers between devices: none -> 104 us  [the longest x15 66.7 us: over(): lax.ppermute(value, 'head', [(i, i ^ step) for i in range(axis_head)])]
    all_gather x1, waiting for transfers between devices: 64.3 us -> 0.01 us  [local(): grad_tokens = lax.all_gather(grad_tokens, 'head', axis=0)]
    all_gather x3 -> x0, blocking collectives: 58 us -> none  [the longest x1 22.7 us: local(): out_memory = lax.all_gather(mem_result.astype(BF), 'head', axis=0)]
    ppermute x0 -> x29, starting transfers between devices: none -> 41.5 us  [the longest x15 22.5 us: over(): lax.ppermute(value, 'head', [(i, i ^ step) for i in range(axis_head)])]
  transfers between devices with their start and end apart: 38 -> 74, of which waited for: 23 -> 30; matrix products, arithmetic and copies ran while one was open for 22% -> 2% of each run, Pallas kernels for 0% -> 25%
where the time goes in v3:
time: 475 us; the launch traced here: 465 us
  waiting for transfers between devices  173 us (36%)
  Pallas kernels  165 us (35%)
  starting transfers between devices  72.5 us (15%)
  local copies, waits for them, and re-layouts  36.3 us (8%)
  between operations  15.3 us (3%)
    pallas_call x39, Pallas kernels, call(): pl.pallas_call(body, out_shape=[jax.ShapeDtypeStruct(s, d) for s, d in ou...  140 us
    ppermute x15, waiting for transfers between devices, over(): lax.ppermute(value, 'head', [(i, i ^ step) for i in range(axis_head)])  66.7 us
    ppermute x42, waiting for transfers between devices, swap(): return lax.ppermute(value, 'seq', [(i, i ^ step) for i in range(axis_seq)])  63.2 us
    ppermute x14, waiting for transfers between devices, cross(): lax.ppermute(value, 'seq', [(i, i ^ steps[i % 2]) for i in range(axis_seq)])  36.8 us
    ppermute x42, starting transfers between devices, swap(): return lax.ppermute(value, 'seq', [(i, i ^ step) for i in range(axis_seq)])  30.5 us
    unnamed x159, local copies, waits for them, and re-layouts  29.8 us
    ppermute x15, starting transfers between devices, over(): lax.ppermute(value, 'head', [(i, i ^ step) for i in range(axis_head)])  22.5 us
    ppermute x14, starting transfers between devices, cross(): lax.ppermute(value, 'seq', [(i, i ^ steps[i % 2]) for i in range(axis_seq)])  19 us
  transfers between devices with their start and end apart: 74, of which 30 were waited for; matrix products, arithmetic and copies ran while one was open for 2% of the time, Pallas kernels for 25%

profile of v3, /device:TPU:0, one launch (start us, length us, event | category | flops | bytes accessed | tf_op | source)
XLA Modules:
  0.0 465.3 jit_solution(14692248049130687572)
XLA Ops:
  16.1 10.8 %collective-permute-done.4.refs_2_ = bf16[4,48,768]{2,1,0:T(8,128)(2,1)S(1)} collective-permute-done((bf16[4,48,768]{2,1,0:T(8,128)(2,1)}, bf16[4,48,768]{2,1,0:T(8,128)(2,1)S(1)}, u32[]{:S(2)}, u32[]{:S(2)}) %collective-permute-start.4) | collective-permute-done | bytes 294944 | tf_op jit(solution)/shard_map/ppermute | solution.py:976
  46.0 12.9 %collective-permute-done.7.refs_4_.refs_11_.refs_10_.refs_8_ = bf16[2,4,48,768]{3,2,1,0:T(8,128)(2,1)S(1)} collective-permute-done((bf16[2,4,48,768]{3,2,1,0:T(8,128)(2,1)S(1)}, bf16[2,4,48,768]{3,2,1,0:T(8,128)(2,1)S(1)}, u32[]{:S(2)}, u32[]{:S(2)}) %collective-permute-start.7) | collective-permute-done | bytes 589856 | tf_op jit(solution)/shard_map/ppermute | solution.py:973
  61.1 7.7 %collective-permute-done.9.refs_6_.refs_1_.refs_13_.refs_12_.refs_10_ = bf16[2,4,48,768]{3,2,1,0:T(8,128)(2,1)S(1)} collective-permute-done((bf16[2,4,48,768]{3,2,1,0:T(8,128)(2,1)S(1)}, bf16[2,4,48,768]{3,2,1,0:T(8,128)(2,1)S(1)}, u32[]{:S(2)}, u32[]{:S(2)}) %collective-permute-start.9) | collective-permute-done | bytes 589856 | tf_op jit(solution)/shard_map/ppermute | solution.py:973
  72.4 12.4 %pack_forward.1 = (bf16[512,768]{1,0:T(8,128)(2,1)}, bf16[512,768]{1,0:T(8,128)(2,1)}, bf16[256,768]{1,0:T(8,128)(2,1)}, bf16[128,896]{1,0:T(8,128)(2,1)}, bf16[128,896]{1,0:T(8,128)(2,1)}) custom-call(s32[16]{0:T(128)} %get-tuple-element.131.refs_0_.info, bf16[512,768]{1,0:T(8,128)(2,1)} %get-tuple-element.132.refs_1_.refs_5_.refs_2_, ...), custom_call_target="tpu_custom_call" | custom-call | flops 1 | bytes 1 | tf_op jit(solution)/shard_map/pack_forward/pallas_call | solution.py:50
  93.5 5.9 %collective-permute-done.16.refs_2_ = bf16[128,896]{1,0:T(8,128)(2,1)S(1)} collective-permute-done((bf16[128,896]{1,0:T(8,128)(2,1)S(1)}, bf16[128,896]{1,0:T(8,128)(2,1)S(1)}, u32[]{:S(2)}, u32[]{:S(2)}) %collective-permute-start.16) | collective-permute-done | bytes 229408 | tf_op jit(solution)/shard_map/ppermute | solution.py:969
  102.8 5.9 %collective-permute-done.18.refs_4_ = bf16[128,896]{1,0:T(8,128)(2,1)S(1)} collective-permute-done((bf16[128,896]{1,0:T(8,128)(2,1)S(1)}, bf16[128,896]{1,0:T(8,128)(2,1)S(1)}, u32[]{:S(2)}, u32[]{:S(2)}) %collective-permute-start.18) | collective-permute-done | bytes 229408 | tf_op jit(solution)/shard_map/ppermute | solution.py:969
  128.2 5.9 %all-gather.7.cloned.1.call-done = bf16[3136,768]{1,0:T(8,128)(2,1)} async-done(((bf16[784,768]{1,0:T(8,128)(2,1)}), bf16[3136,768]{1,0:T(8,128)(2,1)}) %all-gather.7.cloned.1.call-update) | async-done | bytes 4816912 | tf_op jit(solution)/shard_map/all_gather | solution.py:1134
  134.6 5.9 %collective-permute-done.28 = bf16[128,768]{1,0:T(8,128)(2,1)S(1)} collective-permute-done((bf16[128,768]{1,0:T(8,128)(2,1)S(1)}, bf16[128,768]{1,0:T(8,128)(2,1)S(1)}, u32[]{:S(2)}, u32[]{:S(2)}) %collective-permute-start.28) | collective-permute-done | bytes 196640 | tf_op jit(solution)/shard_map/ppermute | solution.py:969
  141.4 12.4 %unpack_forward.1 = (bf16[256,768]{1,0:T(8,128)(2,1)}, bf16[256,768]{1,0:T(8,128)(2,1)}, bf16[512,768]{1,0:T(8,128)(2,1)}, bf16[512,768]{1,0:T(8,128)(2,1)}, f32...) custom-call(s32[16]{0:T(128)} %get-tuple-element.131.refs_0_.info, ...), custom_call_target="tpu_custom_call" | custom-call | flops 1 | bytes 1 | tf_op jit(solution)/shard_map/unpack_forward/pallas_call | solution.py:50
  153.8 17.6 %ffn_forward.1 = (bf16[640,768]{1,0:T(8,128)(2,1)}, bf16[512,768]{1,0:T(8,128)(2,1)}, bf16[4,512,768]{2,1,0:T(8,128)(2,1)}, bf16[4,512,768]{2,1,0:T(8,128)(2,1)}, f32[512,768]{1,0:T(8,128)}, /*index=5*/f32[8,768]{1,0:T(8,128)}) custom-call(s32[16]{0:T(128)} %get-tuple-element.131.refs_0_.info, f32[512,768]{1,0:T(8,128)} %get-tuple-element.148.refs_1_.refs_2_, ...), custom_call_target="tpu_custom_call" | custom-call | flops 1 | bytes 1 | tf_op jit(solution)/shard_map/ffn_forward/pallas_call | solution.py:50
  171.5 13.1 %ffn_backward.1 = (bf16[4,512,768]{2,1,0:T(8,128)(2,1)}, bf16[512,768]{1,0:T(8,128)(2,1)}, bf16[512,768]{1,0:T(8,128)(2,1)}, f32[512,768]{1,0:T(8,128)}, f32[8,768]{1,0:T(8,128)}, /*index=5*/f32[4,1,768]{2,1,0:T(1,128)}) custom-call(s32[16]{0:T(128)} %get-tuple-element.131.refs_0_.info, f32[512,768]{1,0:T(8,128)} %get-tuple-element.156.refs_1_, ...), custom_call_target="tpu_custom_call" | custom-call | flops 1 | bytes 1 | tf_op jit(solution)/shard_map/ffn_backward/pallas_call | solution.py:50
  184.7 8.0 %ffn_weight_grad.2.refs_5_ = bf16[4,768,768]{2,1,0:T(8,128)(2,1)} custom-call(s32[16]{0:T(128)} %get-tuple-element.131.refs_0_.info, s32[1]{0:T(128)S(6)} %sub.7.which.refs_1_, bf16[512,768]{1,0:T(8,128)(2,1)} %get-tuple-element.165.attn_ref, bf16[4,512,768]{2,1,0:T(8,128)(2,1)} %get-tuple-element.166.hid_ref.refs_0_, ...), custom_call_target="tpu_custom_call" | custom-call | flops 1 | bytes 1 | tf_op jit(solution)/shard_map/ffn_weight_grad/pallas_call | solution.py:729
  197.2 15.7 %unpack_backward.1 = (bf16[512,768]{1,0:T(8,128)(2,1)}, bf16[256,768]{1,0:T(8,128)(2,1)}, bf16[256,768]{1,0:T(8,128)(2,1)}, bf16[128,768]{1,0:T(8,128)(2,1)}, bf...) custom-call(s32[16]{0:T(128)} %get-tuple-element.131.refs_0_.info, bf16[512,768]{1,0:T(8,128)(2,1)} %get-tuple-element.152.refs_1_, ...), custom_call_target="tpu_custom_call" | custom-call | flops 1 | bytes 1 | tf_op jit(solution)/shard_map/unpack_backward/pallas_call | solution.py:50
  223.6 9.7 %ffn_weight_grad.3 = (bf16[2,2,192,768]{3,2,1,0:T(8,128)(2,1)}, bf16[2,2,192,768]{3,2,1,0:T(8,128)(2,1)}, bf16[2,2,192,768]{3,2,1,0:T(8,128)(2,1)}, bf16[2,2,192,768]{3,2,1,0:T(8,128)(2,1)}) custom-call(s32[16]{0:T(128)} %get-tuple-element.131.refs_0_.info, s32[1]{0:T(128)} %bitcast.10.which.refs_1_, bf16[512,768]{1,0:T(8,128)(2,1)} %get-tuple-element.165.attn_ref, ...), custom_call_target="tpu_custom_call" | custom-call | flops 1 | bytes 1 | tf_op jit(solution)/shard_map/ffn_weight_grad/pallas_call | solution.py:729
  268.2 13.0 %pack_backward.1 = (bf16[256,768]{1,0:T(8,128)(2,1)}, bf16[512,768]{1,0:T(8,128)(2,1)}, bf16[512,768]{1,0:T(8,128)(2,1)}, bf16[512,768]{1,0:T(8,128)(2,1)}, bf16...) custom-call(s32[16]{0:T(128)} %get-tuple-element.131.refs_0_.info, bf16[256,896]{1,0:T(8,128)(2,1)} %pad_maximum_fusion.refs_1_, ...), custom_call_target="tpu_custom_call" | custom-call | flops 1 | bytes 1 | tf_op jit(solution)/shard_map/pack_backward/pallas_call | solution.py:50
  284.4 7.5 %collective-permute-done.44.got_ref = bf16[2,2,192,768]{3,2,1,0:T(8,128)(2,1)S(1)} collective-permute-done((bf16[2,2,192,768]{3,2,1,0:T(8,128)(2,1)S(1)}, bf16[2,2,192,768]{3,2,1,0:T(8,128)(2,1)S(1)}, u32[]{:S(2)}, u32[]{:S(2)}) %collective-permute-start.44) | collective-permute-done | bytes 1179680 | tf_op jit(solution)/shard_map/ppermute | solution.py:973
  305.8 6.3 %attention_weight_grad.7 = (bf16[2,2,192,768]{3,2,1,0:T(8,128)(2,1)}, bf16[2,2,192,768]{3,2,1,0:T(8,128)(2,1)}) custom-call(s32[16]{0:T(128)} %get-tuple-element.131.refs_0_.info, s32[1]{0:T(128)} %bitcast.10.which.refs_1_, bf16[512,768]{1,0:T(8,128)(2,1)} %get-tuple-element.132.refs_1_.refs_5_.refs_2_, bf16[512,768]{1,0:T(8,128)(2,1)} %get-tuple-element.191.refs_3_, ...), custom_call_target="tpu_custom_call" | custom-call | flops 1 | bytes 1 | tf_op jit(solution)/shard_map/attention_weight_grad/pallas_call | solution.py:50
  321.7 8.2 %collective-permute-done.49.refs_2_ = bf16[2,192,768]{2,1,0:T(8,128)(2,1)S(1)} collective-permute-done((bf16[2,192,768]{2,1,0:T(8,128)(2,1)}, bf16[2,192,768]{2,1,0:T(8,128)(2,1)S(1)}, u32[]{:S(2)}, u32[]{:S(2)}) %collective-permute-start.49) | collective-permute-done | bytes 589856 | tf_op jit(solution)/shard_map/ppermute | solution.py:973
  332.4 12.8 %collective-permute-done.46.refs_3_ = bf16[128,768]{1,0:T(8,128)(2,1)S(1)} collective-permute-done((bf16[128,768]{1,0:T(8,128)(2,1)S(1)}, bf16[128,768]{1,0:T(8,128)(2,1)S(1)}, u32[]{:S(2)}, u32[]{:S(2)}) %collective-permute-start.46) | collective-permute-done | bytes 196640 | tf_op jit(solution)/shard_map/ppermute | solution.py:969
  352.9 6.4 %collective-permute-done.48.refs_5_ = bf16[128,768]{1,0:T(8,128)(2,1)S(1)} collective-permute-done((bf16[128,768]{1,0:T(8,128)(2,1)S(1)}, bf16[128,768]{1,0:T(8,128)(2,1)S(1)}, u32[]{:S(2)}, u32[]{:S(2)}) %collective-permute-start.48) | collective-permute-done | bytes 196640 | tf_op jit(solution)/shard_map/ppermute | solution.py:969
  359.9 6.5 %collective-permute-done.58.refs_2_ = bf16[2,2,192,192]{3,2,1,0:T(8,128)(2,1)S(1)} collective-permute-done((bf16[2,2,192,192]{3,2,1,0:T(8,128)(2,1)S(1)}, bf16[2,2,192,192]{3,2,1,0:T(8,128)(2,1)S(1)}, u32[]{:S(2)}, u32[]{:S(2)}) %collective-permute-start.58) | collective-permute-done | bytes 294944 | tf_op jit(solution)/shard_map/ppermute | solution.py:976
  373.4 15.1 %collective-permute-done.61.refs_2_ = bf16[2,192,192]{2,1,0:T(8,128)(2,1)S(1)} collective-permute-done((bf16[2,192,192]{2,1,0:T(8,128)(2,1)S(1)}, bf16[2,192,192]{2,1,0:T(8,128)(2,1)S(1)}, u32[]{:S(2)}, u32[]{:S(2)}) %collective-permute-start.61) | collective-permute-done | bytes 147488 | tf_op jit(solution)/shard_map/ppermute | solution.py:976
  396.4 20.2 %collective-permute-done.52.refs_2_ = bf16[128,768]{1,0:T(8,128)(2,1)S(1)} collective-permute-done((bf16[128,768]{1,0:T(8,128)(2,1)S(1)}, bf16[128,768]{1,0:T(8,128)(2,1)S(1)}, u32[]{:S(2)}, u32[]{:S(2)}) %collective-permute-start.52) | collective-permute-done | bytes 196640 | tf_op jit(solution)/shard_map/ppermute | solution.py:976
  423.3 9.1 %collective-permute-done.54.refs_4_ = bf16[128,768]{1,0:T(8,128)(2,1)S(1)} collective-permute-done((bf16[128,768]{1,0:T(8,128)(2,1)S(1)}, bf16[128,768]{1,0:T(8,128)(2,1)S(1)}, u32[]{:S(2)}, u32[]{:S(2)}) %collective-permute-start.54) | collective-permute-done | bytes 196640 | tf_op jit(solution)/shard_map/ppermute | solution.py:976
  (354 shorter events, 200.8 us)
Async XLA Ops:
  7.2 126.9 %all-gather.7.cloned.1.call-start = ((), (), s32[]{:S(2)}) async-start(), calls=%async_computation | async-start | bytes 6021120 | tf_op jit(solution)/shard_map/all_gather | solution.py:1134
  13.5 26.2 %collective-permute-start.5 = (bf16[4,48,768]{2,1,0:T(8,128)(2,1)}, bf16[4,48,768]{2,1,0:T(8,128)(2,1)S(1)}, u32[]{:S(2)}, u32[]{:S(2)}) collective-permute-start(bf16[4,48,768]{2,1,0:T(8,128)(2,1)} %get-tuple-element.135.refs_1_), channel_id=1, source_target_pairs={{0,2},{1,3},{2,0},{3,1},{4,6},{5,7},{6,4},{7,5},{8,10},{9,11},{10,... | collective-permute-start | bytes 884744 | tf_op jit(solution)/shard_map/ppermute | solution.py:976
  42.8 225.3 %all-gather.9.cloned.1.call-start = ((), (), s32[]{:S(2)}) async-start(), calls=%async_computation.1 | async-start | bytes 4915200 | tf_op jit(solution)/shard_map/all_gather | solution.py:1191
  92.4 22.5 %collective-permute-start.24 = (bf16[2,4,48,768]{3,2,1,0:T(8,128)(2,1)S(1)}, bf16[2,4,48,768]{3,2,1,0:T(8,128)(2,1)S(1)}, u32[]{:S(2)}, u32[]{:S(2)}) collective-permute-start(bf16[2,4,48,768]{3,2,1,0:T(8,128)(2,1)S(1)} %tie.9.refs_6_.refs_3_.refs_8_), channel_id=1, source_target_pairs={{0,4},{4,0},{8,12},{12,8},{16,20},{20,16},{24,28},{28,24},{1,5},{5... | collective-permute-start | bytes 1769480 | tf_op jit(solution)/shard_map/ppermute | solution.py:969
  92.4 23.2 %collective-permute-start.25 = (bf16[2,4,48,768]{3,2,1,0:T(8,128)(2,1)S(1)}, bf16[2,4,48,768]{3,2,1,0:T(8,128)(2,1)S(1)}, u32[]{:S(2)}, u32[]{:S(2)}) collective-permute-start(bf16[2,4,48,768]{3,2,1,0:T(8,128)(2,1)S(1)} %tie.10.refs_7_.refs_4_.refs_9_), channel_id=1, source_target_pairs={{0,4},{4,0},{8,12},{12,8},{16,20},{20,16},{24,28},{28,24},{1,5},{5... | collective-permute-start | bytes 1769480 | tf_op jit(solution)/shard_map/ppermute | solution.py:969
  99.8 24.6 %collective-permute-start.27 = (bf16[2,4,48,768]{3,2,1,0:T(8,128)(2,1)S(1)}, bf16[2,4,48,768]{3,2,1,0:T(8,128)(2,1)}, u32[]{:S(2)}, u32[]{:S(2)}) collective-permute-start(bf16[2,4,48,768]{3,2,1,0:T(8,128)(2,1)S(1)} %collective-permute-done.20.refs_19_.refs_9_.refs_6_.refs_11_), channel_id=1, source_target_pairs={{0,4},{4,0},{8,12},{12,8},{16,20},{20,16},{24,28},{28,24},{1,5},{5... | collective-permute-start | bytes 1769480 | tf_op jit(solution)/shard_map/ppermute | solution.py:969
  134.1 19.7 %collective-permute-start.29 = (bf16[4,784,768]{2,1,0:T(8,128)(2,1)}, bf16[4,784,768]{2,1,0:T(8,128)(2,1)}, u32[]{:S(2)}, u32[]{:S(2)}) collective-permute-start(bf16[4,784,768]{2,1,0:T(8,128)(2,1)} %tie.12.refs_9_.refs_6_), channel_id=1, source_target_pairs={{0,4},{4,0},{8,12},{12,8},{16,20},{20,16},{24,28},{28,24},{1,5},{5... | collective-permute-start | bytes 14450696 | tf_op jit(solution)/shard_map/ppermute | solution.py:969
  192.6 31.0 %collective-permute-start.35 = (bf16[4,768,768]{2,1,0:T(8,128)(2,1)}, bf16[4,768,768]{2,1,0:T(8,128)(2,1)}, u32[]{:S(2)}, u32[]{:S(2)}) collective-permute-start(bf16[4,768,768]{2,1,0:T(8,128)(2,1)} %ffn_weight_grad.2.refs_5_), channel_id=1, source_target_pairs={{0,4},{4,0},{8,12},{12,8},{16,20},{20,16},{24,28},{28,24},{1,5},{5... | collective-permute-start | bytes 14155784 | tf_op jit(solution)/shard_map/ppermute | solution.py:969
  193.1 255.5 %all-gather.11.cloned.1.call-start = ((), (), s32[]{:S(2)}) async-start(), calls=%async_computation.2 | async-start | bytes 3932160 | tf_op jit(solution)/shard_map/all_gather | solution.py:1270
  264.3 27.7 %collective-permute-start.44 = (bf16[2,2,192,768]{3,2,1,0:T(8,128)(2,1)S(1)}, bf16[2,2,192,768]{3,2,1,0:T(8,128)(2,1)S(1)}, u32[]{:S(2)}, u32[]{:S(2)}) collective-permute-start(bf16[2,2,192,768]{3,2,1,0:T(8,128)(2,1)S(1)} %tie.13), channel_id=1, source_target_pairs={{0,8},{4,20},{8,0},{12,28},{16,24},{20,4},{24,16},{28,12},{1,9},{5... | collective-permute-start | bytes 3538952 | tf_op jit(solution)/shard_map/ppermute | solution.py:973
  312.0 55.0 %collective-permute-start.57 = (bf16[2,2,192,768]{3,2,1,0:T(8,128)(2,1)}, bf16[2,2,192,768]{3,2,1,0:T(8,128)(2,1)S(1)}, u32[]{:S(2)}, u32[]{:S(2)}) collective-permute-start(bf16[2,2,192,768]{3,2,1,0:T(8,128)(2,1)} %get-tuple-element.210), channel_id=1, source_target_pairs={{0,8},{4,20},{8,0},{12,28},{16,24},{20,4},{24,16},{28,12},{1,9},{5... | collective-permute-start | bytes 3538952 | tf_op jit(solution)/shard_map/ppermute | solution.py:973
  318.2 51.4 %collective-permute-start.55 = (bf16[2,192,768]{2,1,0:T(8,128)(2,1)S(1)}, bf16[2,192,768]{2,1,0:T(8,128)(2,1)S(1)}, u32[]{:S(2)}, u32[]{:S(2)}) collective-permute-start(bf16[2,192,768]{2,1,0:T(8,128)(2,1)S(1)} %tie.16), channel_id=1, source_target_pairs={{0,16},{4,12},{8,24},{12,4},{16,0},{20,28},{24,8},{28,20},{1,17},{... | collective-permute-start | bytes 1769480 | tf_op jit(solution)/shard_map/ppermute | solution.py:973
  320.2 49.5 %collective-permute-start.56 = (bf16[2,192,768]{2,1,0:T(8,128)(2,1)S(1)}, bf16[2,192,768]{2,1,0:T(8,128)(2,1)S(1)}, u32[]{:S(2)}, u32[]{:S(2)}) collective-permute-start(bf16[2,192,768]{2,1,0:T(8,128)(2,1)S(1)} %get-tuple-element.209), channel_id=1, source_target_pairs={{0,16},{4,12},{8,24},{12,4},{16,0},{20,28},{24,8},{28,20},{1,17},{... | collective-permute-start | bytes 1769480 | tf_op jit(solution)/shard_map/ppermute | solution.py:973
  320.3 25.0 %collective-permute-start.46 = (bf16[128,768]{1,0:T(8,128)(2,1)S(1)}, bf16[128,768]{1,0:T(8,128)(2,1)S(1)}, u32[]{:S(2)}, u32[]{:S(2)}) collective-permute-start(bf16[128,768]{1,0:T(8,128)(2,1)S(1)} %copy-done.69), channel_id=1, source_target_pairs={{0,8},{4,12},{8,0},{12,4},{16,24},{20,28},{24,16},{28,20},{1,9},{5... | collective-permute-start | bytes 589832 | tf_op jit(solution)/shard_map/ppermute | solution.py:969
  330.0 20.6 %collective-permute-start.47 = (bf16[128,768]{1,0:T(8,128)(2,1)S(1)}, bf16[128,768]{1,0:T(8,128)(2,1)S(1)}, u32[]{:S(2)}, u32[]{:S(2)}) collective-permute-start(bf16[128,768]{1,0:T(8,128)(2,1)S(1)} %get-tuple-element.200), channel_id=1, source_target_pairs={{0,16},{4,20},{8,24},{12,28},{16,0},{20,4},{24,8},{28,12},{1,17},{... | collective-permute-start | bytes 589832 | tf_op jit(solution)/shard_map/ppermute | solution.py:969
  345.3 21.1 %collective-permute-start.58 = (bf16[2,2,192,192]{3,2,1,0:T(8,128)(2,1)S(1)}, bf16[2,2,192,192]{3,2,1,0:T(8,128)(2,1)S(1)}, u32[]{:S(2)}, u32[]{:S(2)}) collective-permute-start(bf16[2,2,192,192]{3,2,1,0:T(8,128)(2,1)S(1)} %get-tuple-element.211), channel_id=1, source_target_pairs={{0,1},{1,0},{2,3},{3,2},{4,5},{5,4},{6,7},{7,6},{8,9},{9,8},{10,11... | collective-permute-start | bytes 884744 | tf_op jit(solution)/shard_map/ppermute | solution.py:976
  368.1 21.1 %collective-permute-start.60 = (bf16[2,192,768]{2,1,0:T(8,128)(2,1)S(1)}, bf16[2,192,768]{2,1,0:T(8,128)(2,1)S(1)}, u32[]{:S(2)}, u32[]{:S(2)}) collective-permute-start(bf16[2,192,768]{2,1,0:T(8,128)(2,1)S(1)} %get-tuple-element.216), channel_id=1, source_target_pairs={{0,16},{4,12},{8,24},{12,4},{16,0},{20,28},{24,8},{28,20},{1,17},{... | collective-permute-start | bytes 1769480 | tf_op jit(solution)/shard_map/ppermute | solution.py:973
  370.5 21.5 %collective-permute-start.59 = (bf16[2,192,768]{2,1,0:T(8,128)(2,1)S(1)}, bf16[2,192,768]{2,1,0:T(8,128)(2,1)S(1)}, u32[]{:S(2)}, u32[]{:S(2)}) collective-permute-start(bf16[2,192,768]{2,1,0:T(8,128)(2,1)S(1)} %get-tuple-element.215), channel_id=1, source_target_pairs={{0,1},{1,0},{2,3},{3,2},{4,5},{5,4},{6,7},{7,6},{8,9},{9,8},{10,11... | collective-permute-start | bytes 1769480 | tf_op jit(solution)/shard_map/ppermute | solution.py:976
  390.2 28.5 %collective-permute-start.63 = (bf16[2,2,192,192]{3,2,1,0:T(8,128)(2,1)S(1)}, bf16[2,2,192,192]{3,2,1,0:T(8,128)(2,1)S(1)}, u32[]{:S(2)}, u32[]{:S(2)}) collective-permute-start(bf16[2,2,192,192]{3,2,1,0:T(8,128)(2,1)S(1)} %get-tuple-element.222), channel_id=1, source_target_pairs={{0,1},{1,0},{2,3},{3,2},{4,5},{5,4},{6,7},{7,6},{8,9},{9,8},{10,11... | collective-permute-start | bytes 884744 | tf_op jit(solution)/shard_map/ppermute | solution.py:976
  392.7 29.9 %collective-permute-start.62 = (bf16[192,768]{1,0:T(8,128)(2,1)S(1)}, bf16[192,768]{1,0:T(8,128)(2,1)S(1)}, u32[]{:S(2)}, u32[]{:S(2)}) collective-permute-start(bf16[192,768]{1,0:T(8,128)(2,1)S(1)} %get-tuple-element.221), channel_id=1, source_target_pairs={{0,2},{1,3},{2,0},{3,1},{4,6},{5,7},{6,4},{7,5},{8,10},{9,11},{10,... | collective-permute-start | bytes 884744 | tf_op jit(solution)/shard_map/ppermute | solution.py:976
  394.3 22.3 %collective-permute-start.52 = (bf16[128,768]{1,0:T(8,128)(2,1)S(1)}, bf16[128,768]{1,0:T(8,128)(2,1)S(1)}, u32[]{:S(2)}, u32[]{:S(2)}) collective-permute-start(bf16[128,768]{1,0:T(8,128)(2,1)S(1)} %memory_total.1.refs_3_.refs_1_), channel_id=1, source_target_pairs={{0,1},{1,0},{2,3},{3,2},{4,5},{5,4},{6,7},{7,6},{8,9},{9,8},{10,11... | collective-permute-start | bytes 589832 | tf_op jit(solution)/shard_map/ppermute | solution.py:976
  396.3 20.9 %collective-permute-start.64 = (f32[2,96,192]{2,1,0:T(8,128)S(1)}, f32[2,96,192]{2,1,0:T(8,128)S(1)}, u32[]{:S(2)}, u32[]{:S(2)}) collective-permute-start(f32[2,96,192]{2,1,0:T(8,128)S(1)} %get-tuple-element.223), channel_id=1, source_target_pairs={{0,4},{4,0},{8,12},{12,8},{16,20},{20,16},{24,28},{28,24},{1,5},{5... | collective-permute-start | bytes 442376 | tf_op jit(solution)/shard_map/ppermute | solution.py:969
  396.4 26.9 %collective-permute-start.53 = (bf16[128,768]{1,0:T(8,128)(2,1)S(1)}, bf16[128,768]{1,0:T(8,128)(2,1)S(1)}, u32[]{:S(2)}, u32[]{:S(2)}) collective-permute-start(bf16[128,768]{1,0:T(8,128)(2,1)S(1)} %memory_total.1.refs_3_.refs_1_), channel_id=1, source_target_pairs={{0,2},{1,3},{2,0},{3,1},{4,6},{5,7},{6,4},{7,5},{8,10},{9,11},{10,... | collective-permute-start | bytes 589832 | tf_op jit(solution)/shard_map/ppermute | solution.py:976
  423.2 25.4 %collective-permute-start.67 = (f32[96,768]{1,0:T(8,128)S(1)}, f32[96,768]{1,0:T(8,128)S(1)}, u32[]{:S(2)}, u32[]{:S(2)}) collective-permute-start(f32[96,768]{1,0:T(8,128)S(1)} %get-tuple-element.230), channel_id=1, source_target_pairs={{0,4},{4,0},{8,12},{12,8},{16,20},{20,16},{24,28},{28,24},{1,5},{5... | collective-permute-start | bytes 884744 | tf_op jit(solution)/shard_map/ppermute | solution.py:969
  (129 other events, 1176.8 us)
Sparse Core Ops, SparseCore 0:
  42.9 91.1 all-gather.6
  193.2 74.8 all-gather.8
  299.0 65.3 all-gather.10

commit v4 on v3

--- a/solution.py
+++ b/solution.py
@@ -142,11 +142,11 @@
         copy.wait()
 
 
-def vectors_kernel(info, mem_vectors, out_vectors, attn_vectors, hid_vec, out):
+def vectors_kernel(info, mem_vectors, out_vectors, hid_vec, out):
     out[...] = jnp.zeros(out.shape, F32)
     out[0:1] = out_vectors[0:1]
     out[1:3] = mem_vectors[0:2]
-    out[3:5] = attn_vectors[0:2]
+    out[3:5] = out_vectors[3:5]
     out[5:7] = out_vectors[1:3]
     for plane in range(hid_vec.shape[0]):
         out[7 + plane : 8 + plane] = hid_vec[plane]
@@ -176,12 +176,14 @@
     out[...] = total.astype(BF)
 
 
-def pick_kernel(info, first, second, third, fourth, out):
+def pick_kernel(info, first, second, third, fourth, out, sem):
     for at, ref in enumerate((first, second, third, fourth)):
 
         @pl.when(info[SLOT] == (info[UNIT] ^ at))
         def _(ref=ref):
-            out[...] = ref[...]
+            copy = pltpu.make_async_copy(ref, out, sem)
+            copy.start()
+            copy.wait()
 
 
 def tie(value, *after):
@@ -469,6 +471,7 @@
 
 GELU_A = math.sqrt(2.0 / math.pi)
 GELU_B = 0.044715
+CHUNK = 256
 
 
 def start_ffn(info, pieces, held, sems):
@@ -494,14 +497,14 @@
             ).wait()
 
 
-def ffn_forward_kernel(info, normed_in, cot, mem_result, *refs):
+def ffn_kernel(info, normed_in, inv_in, cot, mem_result, *refs):
     rows, refs = [r[...][None] for r in refs[:5]], refs[5:]
     attn_gain, attn_bias, out_gain, out_bias, ffn_bias = rows
     pieces, outs = refs[:2], refs[2:]
-    out, attn_low, gelu_out, slope, grad_sum, vectors = outs[:6]
-    held, bias, total, sems, bias_sem = outs[6:]
-    planes = held.shape[1]
-    bias_at = pl.ds(held.shape[2], 16)
+    out, attn_low, ffn_grad, mix_grad, mix_sum, vectors, hid_vec, gelu_out, hid_out = outs[:9]
+    held, bias, total, gelu_low, slope, sems, bias_sem, out_sems = outs[9:]
+    planes, width = held.shape[1], held.shape[2]
+    bias_at = pl.ds(width, 16)
     bias_copies = [
         pltpu.make_async_copy(pieces[0].at[plane, bias_at], bias.at[plane], bias_sem.at[plane])
         for plane in range(planes)
@@ -514,63 +517,55 @@
     total[...] = attn + ffn_bias
     for copy in bias_copies:
         copy.wait()
-
-    def forward(plane, carry):
+    out_copies = []
+    for plane in range(planes):
         wait_ffn(pieces, held, sems, plane)
         parts = bias[plane].astype(F32)
-        hidden = dot(attn_low[...], held[0, plane])
-        hidden = hidden + (parts[0:1] + parts[1:2] + parts[2:3])
-        square = hidden * hidden
-        curve = jnp.tanh(GELU_A * hidden * (1.0 + GELU_B * square))
-        half = 0.5 + 0.5 * curve
-        gelu_out[plane] = (hidden * half).astype(BF)
-        slope[plane] = (
-            half
-            + 0.5 * hidden * (1.0 - curve * curve) * (GELU_A + 3.0 * GELU_A * GELU_B * square)
-        ).astype(BF)
-        total[...] += dot(gelu_out[plane], held[1, plane])
-        return carry
-
-    lax.fori_loop(0, planes, forward, 0)
+        shift = parts[0:1] + parts[1:2] + parts[2:3]
+        for start in range(0, held.shape[3], CHUNK):
+            cols = slice(start, start + CHUNK)
+            hidden = dot(attn_low[...], held[0, plane, :, cols]) + shift[:, cols]
+            square = hidden * hidden
+            half = 1.0 / (1.0 + jnp.exp(hidden * (-2.0 * GELU_A - 2.0 * GELU_A * GELU_B * square)))
+            gelu = hidden * half
+            gelu_low[plane, :, cols] = gelu.astype(BF)
+            inner = 2.0 * GELU_A + 6.0 * GELU_A * GELU_B * square
+            slope[plane, :, cols] = (half + gelu * (1.0 - half) * inner).astype(BF)
+        total[...] += dot(gelu_low[plane], held[1, plane])
+        copy = pltpu.make_async_copy(gelu_low.at[plane], gelu_out.at[plane], out_sems.at[plane, 0])
+        copy.start()
+        out_copies.append(copy)
     out_normed, out_inv = norm_stats(total[...])
-    rows = normed_in.shape[0]
-    out[:rows] = (out_normed * out_gain + out_bias).astype(BF)
-    out[rows:] = mem_result[...]
+    count = normed_in.shape[0]
+    out[:count] = (out_normed * out_gain + out_bias).astype(BF)
+    out[count:] = mem_result[...]
     upstream = cot[...].astype(F32)
     grad = norm_pull(upstream, out_normed, out_inv, out_gain)
+    ffn_grad[...] = grad.astype(BF)
     vectors[0:1] = jnp.sum(grad.astype(BF).astype(F32), axis=0, keepdims=True)
     vectors[1:2] = jnp.sum(upstream * out_normed, axis=0, keepdims=True)
     vectors[2:3] = jnp.sum(upstream, axis=0, keepdims=True)
-    grad_sum[...] = grad
-
-
-def ffn_backward_kernel(info, grad_sum, normed_in, inv_in, slope, attn_gain, *refs):
-    pieces, outs = refs[:2], refs[2:]
-    hid_grad, ffn_grad, mix_grad, mix_sum, vectors, hid_vec = outs[:6]
-    held, total, sems = outs[6:]
-    planes = held.shape[1]
-    start_ffn(info, pieces, held, sems)
-    grad = grad_sum[...]
-    ffn_grad[...] = grad.astype(BF)
     total[...] = grad
-
-    def backward(plane, carry):
-        wait_ffn(pieces, held, sems, plane)
-        pulled = dot_nt(ffn_grad[...], held[1, plane]) * slope[plane].astype(F32)
-        low = pulled.astype(BF)
-        hid_grad[plane] = low
-        hid_vec[plane] = jnp.sum(low.astype(F32), axis=0, keepdims=True)
-        total[...] += dot_nt(low, held[0, plane])
-        return carry
-
-    lax.fori_loop(0, planes, backward, 0)
+    for plane in range(planes):
+        for start in range(0, held.shape[3], CHUNK):
+            cols = slice(start, start + CHUNK)
+            pulled = dot_nt(ffn_grad[...], held[1, plane, cols]) * slope[plane, :, cols].astype(F32)
+            low = pulled.astype(BF)
+            slope[plane, :, cols] = low
+            hid_vec[plane, :, cols] = jnp.sum(low.astype(F32), axis=0, keepdims=True)
+        total[...] += dot_nt(slope[plane], held[0, plane])
+        copy = pltpu.make_async_copy(slope.at[plane], hid_out.at[plane], out_sems.at[plane, 1])
+        copy.start()
+        out_copies.append(copy)
     upstream = total[...]
     normed = normed_in[...]
-    vectors[0:1] = jnp.sum(upstream * normed, axis=0, keepdims=True)
-    vectors[1:2] = jnp.sum(upstream, axis=0, keepdims=True)
-    grad = norm_pull(upstream, normed, inv_in[...], attn_gain[...][None])
+    vectors[3:4] = jnp.sum(upstream * normed, axis=0, keepdims=True)
+    vectors[4:5] = jnp.sum(upstream, axis=0, keepdims=True)
+    grad = norm_pull(upstream, normed, inv_in[...], attn_gain)
     mix_sum[...] = grad
     mix_grad[...] = grad.astype(BF)
+    for copy in out_copies:
+        copy.wait()
 
 
 def unpack_backward_kernel(info, q_in, k_in, v_in, ctx, lse, mix_grad, mix_sum, *refs):
@@ -688,55 +683,64 @@
     attn_low, hid_grad, gelu_out, ffn_grad = operands
     planes, rows, cols = hid_grad.shape
     width = attn_low.shape[1]
-    quarter = width // 4
-
-    def kernel(info, which, attn_ref, hid_ref, gelu_ref, grad_ref, *refs):
+    quarter, half = width // 4, planes // 2
+
+    def kernel(which, info, attn_ref, hid_ref, gelu_ref, grad_ref, *refs):
         plane = pl.program_id(0)
-        refs = refs[:1] * (added is not None) + refs[(added is not None) + len(after) :]
+        refs = refs[len(after) :] if added is None else refs[:2] + refs[2 + len(after) :]
 
         def put(value):
-            if added is None:
-                refs[0][0] = value.astype(BF)
-            else:
-                recv, held = refs[0], refs[5]
-                held[...] = (value + recv[0].astype(F32)).astype(BF)
-                for side, (keep, send) in enumerate((refs[1:3], refs[3:5])):
-
-                    @pl.when(plane // (planes // 2) == side)
-                    def _(keep=keep, send=send):
+            for side in range(2):
+
+                @pl.when(plane // half == side)
+                def _(side=side):
+                    if added is None:
+                        refs[side][0] = value.astype(BF)
+                    else:
+                        recv, held = refs[side], refs[6]
+                        held[...] = (value + recv[0].astype(F32)).astype(BF)
+                        keep, send = refs[2 + 2 * side : 4 + 2 * side]
                         split_pairs(info, held, keep, send, quarter)
 
         @pl.when(which[0] == 0)
         def _():
-            put(dot_tn(attn_ref[...], hid_ref[plane]))
+            put(dot_tn(attn_ref[...], hid_ref[0]))
 
         @pl.when(which[0] == 1)
         def _():
-            put(dot_tn(gelu_ref[plane], grad_ref[...]))
+            put(dot_tn(gelu_ref[0], grad_ref[...]))
 
     vm, sm = pl.BlockSpec(memory_space=pltpu.VMEM), pl.BlockSpec(memory_space=pltpu.SMEM)
-    block = pl.BlockSpec((1, width, cols), lambda i: (i, 0, 0))
-    half = planes // 2
+    blocks = [
+        pl.BlockSpec((1, width, cols), lambda i, w: (jnp.minimum(i, half - 1), 0, 0)),
+        pl.BlockSpec((1, width, cols), lambda i, w: (jnp.maximum(i - half, 0), 0, 0)),
+    ]
     pairs = [
-        pl.BlockSpec((2, 1, quarter, cols), lambda i: (0, jnp.minimum(i, half - 1), 0, 0)),
-        pl.BlockSpec((2, 1, quarter, cols), lambda i: (0, jnp.maximum(i - half, 0), 0, 0)),
+        pl.BlockSpec((2, 1, quarter, cols), lambda i, w: (0, jnp.minimum(i, half - 1), 0, 0)),
+        pl.BlockSpec((2, 1, quarter, cols), lambda i, w: (0, jnp.maximum(i - half, 0), 0, 0)),
     ]
     pair_shape = jax.ShapeDtypeStruct((2, half, quarter, cols), BF)
-    args, specs = [info, role, attn_low, hid_grad, gelu_out, ffn_grad], [sm, sm] + [vm] * 4
+    hid_block = pl.BlockSpec((1, rows, cols), lambda i, w: (i * (1 - w[0]), 0, 0))
+    gelu_block = pl.BlockSpec((1, rows, cols), lambda i, w: (i * w[0], 0, 0))
+    args = [role, info, attn_low, hid_grad, gelu_out, ffn_grad]
+    specs = [sm, vm, hid_block, gelu_block, vm]
     if added is not None:
-        args.append(added)
-        specs.append(block)
+        args += added
+        specs += blocks
     return pl.pallas_call(
         kernel,
-        grid=(planes,),
         out_shape=(
-            jax.ShapeDtypeStruct((planes, width, cols), BF)
+            [jax.ShapeDtypeStruct((half, width, cols), BF)] * 2
             if added is None
             else [pair_shape] * 4
         ),
-        in_specs=specs + [pl.BlockSpec(memory_space=pl.ANY)] * len(after),
-        out_specs=block if added is None else [pairs[0], pairs[0], pairs[1], pairs[1]],
-        scratch_shapes=[] if added is None else [pltpu.VMEM((width, cols), BF)],
+        grid_spec=pltpu.PrefetchScalarGridSpec(
+            num_scalar_prefetch=1,
+            grid=(planes,),
+            in_specs=specs + [pl.BlockSpec(memory_space=pl.ANY)] * len(after),
+            out_specs=blocks if added is None else [pairs[0], pairs[0], pairs[1], pairs[1]],
+            scratch_shapes=[] if added is None else [pltpu.VMEM((width, cols), BF)],
+        ),
         compiler_params=pltpu.CompilerParams(vmem_limit_bytes=60 * MIB),
         cost_estimate=SMALL,
         name="ffn_weight_grad",
@@ -1067,7 +1071,9 @@
             return [value] + [swap(value, j * unit) for j in range(1, SLOTS)]
 
         def fetch_finish(parts, also=()):
-            return run(pick_kernel, "pick_slot", parts, [(parts[0].shape, BF)], also=also)[0]
+            shapes = [(parts[0].shape, BF)]
+            sem = [pltpu.SemaphoreType.DMA]
+            return run(pick_kernel, "pick_slot", parts, shapes, anys=SLOTS, scratch=sem, also=also)[0]
 
         def sum_rows(values):
             total = values[0].astype(F32)
@@ -1157,9 +1163,9 @@
         )
         mix_parts = fetch_start(mix_low)
         mix_picked = fetch_finish(mix_parts, w_un)
-        ffn_rows = tie(ffn_rows, mix_picked)
+        mix_slot = gather_unit(mix_picked)
+        ffn_rows = tie(ffn_rows, mix_slot)
         ffn_parts = [ffn_rows, swap(ffn_rows, 1)]
-        mix_slot = gather_unit(mix_picked)
         k_un, v_un, q_un, tok_ctx, tok_lse, attn_normed, attn_inv = run(
             unpack_forward_kernel,
             "unpack_forward",
@@ -1171,34 +1177,41 @@
         )
         by_plane = (axis_head, block_len, hidden_width)
         held_ffn = pltpu.VMEM((2, axis_head, width, hidden_width), BF)
-        out_result, attn_low, gelu_out, slope, grad_sum, out_vectors = run(
-            ffn_forward_kernel,
-            "ffn_forward",
-            [attn_normed, cot_tok, mem_result]
+        plane_sems = pltpu.SemaphoreType.DMA((axis_head,))
+        (
+            out_result,
+            attn_low,
+            ffn_grad,
+            mix_grad,
+            mix_sum,
+            out_vectors,
+            hid_vec,
+            gelu_out,
+            hid_grad,
+        ) = run(
+            ffn_kernel,
+            "ffn",
+            [attn_normed, attn_inv, cot_tok, mem_result]
             + [attn_gain, attn_bias, out_gain, out_bias, ffn_out_bias]
             + ffn_parts,
-            [((block_len + row_count, width), BF)]
-            + [tok_low, (by_plane, BF), (by_plane, BF), tok_f32, ((8, width), F32)],
+            [((block_len + row_count, width), BF), tok_low, tok_low, tok_low, tok_f32]
+            + [((8, width), F32), ((axis_head, 1, hidden_width), F32)]
+            + [(by_plane, BF), (by_plane, BF)],
             anys=2,
+            out_any=2,
             scratch=[
                 held_ffn,
                 pltpu.VMEM((axis_head, 16, hidden_width), BF),
                 pltpu.VMEM((block_len, width), F32),
+                pltpu.VMEM(by_plane, BF),
+                pltpu.VMEM(by_plane, BF),
                 ffn_sems,
-                pltpu.SemaphoreType.DMA((axis_head,)),
+                plane_sems,
+                pltpu.SemaphoreType.DMA((axis_head, 2)),
             ],
         )
         out_rows = lax.all_gather(out_result, "head", axis=0)
         out_tokens, out_memory = out_rows[:, :block_len], out_rows[:, block_len:]
-        hid_grad, ffn_grad, mix_grad, mix_sum, attn_vectors, hid_vec = run(
-            ffn_backward_kernel,
-            "ffn_backward",
-            [grad_sum, attn_normed, attn_inv, slope, attn_gain] + ffn_parts,
-            [(by_plane, BF), tok_low, tok_low, tok_f32, ((8, width), F32)]
-            + [((axis_head, 1, hidden_width), F32)],
-            anys=2,
-            scratch=[held_ffn, pltpu.VMEM((block_len, width), F32), ffn_sems],
-        )
 
         role_info, other_info = role[None], 1 - role[None]
         ffn_operands = (attn_low, hid_grad, gelu_out, ffn_grad)
@@ -1206,13 +1219,10 @@
         def vectors_step(value, other):
             return run(total_kernel, "vectors", [value, other], [(value.shape, F32)])[0]
 
-        if fast:
-            ffn_sent = run_grid(ffn_weight_grad, other_info, ffn_operands, None)
-            ffn_got = swap(ffn_sent, 1)
         small = run(
             vectors_kernel,
             "vectors",
-            [mem_vectors, out_vectors, attn_vectors, hid_vec],
+            [mem_vectors, out_vectors, hid_vec],
             [((16, width), F32)],
         )[0]
         small_got = swap(small, 1)
@@ -1227,12 +1237,16 @@
         un_operands = (mix_slot, uk_part, uv_part, tok, uq_grad, tok_ctx, mix_grad)
         got = swap(send, unit // 2)
         small = vectors_step(small, small_got)
+        small_got = swap(small, 2)
+        if fast:
+            ffn_sent = run_grid(ffn_weight_grad, other_info, ffn_operands, None)
+            ffn_got = [swap(sent, 1) for sent in ffn_sent]
         parts = to_slots(keep, got, sum_kernel, [], flat, sum_rows, jnp.zeros((), BF))
-        small_got = swap(small, 2)
         if fast:
             ffn_low, low_sent, ffn_high, high_sent = run_grid(
                 ffn_weight_grad, role_info, ffn_operands, ffn_got
             )
+        small = vectors_step(small, small_got)
         mem_mix_grad, packed = run(
             memory_back_kernel,
             "memory_rows_backward",
@@ -1242,21 +1256,12 @@
             scratch=[held_out, out_sems],
         )
         back_parts = fetch_start(packed)
-        small = vectors_step(small, small_got)
-        step = 4
-        while step < axis_seq:
-            small_got = swap(small, step)
-            if fast:
-                un_sent = run_grid(attention_weight_grad, other_info, un_operands, axis_head, None)
-                un_kept, un_sent = run_grid(
-                    attention_weight_grad, role_info, un_operands, axis_head, swap(un_sent, 1)
-                )
-            small = vectors_step(small, small_got)
-            step *= 2
-        back_picked = fetch_finish(back_parts)
         if fast:
-            un_got = cross(tie(un_sent, back_picked), 0)
+            un_sent = run_grid(attention_weight_grad, other_info, un_operands, axis_head, None)
+        back_picked = fetch_finish(back_parts, [out_rows])
+        if fast:
             low_got = cross(tie(low_sent, back_picked), 0)
+            un_got = swap(tie(un_sent, back_picked), 1)
         back = gather_unit(back_picked)
         pq_part, pk_grad, pv_grad, grad_tokens, keep, send = run(
             pack_backward_kernel,
@@ -1265,19 +1270,21 @@
             [slot_low, tok_low, tok_low, tok_low, half_low, half_low],
             anys=8,
             scratch=[held_pair, pair_sems],
-            also=[out_rows],
         )
         grad_tokens = lax.all_gather(grad_tokens, "head", axis=0)
         pack_operands = (tok, pk_grad, pv_grad, mem_slot, pq_part, pack_ctx, mem_mix_grad)
         got = swap(send, unit // 2)
         if fast:
-            un_kept, un_sent = run_grid(add_pairs, un_kept, un_got)
-            un_got = cross(un_sent, 1)
             ffn_low, low_sent = run_grid(add_pairs, ffn_low, low_got)
             high_got = cross(tie(high_sent, ffn_low), 0)
-        if fast:
+            un_kept, un_sent = run_grid(
+                attention_weight_grad, role_info, un_operands, axis_head, un_got
+            )
             pack_sent = run_grid(attention_weight_grad, other_info, pack_operands, axis_head, None)
-            pack_got = swap(pack_sent, 1)
+        step = 4
+        while step < axis_seq:
+            small = vectors_step(small, swap(small, step))
+            step *= 2
         parts = to_slots(keep, got, sum_kernel, [], flat, sum_rows, jnp.zeros((), BF))
 
         rows = (quarter, hidden_width)
@@ -1360,33 +1367,38 @@
             return first + [by_rows(product(left, right))]
 
         if fast:
+            ffn_high, high_sent = run_grid(add_pairs, ffn_high, high_got)
+            low_got, high_got = cross(tie(low_sent, ffn_high), 1), cross(high_sent, 1)
+            pack_got = swap(tie(pack_sent, ffn_high), 1)
             pack_kept, pack_sent = run_grid(
                 attention_weight_grad, role_info, pack_operands, axis_head, pack_got
             )
-            pack_got = cross(pack_sent, 0)
-            ffn_high, high_sent = run_grid(add_pairs, ffn_high, high_got)
-            low_got, high_got = cross(tie(low_sent, ffn_high), 1), cross(high_sent, 1)
-            un_blocks = attention_blocks(un_kept, un_got)
         total = run(memory_total_kernel, "memory_total", [grad_memsum] + parts, [row_low])[0]
         grad_planes = from_planes(total)
-        small_planes = direct_planes(tie(small, total))
         if fast:
-            un_blocks = middle(*un_blocks, pair_rows)
+            un_got = cross(tie(un_sent, total), 0)
+            blocks = ffn_blocks([ffn_low, ffn_high], [low_got, high_got])
+            pack_got = cross(tie(pack_sent, blocks[0]), 0)
+            un_kept, un_sent = run_grid(add_pairs, un_kept, un_got)
+            un_got = cross(un_sent, 1)
             pack_kept, pack_sent = run_grid(add_pairs, pack_kept, pack_got)
             pack_got = cross(pack_sent, 1)
-            blocks = ffn_blocks([ffn_low, ffn_high], [low_got, high_got])
-            un_halves = attention_total(*un_blocks)
+            blocks = middle(*blocks, rows)
+            un_blocks = attention_blocks(un_kept, un_got)
             pack_blocks = attention_blocks(pack_kept, pack_got)
-            blocks = middle(*blocks, rows)
-            un_grads = attention_final(un_halves)
-            pack_blocks = middle(*pack_blocks, pair_rows)
             halves = ffn_total(*blocks)
             grad_memory = all_planes(grad_planes)
+            un_blocks = middle(*un_blocks, pair_rows)
+            pack_blocks = middle(*pack_blocks, pair_rows)
+            small_planes = direct_planes(tie(small, pack_blocks[0]))
+            fi_grad, fo_grad = ffn_final(halves)
+            un_halves = attention_total(*un_blocks)
             pack_halves = attention_total(*pack_blocks)
-            fi_grad, fo_grad = ffn_final(halves)
+            un_grads = attention_final(un_halves)
             pack_grads = attention_final(pack_halves)
         else:
             grad_memory = all_planes(grad_planes)
+            small_planes = direct_planes(small)
             un_grads = attention_simple(un_operands)
             pack_grads = attention_simple(pack_operands)
             fi_grad = jnp.stack([product(attn_low, hid_grad[p]) for p in range(axis_head)])

time: 475 us -> 466 us (0.981)
  waiting for transfers between devices: 173 us -> 157 us
  starting transfers between devices: 72.5 us -> 78.3 us
    ppermute x42 -> x43, waiting for transfers between devices: 63.2 us -> 48.5 us  [swap(): return lax.ppermute(value, 'seq', [(i, i ^ step) for i in range(axis_seq)])]
    ppermute x14, waiting for transfers between devices: 36.8 us -> 48 us  [cross(): lax.ppermute(value, 'seq', [(i, i ^ steps[i % 2]) for i in range(axis_seq)])]
    ppermute x15, waiting for transfers between devices: 66.7 us -> 56.6 us  [over(): lax.ppermute(value, 'head', [(i, i ^ step) for i in range(axis_head)])]
    ppermute x42 -> x43, starting transfers between devices: 30.5 us -> 33.7 us  [swap(): return lax.ppermute(value, 'seq', [(i, i ^ step) for i in range(axis_seq)])]
    unnamed x159 -> x169, local copies, waits for them, and re-layouts: 29.8 us -> 32.3 us
    pallas_call x39 -> x38, Pallas kernels: 140 us -> 139 us  [call(): pl.pallas_call(body, out_shape=[jax.ShapeDtypeStruct(s, d) for s, d in ou...]
  transfers between devices with their start and end apart: 74 -> 75, of which waited for: 30 -> 28; matrix products, arithmetic and copies ran while one was open for 2% -> 2% of each run, Pallas kernels for 25% -> 29%
where the time goes in v4:
time: 466 us; the launch traced here: 458 us
  Pallas kernels  165 us (35%)
  waiting for transfers between devices  157 us (34%)
  starting transfers between devices  78.3 us (17%)
  local copies, waits for them, and re-layouts  38.8 us (8%)
  between operations  15.2 us (3%)
    pallas_call x38, Pallas kernels, call(): pl.pallas_call(body, out_shape=[jax.ShapeDtypeStruct(s, d) for s, d in ou...  139 us
    ppermute x15, waiting for transfers between devices, over(): lax.ppermute(value, 'head', [(i, i ^ step) for i in range(axis_head)])  56.6 us
    ppermute x43, waiting for transfers between devices, swap(): return lax.ppermute(value, 'seq', [(i, i ^ step) for i in range(axis_seq)])  48.5 us
    ppermute x14, waiting for transfers between devices, cross(): lax.ppermute(value, 'seq', [(i, i ^ steps[i % 2]) for i in range(axis_seq)])  48 us
    ppermute x43, starting transfers between devices, swap(): return lax.ppermute(value, 'seq', [(i, i ^ step) for i in range(axis_seq)])  33.7 us
    unnamed x169, local copies, waits for them, and re-layouts  32.3 us
    ppermute x15, starting transfers between devices, over(): lax.ppermute(value, 'head', [(i, i ^ step) for i in range(axis_head)])  22.6 us
    ppermute x14, starting transfers between devices, cross(): lax.ppermute(value, 'seq', [(i, i ^ steps[i % 2]) for i in range(axis_seq)])  21.4 us
  transfers between devices with their start and end apart: 75, of which 28 were waited for; matrix products, arithmetic and copies ran while one was open for 2% of the time, Pallas kernels for 29%

profile of v4, /device:TPU:0, one launch (start us, length us, event | category | flops | bytes accessed | tf_op | source)
XLA Modules:
  0.0 457.5 jit_solution(7218538140383135805)
XLA Ops:
  16.1 10.8 %collective-permute-done.4.refs_2_ = bf16[4,48,768]{2,1,0:T(8,128)(2,1)S(1)} collective-permute-done((bf16[4,48,768]{2,1,0:T(8,128)(2,1)}, bf16[4,48,768]{2,1,0:T(8,128)(2,1)S(1)}, u32[]{:S(2)}, u32[]{:S(2)}) %collective-permute-start.4) | collective-permute-done | bytes 294944 | tf_op jit(solution)/shard_map/ppermute | solution.py:980
  46.9 13.0 %collective-permute-done.7.refs_4_.refs_11_.refs_10_.refs_8_ = bf16[2,4,48,768]{3,2,1,0:T(8,128)(2,1)S(1)} collective-permute-done((bf16[2,4,48,768]{3,2,1,0:T(8,128)(2,1)S(1)}, bf16[2,4,48,768]{3,2,1,0:T(8,128)(2,1)S(1)}, u32[]{:S(2)}, u32[]{:S(2)}) %collective-permute-start.7) | collective-permute-done | bytes 589856 | tf_op jit(solution)/shard_map/ppermute | solution.py:977
  62.0 7.8 %collective-permute-done.9.refs_6_.refs_1_.refs_13_.refs_12_.refs_10_ = bf16[2,4,48,768]{3,2,1,0:T(8,128)(2,1)S(1)} collective-permute-done((bf16[2,4,48,768]{3,2,1,0:T(8,128)(2,1)S(1)}, bf16[2,4,48,768]{3,2,1,0:T(8,128)(2,1)S(1)}, u32[]{:S(2)}, u32[]{:S(2)}) %collective-permute-start.9) | collective-permute-done | bytes 589856 | tf_op jit(solution)/shard_map/ppermute | solution.py:977
  73.3 12.4 %pack_forward.1 = (bf16[512,768]{1,0:T(8,128)(2,1)}, bf16[512,768]{1,0:T(8,128)(2,1)}, bf16[256,768]{1,0:T(8,128)(2,1)}, bf16[128,896]{1,0:T(8,128)(2,1)}, bf16[128,896]{1,0:T(8,128)(2,1)}) custom-call(s32[16]{0:T(128)} %get-tuple-element.130.refs_0_.info, bf16[512,768]{1,0:T(8,128)(2,1)} %get-tuple-element.131.refs_1_.refs_5_.refs_2_, ...), custom_call_target="tpu_custom_call" | custom-call | flops 1 | bytes 1 | tf_op jit(solution)/shard_map/pack_forward/pallas_call | solution.py:50
  94.6 5.8 %collective-permute-done.16.refs_2_ = bf16[128,896]{1,0:T(8,128)(2,1)S(1)} collective-permute-done((bf16[128,896]{1,0:T(8,128)(2,1)S(1)}, bf16[128,896]{1,0:T(8,128)(2,1)S(1)}, u32[]{:S(2)}, u32[]{:S(2)}) %collective-permute-start.16) | collective-permute-done | bytes 229408 | tf_op jit(solution)/shard_map/ppermute | solution.py:973
  103.8 5.9 %collective-permute-done.18.refs_4_ = bf16[128,896]{1,0:T(8,128)(2,1)S(1)} collective-permute-done((bf16[128,896]{1,0:T(8,128)(2,1)S(1)}, bf16[128,896]{1,0:T(8,128)(2,1)S(1)}, u32[]{:S(2)}, u32[]{:S(2)}) %collective-permute-start.18) | collective-permute-done | bytes 229408 | tf_op jit(solution)/shard_map/ppermute | solution.py:973
  110.4 4.4 memory_rows.1
  118.4 4.5 collective-permute-done.21.refs_2_
  135.1 12.4 %unpack_forward.1 = (bf16[256,768]{1,0:T(8,128)(2,1)}, bf16[256,768]{1,0:T(8,128)(2,1)}, bf16[512,768]{1,0:T(8,128)(2,1)}, bf16[512,768]{1,0:T(8,128)(2,1)}, f32...) custom-call(s32[16]{0:T(128)} %get-tuple-element.130.refs_0_.info, ...), custom_call_target="tpu_custom_call" | custom-call | flops 1 | bytes 1 | tf_op jit(solution)/shard_map/unpack_forward/pallas_call | solution.py:50
  147.5 23.4 %ffn.1 = (bf16[640,768]{1,0:T(8,128)(2,1)}, bf16[512,768]{1,0:T(8,128)(2,1)}, bf16[512,768]{1,0:T(8,128)(2,1)}, bf16[512,768]{1,0:T(8,128)(2,1)}, f32[512,768]{1...) custom-call(s32[16]{0:T(128)} %get-tuple-element.130.refs_0_.info, ...), custom_call_target="tpu_custom_call" | custom-call | flops 1 | bytes 1 | tf_op jit(solution)/shard_map/ffn/pallas_call | solution.py:50
  174.8 15.6 %unpack_backward.1 = (bf16[512,768]{1,0:T(8,128)(2,1)}, bf16[256,768]{1,0:T(8,128)(2,1)}, bf16[256,768]{1,0:T(8,128)(2,1)}, bf16[128,768]{1,0:T(8,128)(2,1)}, bf...) custom-call(s32[16]{0:T(128)} %get-tuple-element.130.refs_0_.info, bf16[512,768]{1,0:T(8,128)(2,1)} %get-tuple-element.152.refs_1_, ...), custom_call_target="tpu_custom_call" | custom-call | flops 1 | bytes 1 | tf_op jit(solution)/shard_map/unpack_backward/pallas_call | solution.py:50
  193.6 7.9 %ffn_weight_grad.2 = (bf16[2,768,768]{2,1,0:T(8,128)(2,1)}, bf16[2,768,768]{2,1,0:T(8,128)(2,1)}) custom-call(s32[1]{0:T(128)S(6)} %sub.7.which.refs_1_, s32[16]{0:T(128)} %get-tuple-element.130.refs_0_.info, bf16[512,768]{1,0:T(8,128)(2,1)} %get-tuple-element.163.attn_ref, bf16[4,512,768]{2,1,0:T(8,128)(2,1)} %get-tuple-element.164.hid_ref, ...), custom_call_target="tpu_custom_call" | custom-call | flops 1 | bytes 1 | tf_op jit(solution)/shard_map/ffn_weight_grad/pallas_call | solution.py:730
  216.5 9.8 %ffn_weight_grad.3 = (bf16[2,2,192,768]{3,2,1,0:T(8,128)(2,1)}, bf16[2,2,192,768]{3,2,1,0:T(8,128)(2,1)}, bf16[2,2,192,768]{3,2,1,0:T(8,128)(2,1)}, bf16[2,2,192,768]{3,2,1,0:T(8,128)(2,1)}) custom-call(s32[1]{0:T(128)} %bitcast.10.which.refs_1_, s32[16]{0:T(128)} %get-tuple-element.130.refs_0_.info, bf16[512,768]{1,0:T(8,128)(2,1)} %get-tuple-element.163.attn_ref, ...), custom_call_target="tpu_custom_call" | custom-call | flops 1 | bytes 1 | tf_op jit(solution)/shard_map/ffn_weight_grad/pallas_call | solution.py:730
  237.4 5.2 %attention_weight_grad.4.refs_5_.refs_0_ = bf16[2,768,768]{2,1,0:T(8,128)(2,1)} custom-call(s32[16]{0:T(128)} %get-tuple-element.130.refs_0_.info, s32[1]{0:T(128)S(6)} %sub.7.which.refs_1_, bf16[256,768]{1,0:T(8,128)(2,1)} %copy-done.5, bf16[256,768]{1,0:T(8,128)(2,1)} %get-tuple-element.179.refs_3_, bf16[256,768]{1,0:T(8,128)(2,1)} %get-tuple-element.180.refs_4_, ...), custom_call_target="tpu_custom_call" | custom-call | flops 1 | bytes 1 | tf_op jit(solution)/shard_map/attention_weight_grad/pallas_call | solution.py:50
  256.8 12.9 %pack_backward.1 = (bf16[256,768]{1,0:T(8,128)(2,1)}, bf16[512,768]{1,0:T(8,128)(2,1)}, bf16[512,768]{1,0:T(8,128)(2,1)}, bf16[512,768]{1,0:T(8,128)(2,1)}, bf16...) custom-call(s32[16]{0:T(128)} %get-tuple-element.130.refs_0_.info, bf16[256,896]{1,0:T(8,128)(2,1)} %pad_maximum_fusion.refs_1_, ...), custom_call_target="tpu_custom_call" | custom-call | flops 1 | bytes 1 | tf_op jit(solution)/shard_map/pack_backward/pallas_call | solution.py:50
  276.8 5.4 %attention_weight_grad.5 = (bf16[2,2,192,768]{3,2,1,0:T(8,128)(2,1)}, bf16[2,2,192,768]{3,2,1,0:T(8,128)(2,1)}) custom-call(s32[16]{0:T(128)} %get-tuple-element.130.refs_0_.info, s32[1]{0:T(128)} %bitcast.10.which.refs_1_, bf16[256,768]{1,0:T(8,128)(2,1)} %copy-done.5, bf16[256,768]{1,0:T(8,128)(2,1)} %get-tuple-element.179.refs_3_, ...), custom_call_target="tpu_custom_call" | custom-call | flops 1 | bytes 1 | tf_op jit(solution)/shard_map/attention_weight_grad/pallas_call | solution.py:50
  303.2 6.1 %attention_weight_grad.7 = (bf16[2,2,192,768]{3,2,1,0:T(8,128)(2,1)}, bf16[2,2,192,768]{3,2,1,0:T(8,128)(2,1)}) custom-call(s32[16]{0:T(128)} %get-tuple-element.130.refs_0_.info, s32[1]{0:T(128)} %bitcast.10.which.refs_1_, bf16[512,768]{1,0:T(8,128)(2,1)} %get-tuple-element.131.refs_1_.refs_5_.refs_2_, bf16[512,768]{1,0:T(8,128)(2,1)} %get-tuple-element.188.refs_3_, ...), custom_call_target="tpu_custom_call" | custom-call | flops 1 | bytes 1 | tf_op jit(solution)/shard_map/attention_weight_grad/pallas_call | solution.py:50
  309.3 10.7 %collective-permute-done.47.refs_4_ = bf16[128,768]{1,0:T(8,128)(2,1)} collective-permute-done((bf16[128,768]{1,0:T(8,128)(2,1)}, bf16[128,768]{1,0:T(8,128)(2,1)}, u32[]{:S(2)}, u32[]{:S(2)}) %collective-permute-start.47) | collective-permute-done | bytes 196640 | tf_op jit(solution)/shard_map/ppermute | solution.py:973
  326.1 12.6 %collective-permute-done.58.got_ref = bf16[2,2,192,768]{3,2,1,0:T(8,128)(2,1)S(1)} collective-permute-done((bf16[2,2,192,768]{3,2,1,0:T(8,128)(2,1)S(1)}, bf16[2,2,192,768]{3,2,1,0:T(8,128)(2,1)S(1)}, u32[]{:S(2)}, u32[]{:S(2)}) %collective-permute-start.58) | collective-permute-done | bytes 1179680 | tf_op jit(solution)/shard_map/ppermute | solution.py:977
  343.2 14.4 %collective-permute-done.57.got_ref = bf16[2,2,192,768]{3,2,1,0:T(8,128)(2,1)S(1)} collective-permute-done((bf16[2,2,192,768]{3,2,1,0:T(8,128)(2,1)S(1)}, bf16[2,2,192,768]{3,2,1,0:T(8,128)(2,1)S(1)}, u32[]{:S(2)}, u32[]{:S(2)}) %collective-permute-start.57) | collective-permute-done | bytes 1179680 | tf_op jit(solution)/shard_map/ppermute | solution.py:977
  362.2 6.3 %collective-permute-done.56.refs_2_ = bf16[2,192,768]{2,1,0:T(8,128)(2,1)S(1)} collective-permute-done((bf16[2,192,768]{2,1,0:T(8,128)(2,1)S(1)}, bf16[2,192,768]{2,1,0:T(8,128)(2,1)S(1)}, u32[]{:S(2)}, u32[]{:S(2)}) %collective-permute-start.56) | collective-permute-done | bytes 589856 | tf_op jit(solution)/shard_map/ppermute | solution.py:980
  376.3 4.5 collective-permute-done.51.refs_2_
  385.9 15.9 %collective-permute-done.52.refs_3_ = bf16[128,768]{1,0:T(8,128)(2,1)S(1)} collective-permute-done((bf16[128,768]{1,0:T(8,128)(2,1)S(1)}, bf16[128,768]{1,0:T(8,128)(2,1)S(1)}, u32[]{:S(2)}, u32[]{:S(2)}) %collective-permute-start.52) | collective-permute-done | bytes 196640 | tf_op jit(solution)/shard_map/ppermute | solution.py:980
  414.6 12.0 %collective-permute-done.65.refs_2_ = bf16[2,192,192]{2,1,0:T(8,128)(2,1)S(1)} collective-permute-done((bf16[2,192,192]{2,1,0:T(8,128)(2,1)S(1)}, bf16[2,192,192]{2,1,0:T(8,128)(2,1)S(1)}, u32[]{:S(2)}, u32[]{:S(2)}) %collective-permute-start.65) | collective-permute-done | bytes 147488 | tf_op jit(solution)/shard_map/ppermute | solution.py:980
  (368 shorter events, 202.5 us)
Async XLA Ops:
  7.2 127.9 %all-gather.7.cloned.1.call-start = ((), (), s32[]{:S(2)}) async-start(), calls=%async_computation | async-start | bytes 6021120 | tf_op jit(solution)/shard_map/all_gather | solution.py:1140
  13.5 28.7 %collective-permute-start.5 = (bf16[4,48,768]{2,1,0:T(8,128)(2,1)}, bf16[4,48,768]{2,1,0:T(8,128)(2,1)S(1)}, u32[]{:S(2)}, u32[]{:S(2)}) collective-permute-start(bf16[4,48,768]{2,1,0:T(8,128)(2,1)} %get-tuple-element.134.refs_1_), channel_id=1, source_target_pairs={{0,2},{1,3},{2,0},{3,1},{4,6},{5,7},{6,4},{7,5},{8,10},{9,11},{10,... | collective-permute-start | bytes 884744 | tf_op jit(solution)/shard_map/ppermute | solution.py:980
  43.9 203.1 %all-gather.9.cloned.1.call-start = ((), (), s32[]{:S(2)}) async-start(), calls=%async_computation.1 | async-start | bytes 4915200 | tf_op jit(solution)/shard_map/all_gather | solution.py:1213
  93.5 22.4 %collective-permute-start.24 = (bf16[2,4,48,768]{3,2,1,0:T(8,128)(2,1)S(1)}, bf16[2,4,48,768]{3,2,1,0:T(8,128)(2,1)S(1)}, u32[]{:S(2)}, u32[]{:S(2)}) collective-permute-start(bf16[2,4,48,768]{3,2,1,0:T(8,128)(2,1)S(1)} %tie.12.refs_6_.refs_3_.refs_8_), channel_id=1, source_target_pairs={{0,4},{4,0},{8,12},{12,8},{16,20},{20,16},{24,28},{28,24},{1,5},{5... | collective-permute-start | bytes 1769480 | tf_op jit(solution)/shard_map/ppermute | solution.py:973
  93.5 23.4 %collective-permute-start.25 = (bf16[2,4,48,768]{3,2,1,0:T(8,128)(2,1)S(1)}, bf16[2,4,48,768]{3,2,1,0:T(8,128)(2,1)S(1)}, u32[]{:S(2)}, u32[]{:S(2)}) collective-permute-start(bf16[2,4,48,768]{3,2,1,0:T(8,128)(2,1)S(1)} %tie.13.refs_7_.refs_4_.refs_9_), channel_id=1, source_target_pairs={{0,4},{4,0},{8,12},{12,8},{16,20},{20,16},{24,28},{28,24},{1,5},{5... | collective-permute-start | bytes 1769480 | tf_op jit(solution)/shard_map/ppermute | solution.py:973
  100.4 18.0 %collective-permute-start.26 = (bf16[2,4,48,768]{3,2,1,0:T(8,128)(2,1)S(1)}, bf16[2,4,48,768]{3,2,1,0:T(8,128)(2,1)}, u32[]{:S(2)}, u32[]{:S(2)}) collective-permute-start(bf16[2,4,48,768]{3,2,1,0:T(8,128)(2,1)S(1)} %collective-permute-done.15.refs_5_.refs_8_.refs_10_), channel_id=1, source_target_pairs={{0,4},{4,0},{8,12},{12,8},{16,20},{20,16},{24,28},{28,24},{1,5},{5... | collective-permute-start | bytes 1769480 | tf_op jit(solution)/shard_map/ppermute | solution.py:973
  100.8 25.0 %collective-permute-start.27 = (bf16[2,4,48,768]{3,2,1,0:T(8,128)(2,1)S(1)}, bf16[2,4,48,768]{3,2,1,0:T(8,128)(2,1)}, u32[]{:S(2)}, u32[]{:S(2)}) collective-permute-start(bf16[2,4,48,768]{3,2,1,0:T(8,128)(2,1)S(1)} %collective-permute-done.20.refs_19_.refs_9_.refs_6_.refs_11_), channel_id=1, source_target_pairs={{0,4},{4,0},{8,12},{12,8},{16,20},{20,16},{24,28},{28,24},{1,5},{5... | collective-permute-start | bytes 1769480 | tf_op jit(solution)/shard_map/ppermute | solution.py:973
  171.0 270.0 %all-gather.11.cloned.1.call-start = ((), (), s32[]{:S(2)}) async-start(), calls=%async_computation.2 | async-start | bytes 3932160 | tf_op jit(solution)/shard_map/all_gather | solution.py:1274
  210.0 18.7 %collective-permute-start.32 = (bf16[128,768]{1,0:T(8,128)(2,1)S(1)}, bf16[128,768]{1,0:T(8,128)(2,1)S(1)}, u32[]{:S(2)}, u32[]{:S(2)}) collective-permute-start(bf16[128,768]{1,0:T(8,128)(2,1)S(1)} %get-tuple-element.170), channel_id=1, source_target_pairs={{0,8},{4,12},{8,0},{12,4},{16,24},{20,28},{24,16},{28,20},{1,9},{5... | collective-permute-start | bytes 589832 | tf_op jit(solution)/shard_map/ppermute | solution.py:973
  251.1 25.7 %collective-permute-start.44 = (bf16[2,768,768]{2,1,0:T(8,128)(2,1)S(1)}, bf16[2,768,768]{2,1,0:T(8,128)(2,1)}, u32[]{:S(2)}, u32[]{:S(2)}) collective-permute-start(bf16[2,768,768]{2,1,0:T(8,128)(2,1)S(1)} %tie.16), channel_id=1, source_target_pairs={{0,4},{4,0},{8,12},{12,8},{16,20},{20,16},{24,28},{28,24},{1,5},{5... | collective-permute-start | bytes 7077896 | tf_op jit(solution)/shard_map/ppermute | solution.py:973
  252.5 17.2 %collective-permute-start.45 = (bf16[2,2,192,768]{3,2,1,0:T(8,128)(2,1)S(1)}, bf16[2,2,192,768]{3,2,1,0:T(8,128)(2,1)}, u32[]{:S(2)}, u32[]{:S(2)}) collective-permute-start(bf16[2,2,192,768]{3,2,1,0:T(8,128)(2,1)S(1)} %tie.17), channel_id=1, source_target_pairs={{0,8},{4,20},{8,0},{12,28},{16,24},{20,4},{24,16},{28,12},{1,9},{5... | collective-permute-start | bytes 3538952 | tf_op jit(solution)/shard_map/ppermute | solution.py:977
  297.1 26.4 %collective-permute-start.54 = (bf16[2,192,768]{2,1,0:T(8,128)(2,1)}, bf16[2,192,768]{2,1,0:T(8,128)(2,1)S(1)}, u32[]{:S(2)}, u32[]{:S(2)}) collective-permute-start(bf16[2,192,768]{2,1,0:T(8,128)(2,1)} %tie.20), channel_id=1, source_target_pairs={{0,16},{4,12},{8,24},{12,4},{16,0},{20,28},{24,8},{28,20},{1,17},{... | collective-permute-start | bytes 1769480 | tf_op jit(solution)/shard_map/ppermute | solution.py:977
  298.5 24.9 %collective-permute-start.55 = (bf16[2,192,768]{2,1,0:T(8,128)(2,1)}, bf16[2,192,768]{2,1,0:T(8,128)(2,1)}, u32[]{:S(2)}, u32[]{:S(2)}) collective-permute-start(bf16[2,192,768]{2,1,0:T(8,128)(2,1)} %get-tuple-element.203), channel_id=1, source_target_pairs={{0,16},{4,12},{8,24},{12,4},{16,0},{20,28},{24,8},{28,20},{1,17},{... | collective-permute-start | bytes 1769480 | tf_op jit(solution)/shard_map/ppermute | solution.py:977
  300.2 19.8 %collective-permute-start.47 = (bf16[128,768]{1,0:T(8,128)(2,1)}, bf16[128,768]{1,0:T(8,128)(2,1)}, u32[]{:S(2)}, u32[]{:S(2)}) collective-permute-start(bf16[128,768]{1,0:T(8,128)(2,1)} %get-tuple-element.196), channel_id=1, source_target_pairs={{0,16},{4,20},{8,24},{12,28},{16,0},{20,4},{24,8},{28,12},{1,17},{... | collective-permute-start | bytes 589832 | tf_op jit(solution)/shard_map/ppermute | solution.py:973
  301.6 18.4 %collective-permute-start.48 = (bf16[128,768]{1,0:T(8,128)(2,1)S(1)}, bf16[128,768]{1,0:T(8,128)(2,1)S(1)}, u32[]{:S(2)}, u32[]{:S(2)}) collective-permute-start(bf16[128,768]{1,0:T(8,128)(2,1)S(1)} %get-tuple-element.197), channel_id=1, source_target_pairs={{0,24},{4,28},{8,16},{12,20},{16,8},{20,12},{24,0},{28,4},{1,25},{... | collective-permute-start | bytes 589832 | tf_op jit(solution)/shard_map/ppermute | solution.py:973
  324.9 32.7 %collective-permute-start.57 = (bf16[2,2,192,768]{3,2,1,0:T(8,128)(2,1)S(1)}, bf16[2,2,192,768]{3,2,1,0:T(8,128)(2,1)S(1)}, u32[]{:S(2)}, u32[]{:S(2)}) collective-permute-start(bf16[2,2,192,768]{3,2,1,0:T(8,128)(2,1)S(1)} %tie.21), channel_id=1, source_target_pairs={{0,8},{4,20},{8,0},{12,28},{16,24},{20,4},{24,16},{28,12},{1,9},{5... | collective-permute-start | bytes 3538952 | tf_op jit(solution)/shard_map/ppermute | solution.py:977
  326.1 42.4 %collective-permute-start.56 = (bf16[2,192,768]{2,1,0:T(8,128)(2,1)S(1)}, bf16[2,192,768]{2,1,0:T(8,128)(2,1)S(1)}, u32[]{:S(2)}, u32[]{:S(2)}) collective-permute-start(bf16[2,192,768]{2,1,0:T(8,128)(2,1)S(1)} %get-tuple-element.205), channel_id=1, source_target_pairs={{0,1},{1,0},{2,3},{3,2},{4,5},{5,4},{6,7},{7,6},{8,9},{9,8},{10,11... | collective-permute-start | bytes 1769480 | tf_op jit(solution)/shard_map/ppermute | solution.py:980
  339.6 31.2 %collective-permute-start.61 = (bf16[2,192,768]{2,1,0:T(8,128)(2,1)S(1)}, bf16[2,192,768]{2,1,0:T(8,128)(2,1)S(1)}, u32[]{:S(2)}, u32[]{:S(2)}) collective-permute-start(bf16[2,192,768]{2,1,0:T(8,128)(2,1)S(1)} %get-tuple-element.213), channel_id=1, source_target_pairs={{0,16},{4,12},{8,24},{12,4},{16,0},{20,28},{24,8},{28,20},{1,17},{... | collective-permute-start | bytes 1769480 | tf_op jit(solution)/shard_map/ppermute | solution.py:977
  371.8 35.5 %collective-permute-start.63 = (bf16[2,2,192,192]{3,2,1,0:T(8,128)(2,1)S(1)}, bf16[2,2,192,192]{3,2,1,0:T(8,128)(2,1)S(1)}, u32[]{:S(2)}, u32[]{:S(2)}) collective-permute-start(bf16[2,2,192,192]{3,2,1,0:T(8,128)(2,1)S(1)} %get-tuple-element.218), channel_id=1, source_target_pairs={{0,1},{1,0},{2,3},{3,2},{4,5},{5,4},{6,7},{7,6},{8,9},{9,8},{10,11... | collective-permute-start | bytes 884744 | tf_op jit(solution)/shard_map/ppermute | solution.py:980
  373.4 39.1 %collective-permute-start.62 = (bf16[2,2,192,192]{3,2,1,0:T(8,128)(2,1)S(1)}, bf16[2,2,192,192]{3,2,1,0:T(8,128)(2,1)S(1)}, u32[]{:S(2)}, u32[]{:S(2)}) collective-permute-start(bf16[2,2,192,192]{3,2,1,0:T(8,128)(2,1)S(1)} %get-tuple-element.217), channel_id=1, source_target_pairs={{0,1},{1,0},{2,3},{3,2},{4,5},{5,4},{6,7},{7,6},{8,9},{9,8},{10,11... | collective-permute-start | bytes 884744 | tf_op jit(solution)/shard_map/ppermute | solution.py:980
  375.0 26.9 %collective-permute-start.52 = (bf16[128,768]{1,0:T(8,128)(2,1)S(1)}, bf16[128,768]{1,0:T(8,128)(2,1)S(1)}, u32[]{:S(2)}, u32[]{:S(2)}) collective-permute-start(bf16[128,768]{1,0:T(8,128)(2,1)S(1)} %memory_total.1.refs_5_.refs_1_), channel_id=1, source_target_pairs={{0,2},{1,3},{2,0},{3,1},{4,6},{5,7},{6,4},{7,5},{8,10},{9,11},{10,... | collective-permute-start | bytes 589832 | tf_op jit(solution)/shard_map/ppermute | solution.py:980
  380.8 25.0 %collective-permute-start.53 = (bf16[128,768]{1,0:T(8,128)(2,1)S(1)}, bf16[128,768]{1,0:T(8,128)(2,1)S(1)}, u32[]{:S(2)}, u32[]{:S(2)}) collective-permute-start(bf16[128,768]{1,0:T(8,128)(2,1)S(1)} %collective-permute-done.51.refs_2_), channel_id=1, source_target_pairs={{0,2},{1,3},{2,0},{3,1},{4,6},{5,7},{6,4},{7,5},{8,10},{9,11},{10,... | collective-permute-start | bytes 589832 | tf_op jit(solution)/shard_map/ppermute | solution.py:980
  385.9 27.4 %collective-permute-start.66 = (f32[96,768]{1,0:T(8,128)S(1)}, f32[96,768]{1,0:T(8,128)S(1)}, u32[]{:S(2)}, u32[]{:S(2)}) collective-permute-start(f32[96,768]{1,0:T(8,128)S(1)} %get-tuple-element.223), channel_id=1, source_target_pairs={{0,4},{4,0},{8,12},{12,8},{16,20},{20,16},{24,28},{28,24},{1,5},{5... | collective-permute-start | bytes 884744 | tf_op jit(solution)/shard_map/ppermute | solution.py:973
  409.0 17.6 %collective-permute-start.65 = (bf16[2,192,192]{2,1,0:T(8,128)(2,1)S(1)}, bf16[2,192,192]{2,1,0:T(8,128)(2,1)S(1)}, u32[]{:S(2)}, u32[]{:S(2)}) collective-permute-start(bf16[2,192,192]{2,1,0:T(8,128)(2,1)S(1)} %get-tuple-element.222), channel_id=1, source_target_pairs={{0,2},{1,3},{2,0},{3,1},{4,6},{5,7},{6,4},{7,5},{8,10},{9,11},{10,... | collective-permute-start | bytes 442376 | tf_op jit(solution)/shard_map/ppermute | solution.py:980
  (135 other events, 1119.6 us)
Sparse Core Ops, SparseCore 0:
  44.0 91.0 all-gather.6
  171.1 75.1 all-gather.8
  297.2 71.4 all-gather.10

commit v5 on v4

--- a/solution.py
+++ b/solution.py
@@ -1373,7 +1373,10 @@
             pack_kept, pack_sent = run_grid(
                 attention_weight_grad, role_info, pack_operands, axis_head, pack_got
             )
-        total = run(memory_total_kernel, "memory_total", [grad_memsum] + parts, [row_low])[0]
+        done = [out_tokens, out_memory]
+        total = run(
+            memory_total_kernel, "memory_total", [grad_memsum] + parts, [row_low], also=done
+        )[0]
         grad_planes = from_planes(total)
         if fast:
             un_got = cross(tie(un_sent, total), 0)
@@ -1390,15 +1393,29 @@
             grad_memory = all_planes(grad_planes)
             un_blocks = middle(*un_blocks, pair_rows)
             pack_blocks = middle(*pack_blocks, pair_rows)
-            small_planes = direct_planes(tie(small, pack_blocks[0]))
+            small_planes = direct_planes(tie(small, grad_memory))
             fi_grad, fo_grad = ffn_final(halves)
             un_halves = attention_total(*un_blocks)
+            small = run(
+                plane_vectors_kernel,
+                "vectors",
+                small_planes,
+                [(small.shape, F32)],
+                scratch=[pltpu.VMEM((axis_head,) + small.shape, F32)],
+            )[0]
             pack_halves = attention_total(*pack_blocks)
             un_grads = attention_final(un_halves)
             pack_grads = attention_final(pack_halves)
         else:
             grad_memory = all_planes(grad_planes)
             small_planes = direct_planes(small)
+            small = run(
+                plane_vectors_kernel,
+                "vectors",
+                small_planes,
+                [(small.shape, F32)],
+                scratch=[pltpu.VMEM((axis_head,) + small.shape, F32)],
+            )[0]
             un_grads = attention_simple(un_operands)
             pack_grads = attention_simple(pack_operands)
             fi_grad = jnp.stack([product(attn_low, hid_grad[p]) for p in range(axis_head)])
@@ -1406,13 +1423,6 @@
             fo_grad = jnp.stack([product(gelu_out[p], ffn_grad) for p in range(axis_head)])
             fo_grad = scatter(scatter(fo_grad, "seq", 1), "head", 0)[0].astype(F32)
 
-        small = run(
-            plane_vectors_kernel,
-            "vectors",
-            small_planes,
-            [(small.shape, F32)],
-            scratch=[pltpu.VMEM((axis_head,) + small.shape, F32)],
-        )[0]
         share = width // axis_seq
         vectors = lax.dynamic_slice_in_dim(small[:7], seq_index * share, share, 1)
         fib = mine(small[7 : 7 + axis_head].reshape(axis_head, -1))

time: 466 us -> 456 us (0.979)
  waiting for transfers between devices: 157 us -> 150 us
  starting transfers between devices: 78.3 us -> 72.6 us
    ppermute x15, waiting for transfers between devices: 56.6 us -> 51.4 us  [over(): lax.ppermute(value, 'head', [(i, i ^ step) for i in range(axis_head)])]
    unnamed x169 -> x173, local copies, waits for them, and re-layouts: 32.3 us -> 34.7 us
  transfers between devices with their start and end apart: 75 -> 75, of which waited for: 28 -> 28; matrix products, arithmetic and copies ran while one was open for 2% -> 2% of each run, Pallas kernels for 29% -> 30%
where the time goes in v5:
time: 456 us; the launch traced here: 448 us
  Pallas kernels  167 us (37%)
  waiting for transfers between devices  150 us (33%)
  starting transfers between devices  72.6 us (16%)
  local copies, waits for them, and re-layouts  40.4 us (9%)
  between operations  15.3 us (3%)
    pallas_call x38, Pallas kernels, call(): pl.pallas_call(body, out_shape=[jax.ShapeDtypeStruct(s, d) for s, d in ou...  141 us
    ppermute x15, waiting for transfers between devices, over(): lax.ppermute(value, 'head', [(i, i ^ step) for i in range(axis_head)])  51.4 us
    ppermute x14, waiting for transfers between devices, cross(): lax.ppermute(value, 'seq', [(i, i ^ steps[i % 2]) for i in range(axis_seq)])  48.7 us
    ppermute x43, waiting for transfers between devices, swap(): return lax.ppermute(value, 'seq', [(i, i ^ step) for i in range(axis_seq)])  46.1 us
    unnamed x173, local copies, waits for them, and re-layouts  34.7 us
    ppermute x43, starting transfers between devices, swap(): return lax.ppermute(value, 'seq', [(i, i ^ step) for i in range(axis_seq)])  33.2 us
    ppermute x15, starting transfers between devices, over(): lax.ppermute(value, 'head', [(i, i ^ step) for i in range(axis_head)])  20.5 us
    ppermute x14, starting transfers between devices, cross(): lax.ppermute(value, 'seq', [(i, i ^ steps[i % 2]) for i in range(axis_seq)])  18.4 us
  transfers between devices with their start and end apart: 75, of which 28 were waited for; matrix products, arithmetic and copies ran while one was open for 2% of the time, Pallas kernels for 30%

profile of v5, /device:TPU:0, one launch (start us, length us, event | category | flops | bytes accessed | tf_op | source)
XLA Modules:
  0.0 447.9 jit_solution(16304366458131338173)
XLA Ops:
  16.1 10.8 %collective-permute-done.4.refs_2_ = bf16[4,48,768]{2,1,0:T(8,128)(2,1)S(1)} collective-permute-done((bf16[4,48,768]{2,1,0:T(8,128)(2,1)}, bf16[4,48,768]{2,1,0:T(8,128)(2,1)S(1)}, u32[]{:S(2)}, u32[]{:S(2)}) %collective-permute-start.4) | collective-permute-done | bytes 294944 | tf_op jit(solution)/shard_map/ppermute | solution.py:980
  46.9 13.0 %collective-permute-done.7.refs_4_.refs_11_.refs_10_.refs_8_ = bf16[2,4,48,768]{3,2,1,0:T(8,128)(2,1)S(1)} collective-permute-done((bf16[2,4,48,768]{3,2,1,0:T(8,128)(2,1)S(1)}, bf16[2,4,48,768]{3,2,1,0:T(8,128)(2,1)S(1)}, u32[]{:S(2)}, u32[]{:S(2)}) %collective-permute-start.7) | collective-permute-done | bytes 589856 | tf_op jit(solution)/shard_map/ppermute | solution.py:977
  62.0 7.7 %collective-permute-done.9.refs_6_.refs_1_.refs_13_.refs_12_.refs_10_ = bf16[2,4,48,768]{3,2,1,0:T(8,128)(2,1)S(1)} collective-permute-done((bf16[2,4,48,768]{3,2,1,0:T(8,128)(2,1)S(1)}, bf16[2,4,48,768]{3,2,1,0:T(8,128)(2,1)S(1)}, u32[]{:S(2)}, u32[]{:S(2)}) %collective-permute-start.9) | collective-permute-done | bytes 589856 | tf_op jit(solution)/shard_map/ppermute | solution.py:977
  73.3 12.4 %pack_forward.1 = (bf16[512,768]{1,0:T(8,128)(2,1)}, bf16[512,768]{1,0:T(8,128)(2,1)}, bf16[256,768]{1,0:T(8,128)(2,1)}, bf16[128,896]{1,0:T(8,128)(2,1)}, bf16[128,896]{1,0:T(8,128)(2,1)}) custom-call(s32[16]{0:T(128)} %get-tuple-element.130.refs_0_.info, bf16[512,768]{1,0:T(8,128)(2,1)} %get-tuple-element.131.refs_1_.refs_5_.refs_2_, ...), custom_call_target="tpu_custom_call" | custom-call | flops 1 | bytes 1 | tf_op jit(solution)/shard_map/pack_forward/pallas_call | solution.py:50
  94.6 5.8 %collective-permute-done.16.refs_2_ = bf16[128,896]{1,0:T(8,128)(2,1)S(1)} collective-permute-done((bf16[128,896]{1,0:T(8,128)(2,1)S(1)}, bf16[128,896]{1,0:T(8,128)(2,1)S(1)}, u32[]{:S(2)}, u32[]{:S(2)}) %collective-permute-start.16) | collective-permute-done | bytes 229408 | tf_op jit(solution)/shard_map/ppermute | solution.py:973
  103.8 6.0 %collective-permute-done.18.refs_4_ = bf16[128,896]{1,0:T(8,128)(2,1)S(1)} collective-permute-done((bf16[128,896]{1,0:T(8,128)(2,1)S(1)}, bf16[128,896]{1,0:T(8,128)(2,1)S(1)}, u32[]{:S(2)}, u32[]{:S(2)}) %collective-permute-start.18) | collective-permute-done | bytes 229408 | tf_op jit(solution)/shard_map/ppermute | solution.py:973
  135.1 12.4 %unpack_forward.1 = (bf16[256,768]{1,0:T(8,128)(2,1)}, bf16[256,768]{1,0:T(8,128)(2,1)}, bf16[512,768]{1,0:T(8,128)(2,1)}, bf16[512,768]{1,0:T(8,128)(2,1)}, f32...) custom-call(s32[16]{0:T(128)} %get-tuple-element.130.refs_0_.info, ...), custom_call_target="tpu_custom_call" | custom-call | flops 1 | bytes 1 | tf_op jit(solution)/shard_map/unpack_forward/pallas_call | solution.py:50
  147.5 23.3 %ffn.1 = (bf16[640,768]{1,0:T(8,128)(2,1)}, bf16[512,768]{1,0:T(8,128)(2,1)}, bf16[512,768]{1,0:T(8,128)(2,1)}, bf16[512,768]{1,0:T(8,128)(2,1)}, f32[512,768]{1...) custom-call(s32[16]{0:T(128)} %get-tuple-element.130.refs_0_.info, ...), custom_call_target="tpu_custom_call" | custom-call | flops 1 | bytes 1 | tf_op jit(solution)/shard_map/ffn/pallas_call | solution.py:50
  174.7 15.6 %unpack_backward.1 = (bf16[512,768]{1,0:T(8,128)(2,1)}, bf16[256,768]{1,0:T(8,128)(2,1)}, bf16[256,768]{1,0:T(8,128)(2,1)}, bf16[128,768]{1,0:T(8,128)(2,1)}, bf...) custom-call(s32[16]{0:T(128)} %get-tuple-element.130.refs_0_.info, bf16[512,768]{1,0:T(8,128)(2,1)} %get-tuple-element.152.refs_1_, ...), custom_call_target="tpu_custom_call" | custom-call | flops 1 | bytes 1 | tf_op jit(solution)/shard_map/unpack_backward/pallas_call | solution.py:50
  193.5 7.9 %ffn_weight_grad.2 = (bf16[2,768,768]{2,1,0:T(8,128)(2,1)}, bf16[2,768,768]{2,1,0:T(8,128)(2,1)}) custom-call(s32[1]{0:T(128)S(6)} %sub.7.which.refs_1_, s32[16]{0:T(128)} %get-tuple-element.130.refs_0_.info, bf16[512,768]{1,0:T(8,128)(2,1)} %get-tuple-element.163.attn_ref, bf16[4,512,768]{2,1,0:T(8,128)(2,1)} %get-tuple-element.164.hid_ref, ...), custom_call_target="tpu_custom_call" | custom-call | flops 1 | bytes 1 | tf_op jit(solution)/shard_map/ffn_weight_grad/pallas_call | solution.py:730
  216.3 9.8 %ffn_weight_grad.3 = (bf16[2,2,192,768]{3,2,1,0:T(8,128)(2,1)}, bf16[2,2,192,768]{3,2,1,0:T(8,128)(2,1)}, bf16[2,2,192,768]{3,2,1,0:T(8,128)(2,1)}, bf16[2,2,192,768]{3,2,1,0:T(8,128)(2,1)}) custom-call(s32[1]{0:T(128)} %bitcast.10.which.refs_1_, s32[16]{0:T(128)} %get-tuple-element.130.refs_0_.info, bf16[512,768]{1,0:T(8,128)(2,1)} %get-tuple-element.163.attn_ref, ...), custom_call_target="tpu_custom_call" | custom-call | flops 1 | bytes 1 | tf_op jit(solution)/shard_map/ffn_weight_grad/pallas_call | solution.py:730
  237.3 5.3 %attention_weight_grad.4.refs_5_.refs_0_ = bf16[2,768,768]{2,1,0:T(8,128)(2,1)} custom-call(s32[16]{0:T(128)} %get-tuple-element.130.refs_0_.info, s32[1]{0:T(128)S(6)} %sub.7.which.refs_1_, bf16[256,768]{1,0:T(8,128)(2,1)} %copy-done.6, bf16[256,768]{1,0:T(8,128)(2,1)} %get-tuple-element.179.refs_3_, bf16[256,768]{1,0:T(8,128)(2,1)} %get-tuple-element.180.refs_4_, ...), custom_call_target="tpu_custom_call" | custom-call | flops 1 | bytes 1 | tf_op jit(solution)/shard_map/attention_weight_grad/pallas_call | solution.py:50
  242.6 4.7 %collective-permute-done.39.refs_3_ = bf16[128,896]{1,0:T(8,128)(2,1)S(1)} collective-permute-done((bf16[128,896]{1,0:T(8,128)(2,1)}, bf16[128,896]{1,0:T(8,128)(2,1)S(1)}, u32[]{:S(2)}, u32[]{:S(2)}) %collective-permute-start.39) | collective-permute-done | bytes 229408 | tf_op jit(solution)/shard_map/ppermute | solution.py:973
  257.2 13.0 %pack_backward.1 = (bf16[256,768]{1,0:T(8,128)(2,1)}, bf16[512,768]{1,0:T(8,128)(2,1)}, bf16[512,768]{1,0:T(8,128)(2,1)}, bf16[512,768]{1,0:T(8,128)(2,1)}, bf16...) custom-call(s32[16]{0:T(128)} %get-tuple-element.130.refs_0_.info, bf16[256,896]{1,0:T(8,128)(2,1)} %pad_maximum_fusion.refs_1_, ...), custom_call_target="tpu_custom_call" | custom-call | flops 1 | bytes 1 | tf_op jit(solution)/shard_map/pack_backward/pallas_call | solution.py:50
  276.0 5.4 %attention_weight_grad.5 = (bf16[2,2,192,768]{3,2,1,0:T(8,128)(2,1)}, bf16[2,2,192,768]{3,2,1,0:T(8,128)(2,1)}) custom-call(s32[16]{0:T(128)} %get-tuple-element.130.refs_0_.info, s32[1]{0:T(128)} %bitcast.10.which.refs_1_, bf16[256,768]{1,0:T(8,128)(2,1)} %copy-done.6, bf16[256,768]{1,0:T(8,128)(2,1)} %get-tuple-element.179.refs_3_, ...), custom_call_target="tpu_custom_call" | custom-call | flops 1 | bytes 1 | tf_op jit(solution)/shard_map/attention_weight_grad/pallas_call | solution.py:50
  295.1 4.7 %collective-permute-start.50 = (bf16[2,768,768]{2,1,0:T(8,128)(2,1)S(1)}, bf16[2,768,768]{2,1,0:T(8,128)(2,1)}, u32[]{:S(2)}, u32[]{:S(2)}) collective-permute-start(bf16[2,768,768]{2,1,0:T(8,128)(2,1)S(1)} %tie.19), channel_id=1, source_target_pairs={{0,4},{4,0},{8,12},{12,8},{16,20},{20,16},{24,28},{28,24},{1,5},{5... | collective-permute-start | bytes 7077896 | tf_op jit(solution)/shard_map/ppermute | solution.py:973
  310.7 5.8 %attention_weight_grad.7 = (bf16[2,2,192,768]{3,2,1,0:T(8,128)(2,1)}, bf16[2,2,192,768]{3,2,1,0:T(8,128)(2,1)}) custom-call(s32[16]{0:T(128)} %get-tuple-element.130.refs_0_.info, s32[1]{0:T(128)} %bitcast.10.which.refs_1_, bf16[512,768]{1,0:T(8,128)(2,1)} %get-tuple-element.131.refs_1_.refs_5_.refs_2_, bf16[512,768]{1,0:T(8,128)(2,1)} %get-tuple-element.188.refs_3_, ...), custom_call_target="tpu_custom_call" | custom-call | flops 1 | bytes 1 | tf_op jit(solution)/shard_map/attention_weight_grad/pallas_call | solution.py:50
  316.5 7.4 %collective-permute-done.47.refs_4_ = bf16[128,768]{1,0:T(8,128)(2,1)} collective-permute-done((bf16[128,768]{1,0:T(8,128)(2,1)}, bf16[128,768]{1,0:T(8,128)(2,1)}, u32[]{:S(2)}, u32[]{:S(2)}) %collective-permute-start.47) | collective-permute-done | bytes 196640 | tf_op jit(solution)/shard_map/ppermute | solution.py:973
  331.5 12.5 %collective-permute-done.58.got_ref = bf16[2,2,192,768]{3,2,1,0:T(8,128)(2,1)S(1)} collective-permute-done((bf16[2,2,192,768]{3,2,1,0:T(8,128)(2,1)S(1)}, bf16[2,2,192,768]{3,2,1,0:T(8,128)(2,1)S(1)}, u32[]{:S(2)}, u32[]{:S(2)}) %collective-permute-start.58) | collective-permute-done | bytes 1179680 | tf_op jit(solution)/shard_map/ppermute | solution.py:977
  347.6 15.5 %collective-permute-done.57.got_ref = bf16[2,2,192,768]{3,2,1,0:T(8,128)(2,1)S(1)} collective-permute-done((bf16[2,2,192,768]{3,2,1,0:T(8,128)(2,1)S(1)}, bf16[2,2,192,768]{3,2,1,0:T(8,128)(2,1)S(1)}, u32[]{:S(2)}, u32[]{:S(2)}) %collective-permute-start.57) | collective-permute-done | bytes 1179680 | tf_op jit(solution)/shard_map/ppermute | solution.py:977
  378.0 6.0 %collective-permute-done.51.refs_2_ = bf16[128,768]{1,0:T(8,128)(2,1)S(1)} collective-permute-done((bf16[128,768]{1,0:T(8,128)(2,1)S(1)}, bf16[128,768]{1,0:T(8,128)(2,1)S(1)}, u32[]{:S(2)}, u32[]{:S(2)}) %collective-permute-start.51) | collective-permute-done | bytes 196640 | tf_op jit(solution)/shard_map/ppermute | solution.py:980
  388.9 7.8 %collective-permute-done.52.refs_3_ = bf16[128,768]{1,0:T(8,128)(2,1)S(1)} collective-permute-done((bf16[128,768]{1,0:T(8,128)(2,1)S(1)}, bf16[128,768]{1,0:T(8,128)(2,1)S(1)}, u32[]{:S(2)}, u32[]{:S(2)}) %collective-permute-start.52) | collective-permute-done | bytes 196640 | tf_op jit(solution)/shard_map/ppermute | solution.py:980
  396.6 8.3 %collective-permute-done.53.refs_4_ = bf16[128,768]{1,0:T(8,128)(2,1)S(1)} collective-permute-done((bf16[128,768]{1,0:T(8,128)(2,1)S(1)}, bf16[128,768]{1,0:T(8,128)(2,1)S(1)}, u32[]{:S(2)}, u32[]{:S(2)}) %collective-permute-start.53) | collective-permute-done | bytes 196640 | tf_op jit(solution)/shard_map/ppermute | solution.py:980
  416.8 9.2 %collective-permute-done.68.refs_2_ = bf16[2,192,192]{2,1,0:T(8,128)(2,1)S(1)} collective-permute-done((bf16[2,192,192]{2,1,0:T(8,128)(2,1)S(1)}, bf16[2,192,192]{2,1,0:T(8,128)(2,1)S(1)}, u32[]{:S(2)}, u32[]{:S(2)}) %collective-permute-start.68) | collective-permute-done | bytes 147488 | tf_op jit(solution)/shard_map/ppermute | solution.py:980
  (372 shorter events, 202.3 us)
Async XLA Ops:
  7.2 127.9 %all-gather.7.cloned.1.call-start = ((), (), s32[]{:S(2)}) async-start(), calls=%async_computation | async-start | bytes 6021120 | tf_op jit(solution)/shard_map/all_gather | solution.py:1140
  13.5 28.6 %collective-permute-start.5 = (bf16[4,48,768]{2,1,0:T(8,128)(2,1)}, bf16[4,48,768]{2,1,0:T(8,128)(2,1)S(1)}, u32[]{:S(2)}, u32[]{:S(2)}) collective-permute-start(bf16[4,48,768]{2,1,0:T(8,128)(2,1)} %get-tuple-element.134.refs_1_), channel_id=1, source_target_pairs={{0,2},{1,3},{2,0},{3,1},{4,6},{5,7},{6,4},{7,5},{8,10},{9,11},{10,... | collective-permute-start | bytes 884744 | tf_op jit(solution)/shard_map/ppermute | solution.py:980
  43.8 203.5 %all-gather.9.cloned.1.call-start = ((), (), s32[]{:S(2)}) async-start(), calls=%async_computation.1 | async-start | bytes 4915200 | tf_op jit(solution)/shard_map/all_gather | solution.py:1213
  93.5 22.4 %collective-permute-start.24 = (bf16[2,4,48,768]{3,2,1,0:T(8,128)(2,1)S(1)}, bf16[2,4,48,768]{3,2,1,0:T(8,128)(2,1)S(1)}, u32[]{:S(2)}, u32[]{:S(2)}) collective-permute-start(bf16[2,4,48,768]{3,2,1,0:T(8,128)(2,1)S(1)} %tie.12.refs_6_.refs_3_.refs_8_), channel_id=1, source_target_pairs={{0,4},{4,0},{8,12},{12,8},{16,20},{20,16},{24,28},{28,24},{1,5},{5... | collective-permute-start | bytes 1769480 | tf_op jit(solution)/shard_map/ppermute | solution.py:973
  93.5 23.2 %collective-permute-start.25 = (bf16[2,4,48,768]{3,2,1,0:T(8,128)(2,1)S(1)}, bf16[2,4,48,768]{3,2,1,0:T(8,128)(2,1)}, u32[]{:S(2)}, u32[]{:S(2)}) collective-permute-start(bf16[2,4,48,768]{3,2,1,0:T(8,128)(2,1)S(1)} %tie.13.refs_7_.refs_4_.refs_9_), channel_id=1, source_target_pairs={{0,4},{4,0},{8,12},{12,8},{16,20},{20,16},{24,28},{28,24},{1,5},{5... | collective-permute-start | bytes 1769480 | tf_op jit(solution)/shard_map/ppermute | solution.py:973
  100.8 25.0 %collective-permute-start.27 = (bf16[2,4,48,768]{3,2,1,0:T(8,128)(2,1)S(1)}, bf16[2,4,48,768]{3,2,1,0:T(8,128)(2,1)}, u32[]{:S(2)}, u32[]{:S(2)}) collective-permute-start(bf16[2,4,48,768]{3,2,1,0:T(8,128)(2,1)S(1)} %collective-permute-done.20.refs_19_.refs_9_.refs_6_.refs_11_), channel_id=1, source_target_pairs={{0,4},{4,0},{8,12},{12,8},{16,20},{20,16},{24,28},{28,24},{1,5},{5... | collective-permute-start | bytes 1769480 | tf_op jit(solution)/shard_map/ppermute | solution.py:973
  170.9 244.5 %all-gather.11.cloned.1.call-start = ((), (), s32[]{:S(2)}) async-start(), calls=%async_computation.2 | async-start | bytes 3932160 | tf_op jit(solution)/shard_map/all_gather | solution.py:1274
  209.9 18.7 %collective-permute-start.32 = (bf16[128,768]{1,0:T(8,128)(2,1)S(1)}, bf16[128,768]{1,0:T(8,128)(2,1)S(1)}, u32[]{:S(2)}, u32[]{:S(2)}) collective-permute-start(bf16[128,768]{1,0:T(8,128)(2,1)S(1)} %get-tuple-element.170), channel_id=1, source_target_pairs={{0,8},{4,12},{8,0},{12,4},{16,24},{20,28},{24,16},{28,20},{1,9},{5... | collective-permute-start | bytes 589832 | tf_op jit(solution)/shard_map/ppermute | solution.py:973
  251.5 24.5 %collective-permute-start.44 = (bf16[2,768,768]{2,1,0:T(8,128)(2,1)S(1)}, bf16[2,768,768]{2,1,0:T(8,128)(2,1)}, u32[]{:S(2)}, u32[]{:S(2)}) collective-permute-start(bf16[2,768,768]{2,1,0:T(8,128)(2,1)S(1)} %tie.16), channel_id=1, source_target_pairs={{0,4},{4,0},{8,12},{12,8},{16,20},{20,16},{24,28},{28,24},{1,5},{5... | collective-permute-start | bytes 7077896 | tf_op jit(solution)/shard_map/ppermute | solution.py:973
  299.9 28.0 %collective-permute-start.54 = (bf16[2,192,768]{2,1,0:T(8,128)(2,1)}, bf16[2,192,768]{2,1,0:T(8,128)(2,1)}, u32[]{:S(2)}, u32[]{:S(2)}) collective-permute-start(bf16[2,192,768]{2,1,0:T(8,128)(2,1)} %tie.20), channel_id=1, source_target_pairs={{0,16},{4,12},{8,24},{12,4},{16,0},{20,28},{24,8},{28,20},{1,17},{... | collective-permute-start | bytes 1769480 | tf_op jit(solution)/shard_map/ppermute | solution.py:977
  301.5 26.4 %collective-permute-start.55 = (bf16[2,192,768]{2,1,0:T(8,128)(2,1)}, bf16[2,192,768]{2,1,0:T(8,128)(2,1)}, u32[]{:S(2)}, u32[]{:S(2)}) collective-permute-start(bf16[2,192,768]{2,1,0:T(8,128)(2,1)} %get-tuple-element.203), channel_id=1, source_target_pairs={{0,16},{4,12},{8,24},{12,4},{16,0},{20,28},{24,8},{28,20},{1,17},{... | collective-permute-start | bytes 1769480 | tf_op jit(solution)/shard_map/ppermute | solution.py:977
  303.1 20.8 %collective-permute-start.47 = (bf16[128,768]{1,0:T(8,128)(2,1)}, bf16[128,768]{1,0:T(8,128)(2,1)}, u32[]{:S(2)}, u32[]{:S(2)}) collective-permute-start(bf16[128,768]{1,0:T(8,128)(2,1)} %get-tuple-element.196), channel_id=1, source_target_pairs={{0,16},{4,20},{8,24},{12,28},{16,0},{20,4},{24,8},{28,12},{1,17},{... | collective-permute-start | bytes 589832 | tf_op jit(solution)/shard_map/ppermute | solution.py:973
  304.2 19.8 %collective-permute-start.48 = (bf16[128,768]{1,0:T(8,128)(2,1)}, bf16[128,768]{1,0:T(8,128)(2,1)}, u32[]{:S(2)}, u32[]{:S(2)}) collective-permute-start(bf16[128,768]{1,0:T(8,128)(2,1)} %get-tuple-element.197), channel_id=1, source_target_pairs={{0,24},{4,28},{8,16},{12,20},{16,8},{20,12},{24,0},{28,4},{1,25},{... | collective-permute-start | bytes 589832 | tf_op jit(solution)/shard_map/ppermute | solution.py:973
  330.5 32.5 %collective-permute-start.57 = (bf16[2,2,192,768]{3,2,1,0:T(8,128)(2,1)S(1)}, bf16[2,2,192,768]{3,2,1,0:T(8,128)(2,1)S(1)}, u32[]{:S(2)}, u32[]{:S(2)}) collective-permute-start(bf16[2,2,192,768]{3,2,1,0:T(8,128)(2,1)S(1)} %tie.21), channel_id=1, source_target_pairs={{0,8},{4,20},{8,0},{12,28},{16,24},{20,4},{24,16},{28,12},{1,9},{5... | collective-permute-start | bytes 3538952 | tf_op jit(solution)/shard_map/ppermute | solution.py:977
  331.5 39.7 %collective-permute-start.56 = (bf16[2,192,768]{2,1,0:T(8,128)(2,1)S(1)}, bf16[2,192,768]{2,1,0:T(8,128)(2,1)S(1)}, u32[]{:S(2)}, u32[]{:S(2)}) collective-permute-start(bf16[2,192,768]{2,1,0:T(8,128)(2,1)S(1)} %get-tuple-element.205), channel_id=1, source_target_pairs={{0,1},{1,0},{2,3},{3,2},{4,5},{5,4},{6,7},{7,6},{8,9},{9,8},{10,11... | collective-permute-start | bytes 1769480 | tf_op jit(solution)/shard_map/ppermute | solution.py:980
  345.1 29.7 %collective-permute-start.61 = (bf16[2,192,768]{2,1,0:T(8,128)(2,1)S(1)}, bf16[2,192,768]{2,1,0:T(8,128)(2,1)S(1)}, u32[]{:S(2)}, u32[]{:S(2)}) collective-permute-start(bf16[2,192,768]{2,1,0:T(8,128)(2,1)S(1)} %get-tuple-element.213), channel_id=1, source_target_pairs={{0,16},{4,12},{8,24},{12,4},{16,0},{20,28},{24,8},{28,20},{1,17},{... | collective-permute-start | bytes 1769480 | tf_op jit(solution)/shard_map/ppermute | solution.py:977
  364.0 22.8 %collective-permute-start.60 = (bf16[2,192,768]{2,1,0:T(8,128)(2,1)S(1)}, bf16[2,192,768]{2,1,0:T(8,128)(2,1)S(1)}, u32[]{:S(2)}, u32[]{:S(2)}) collective-permute-start(bf16[2,192,768]{2,1,0:T(8,128)(2,1)S(1)} %get-tuple-element.212), channel_id=1, source_target_pairs={{0,16},{4,12},{8,24},{12,4},{16,0},{20,28},{24,8},{28,20},{1,17},{... | collective-permute-start | bytes 1769480 | tf_op jit(solution)/shard_map/ppermute | solution.py:977
  375.8 30.6 %collective-permute-start.63 = (bf16[2,2,192,192]{3,2,1,0:T(8,128)(2,1)S(1)}, bf16[2,2,192,192]{3,2,1,0:T(8,128)(2,1)S(1)}, u32[]{:S(2)}, u32[]{:S(2)}) collective-permute-start(bf16[2,2,192,192]{3,2,1,0:T(8,128)(2,1)S(1)} %get-tuple-element.218), channel_id=1, source_target_pairs={{0,1},{1,0},{2,3},{3,2},{4,5},{5,4},{6,7},{7,6},{8,9},{9,8},{10,11... | collective-permute-start | bytes 884744 | tf_op jit(solution)/shard_map/ppermute | solution.py:980
  375.9 20.7 %collective-permute-start.52 = (bf16[128,768]{1,0:T(8,128)(2,1)S(1)}, bf16[128,768]{1,0:T(8,128)(2,1)S(1)}, u32[]{:S(2)}, u32[]{:S(2)}) collective-permute-start(bf16[128,768]{1,0:T(8,128)(2,1)S(1)} %memory_total.1.refs_5_.refs_1_), channel_id=1, source_target_pairs={{0,2},{1,3},{2,0},{3,1},{4,6},{5,7},{6,4},{7,5},{8,10},{9,11},{10,... | collective-permute-start | bytes 589832 | tf_op jit(solution)/shard_map/ppermute | solution.py:980
  383.9 21.0 %collective-permute-start.53 = (bf16[128,768]{1,0:T(8,128)(2,1)S(1)}, bf16[128,768]{1,0:T(8,128)(2,1)S(1)}, u32[]{:S(2)}, u32[]{:S(2)}) collective-permute-start(bf16[128,768]{1,0:T(8,128)(2,1)S(1)} %collective-permute-done.51.refs_2_), channel_id=1, source_target_pairs={{0,2},{1,3},{2,0},{3,1},{4,6},{5,7},{6,4},{7,5},{8,10},{9,11},{10,... | collective-permute-start | bytes 589832 | tf_op jit(solution)/shard_map/ppermute | solution.py:980
  387.9 23.9 %collective-permute-start.62 = (bf16[2,2,192,192]{3,2,1,0:T(8,128)(2,1)S(1)}, bf16[2,2,192,192]{3,2,1,0:T(8,128)(2,1)S(1)}, u32[]{:S(2)}, u32[]{:S(2)}) collective-permute-start(bf16[2,2,192,192]{3,2,1,0:T(8,128)(2,1)S(1)} %get-tuple-element.217), channel_id=1, source_target_pairs={{0,1},{1,0},{2,3},{3,2},{4,5},{5,4},{6,7},{7,6},{8,9},{9,8},{10,11... | collective-permute-start | bytes 884744 | tf_op jit(solution)/shard_map/ppermute | solution.py:980
  388.8 24.8 %collective-permute-start.69 = (f32[96,768]{1,0:T(8,128)S(1)}, f32[96,768]{1,0:T(8,128)S(1)}, u32[]{:S(2)}, u32[]{:S(2)}) collective-permute-start(f32[96,768]{1,0:T(8,128)S(1)} %get-tuple-element.223), channel_id=1, source_target_pairs={{0,4},{4,0},{8,12},{12,8},{16,20},{20,16},{24,28},{28,24},{1,5},{5... | collective-permute-start | bytes 884744 | tf_op jit(solution)/shard_map/ppermute | solution.py:973
  408.3 19.3 %collective-permute-start.65 = (f32[16,768]{1,0:T(8,128)S(1)}, f32[16,768]{1,0:T(8,128)S(1)}, u32[]{:S(2)}, u32[]{:S(2)}) collective-permute-start(f32[16,768]{1,0:T(8,128)S(1)} %tie.23.refs_1_), channel_id=1, source_target_pairs={{0,1},{1,0},{2,3},{3,2},{4,5},{5,4},{6,7},{7,6},{8,9},{9,8},{10,11... | collective-permute-start | bytes 147464 | tf_op jit(solution)/shard_map/ppermute | solution.py:980
  413.6 18.7 %collective-permute-start.64 = (bf16[2,192,192]{2,1,0:T(8,128)(2,1)S(1)}, bf16[2,192,192]{2,1,0:T(8,128)(2,1)S(1)}, u32[]{:S(2)}, u32[]{:S(2)}) collective-permute-start(bf16[2,192,192]{2,1,0:T(8,128)(2,1)S(1)} %get-tuple-element.221), channel_id=1, source_target_pairs={{0,2},{1,3},{2,0},{3,1},{4,6},{5,7},{6,4},{7,5},{8,10},{9,11},{10,... | collective-permute-start | bytes 442376 | tf_op jit(solution)/shard_map/ppermute | solution.py:980
  (137 other events, 1126.0 us)
Sparse Core Ops, SparseCore 0:
  44.0 91.0 all-gather.6
  171.0 75.1 all-gather.8
  300.0 70.0 all-gather.10

commit v6 on v5

--- a/solution.py
+++ b/solution.py
@@ -643,7 +643,9 @@
         pv[:, cols] = dv.astype(BF)
     total = dot(pk[...], weight(held, sems, pieces, 0, 0))
     total = total + dot(pv[...], weight(held, sems, pieces, 0, 1))
-    tok_grad[...] = (total + tok_part[...]).astype(BF)
+    count = tok_part.shape[0]
+    tok_grad[:count] = (total + tok_part[...]).astype(BF)
+    tok_grad[count:] = jnp.zeros((tok_grad.shape[0] - count, tok_grad.shape[1]), BF)
     put_halves(info, keep, send, dot(pq[...], weight(held, sems, pieces, 1, 0)).astype(BF))
     weight(held, sems, pieces, 1, 1)
 
@@ -1267,11 +1269,11 @@
             pack_backward_kernel,
             "pack_backward",
             [back, sel, q_pack, k_pack, v_pack, tok_part] + w_pack,
-            [slot_low, tok_low, tok_low, tok_low, half_low, half_low],
+            [slot_low, tok_low, tok_low, ((block_len + 16, width), BF), half_low, half_low],
             anys=8,
             scratch=[held_pair, pair_sems],
         )
-        grad_tokens = lax.all_gather(grad_tokens, "head", axis=0)
+        grad_tokens = lax.all_gather(grad_tokens, "head", axis=0)[:, :block_len]
         pack_operands = (tok, pk_grad, pv_grad, mem_slot, pq_part, pack_ctx, mem_mix_grad)
         got = swap(send, unit // 2)
         if fast:
@@ -1314,7 +1316,8 @@
             return [keep, swap(send, 1)]
 
         def ffn_final(halves):
-            return run(ffn_final_kernel, "weight_rows", halves, [(half, F32)] * 2)
+            outs = [(half, F32)] * 2
+            return run(ffn_final_kernel, "weight_rows", halves, outs, also=[grad_tokens])
 
         def attention_blocks(kept, got):
             keep, send = run(

time: 456 us -> 442 us (0.969)
  the two profiles are of different devices: /device:TPU:0 before, /device:TPU:5 now
where the time goes in v6:
time: 442 us; the launch traced here: 434 us
  Pallas kernels  167 us (38%)
  waiting for transfers between devices  149 us (34%)
  starting transfers between devices  64.1 us (15%)
  local copies, waits for them, and re-layouts  34.7 us (8%)
  between operations  15.2 us (3%)
    pallas_call x38, Pallas kernels, call(): pl.pallas_call(body, out_shape=[jax.ShapeDtypeStruct(s, d) for s, d in ou...  140 us
    ppermute x43, waiting for transfers between devices, swap(): return lax.ppermute(value, 'seq', [(i, i ^ step) for i in range(axis_seq)])  52.6 us
    ppermute x15, waiting for transfers between devices, over(): lax.ppermute(value, 'head', [(i, i ^ step) for i in range(axis_head)])  46.4 us
    ppermute x14, waiting for transfers between devices, cross(): lax.ppermute(value, 'seq', [(i, i ^ steps[i % 2]) for i in range(axis_seq)])  45.7 us
    ppermute x43, starting transfers between devices, swap(): return lax.ppermute(value, 'seq', [(i, i ^ step) for i in range(axis_seq)])  36.5 us
    unnamed x174, local copies, waits for them, and re-layouts  30.7 us
    pallas_call x2, Pallas kernels, ffn_weight_grad(): pl.pallas_call(kernel, out_shape=[jax.ShapeDtypeStruct((half, width, cols...  18 us
    ppermute x15, starting transfers between devices, over(): lax.ppermute(value, 'head', [(i, i ^ step) for i in range(axis_head)])  15.4 us
  transfers between devices with their start and end apart: 75, of which 31 were waited for; matrix products, arithmetic and copies ran while one was open for 2% of the time, Pallas kernels for 31%

profile of v6, /device:TPU:5, one launch (start us, length us, event | category | flops | bytes accessed | tf_op | source)
XLA Modules:
  0.0 434.3 jit_solution(12930618312150526041)
XLA Ops:
  14.1 10.7 %collective-permute-done.4.refs_2_ = bf16[4,48,768]{2,1,0:T(8,128)(2,1)S(1)} collective-permute-done((bf16[4,48,768]{2,1,0:T(8,128)(2,1)}, bf16[4,48,768]{2,1,0:T(8,128)(2,1)S(1)}, u32[]{:S(2)}, u32[]{:S(2)}) %collective-permute-start.4) | collective-permute-done | bytes 294944 | tf_op jit(solution)/shard_map/ppermute | solution.py:982
  44.1 11.6 %collective-permute-done.7.refs_4_.refs_11_.refs_10_.refs_8_ = bf16[2,4,48,768]{3,2,1,0:T(8,128)(2,1)S(1)} collective-permute-done((bf16[2,4,48,768]{3,2,1,0:T(8,128)(2,1)S(1)}, bf16[2,4,48,768]{3,2,1,0:T(8,128)(2,1)S(1)}, u32[]{:S(2)}, u32[]{:S(2)}) %collective-permute-start.7) | collective-permute-done | bytes 589856 | tf_op jit(solution)/shard_map/ppermute | solution.py:979
  60.2 5.4 %collective-permute-done.9.refs_6_.refs_1_.refs_13_.refs_12_.refs_10_ = bf16[2,4,48,768]{3,2,1,0:T(8,128)(2,1)S(1)} collective-permute-done((bf16[2,4,48,768]{3,2,1,0:T(8,128)(2,1)S(1)}, bf16[2,4,48,768]{3,2,1,0:T(8,128)(2,1)S(1)}, u32[]{:S(2)}, u32[]{:S(2)}) %collective-permute-start.9) | collective-permute-done | bytes 589856 | tf_op jit(solution)/shard_map/ppermute | solution.py:979
  72.2 12.5 %pack_forward.1 = (bf16[512,768]{1,0:T(8,128)(2,1)}, bf16[512,768]{1,0:T(8,128)(2,1)}, bf16[256,768]{1,0:T(8,128)(2,1)}, bf16[128,896]{1,0:T(8,128)(2,1)}, bf16[128,896]{1,0:T(8,128)(2,1)}) custom-call(s32[16]{0:T(128)} %get-tuple-element.130.refs_0_.info, bf16[512,768]{1,0:T(8,128)(2,1)} %get-tuple-element.131.refs_1_.refs_5_.refs_2_, ...), custom_call_target="tpu_custom_call" | custom-call | flops 1 | bytes 1 | tf_op jit(solution)/shard_map/pack_forward/pallas_call | solution.py:50
  93.0 6.8 %collective-permute-done.16.refs_2_ = bf16[128,896]{1,0:T(8,128)(2,1)S(1)} collective-permute-done((bf16[128,896]{1,0:T(8,128)(2,1)S(1)}, bf16[128,896]{1,0:T(8,128)(2,1)S(1)}, u32[]{:S(2)}, u32[]{:S(2)}) %collective-permute-start.16) | collective-permute-done | bytes 229408 | tf_op jit(solution)/shard_map/ppermute | solution.py:975
  101.2 6.5 %collective-permute-done.18.refs_4_ = bf16[128,896]{1,0:T(8,128)(2,1)S(1)} collective-permute-done((bf16[128,896]{1,0:T(8,128)(2,1)S(1)}, bf16[128,896]{1,0:T(8,128)(2,1)S(1)}, u32[]{:S(2)}, u32[]{:S(2)}) %collective-permute-start.18) | collective-permute-done | bytes 229408 | tf_op jit(solution)/shard_map/ppermute | solution.py:975
  134.3 12.5 %unpack_forward.1 = (bf16[256,768]{1,0:T(8,128)(2,1)}, bf16[256,768]{1,0:T(8,128)(2,1)}, bf16[512,768]{1,0:T(8,128)(2,1)}, bf16[512,768]{1,0:T(8,128)(2,1)}, f32...) custom-call(s32[16]{0:T(128)} %get-tuple-element.130.refs_0_.info, ...), custom_call_target="tpu_custom_call" | custom-call | flops 1 | bytes 1 | tf_op jit(solution)/shard_map/unpack_forward/pallas_call | solution.py:50
  146.8 23.3 %ffn.1 = (bf16[640,768]{1,0:T(8,128)(2,1)}, bf16[512,768]{1,0:T(8,128)(2,1)}, bf16[512,768]{1,0:T(8,128)(2,1)}, bf16[512,768]{1,0:T(8,128)(2,1)}, f32[512,768]{1...) custom-call(s32[16]{0:T(128)} %get-tuple-element.130.refs_0_.info, ...), custom_call_target="tpu_custom_call" | custom-call | flops 1 | bytes 1 | tf_op jit(solution)/shard_map/ffn/pallas_call | solution.py:50
  174.0 15.5 %unpack_backward.1 = (bf16[512,768]{1,0:T(8,128)(2,1)}, bf16[256,768]{1,0:T(8,128)(2,1)}, bf16[256,768]{1,0:T(8,128)(2,1)}, bf16[128,768]{1,0:T(8,128)(2,1)}, bf...) custom-call(s32[16]{0:T(128)} %get-tuple-element.130.refs_0_.info, bf16[512,768]{1,0:T(8,128)(2,1)} %get-tuple-element.152.refs_1_, ...), custom_call_target="tpu_custom_call" | custom-call | flops 1 | bytes 1 | tf_op jit(solution)/shard_map/unpack_backward/pallas_call | solution.py:50
  192.6 7.9 %ffn_weight_grad.2 = (bf16[2,768,768]{2,1,0:T(8,128)(2,1)}, bf16[2,768,768]{2,1,0:T(8,128)(2,1)}) custom-call(s32[1]{0:T(128)S(6)} %sub.7.which.refs_1_, s32[16]{0:T(128)} %get-tuple-element.130.refs_0_.info, bf16[512,768]{1,0:T(8,128)(2,1)} %get-tuple-element.163.attn_ref, bf16[4,512,768]{2,1,0:T(8,128)(2,1)} %get-tuple-element.164.hid_ref, ...), custom_call_target="tpu_custom_call" | custom-call | flops 1 | bytes 1 | tf_op jit(solution)/shard_map/ffn_weight_grad/pallas_call | solution.py:732
  201.1 4.5 %collective-permute-done.30.refs_2_ = bf16[128,768]{1,0:T(8,128)(2,1)S(1)} collective-permute-done((bf16[128,768]{1,0:T(8,128)(2,1)S(1)}, bf16[128,768]{1,0:T(8,128)(2,1)S(1)}, u32[]{:S(2)}, u32[]{:S(2)}) %collective-permute-start.30) | collective-permute-done | bytes 196640 | tf_op jit(solution)/shard_map/ppermute | solution.py:975
  214.2 10.0 %ffn_weight_grad.3 = (bf16[2,2,192,768]{3,2,1,0:T(8,128)(2,1)}, bf16[2,2,192,768]{3,2,1,0:T(8,128)(2,1)}, bf16[2,2,192,768]{3,2,1,0:T(8,128)(2,1)}, bf16[2,2,192,768]{3,2,1,0:T(8,128)(2,1)}) custom-call(s32[1]{0:T(128)} %bitcast.10.which.refs_1_, s32[16]{0:T(128)} %get-tuple-element.130.refs_0_.info, bf16[512,768]{1,0:T(8,128)(2,1)} %get-tuple-element.163.attn_ref, ...), custom_call_target="tpu_custom_call" | custom-call | flops 1 | bytes 1 | tf_op jit(solution)/shard_map/ffn_weight_grad/pallas_call | solution.py:732
  234.6 4.6 %attention_weight_grad.4.refs_5_.refs_0_ = bf16[2,768,768]{2,1,0:T(8,128)(2,1)} custom-call(s32[16]{0:T(128)} %get-tuple-element.130.refs_0_.info, s32[1]{0:T(128)S(6)} %sub.7.which.refs_1_, bf16[256,768]{1,0:T(8,128)(2,1)} %copy-done.7, bf16[256,768]{1,0:T(8,128)(2,1)} %get-tuple-element.179.refs_3_, bf16[256,768]{1,0:T(8,128)(2,1)} %get-tuple-element.180.refs_4_, ...), custom_call_target="tpu_custom_call" | custom-call | flops 1 | bytes 1 | tf_op jit(solution)/shard_map/attention_weight_grad/pallas_call | solution.py:50
  255.4 12.9 %pack_backward.1 = (bf16[256,768]{1,0:T(8,128)(2,1)}, bf16[512,768]{1,0:T(8,128)(2,1)}, bf16[512,768]{1,0:T(8,128)(2,1)}, bf16[528,768]{1,0:T(8,128)(2,1)}, bf16...) custom-call(s32[16]{0:T(128)} %get-tuple-element.130.refs_0_.info, bf16[256,896]{1,0:T(8,128)(2,1)} %pad_maximum_fusion.refs_1_, ...), custom_call_target="tpu_custom_call" | custom-call | flops 1 | bytes 1 | tf_op jit(solution)/shard_map/pack_backward/pallas_call | solution.py:50
  274.6 6.1 %attention_weight_grad.5 = (bf16[2,2,192,768]{3,2,1,0:T(8,128)(2,1)}, bf16[2,2,192,768]{3,2,1,0:T(8,128)(2,1)}) custom-call(s32[16]{0:T(128)} %get-tuple-element.130.refs_0_.info, s32[1]{0:T(128)} %bitcast.10.which.refs_1_, bf16[256,768]{1,0:T(8,128)(2,1)} %copy-done.7, bf16[256,768]{1,0:T(8,128)(2,1)} %get-tuple-element.179.refs_3_, ...), custom_call_target="tpu_custom_call" | custom-call | flops 1 | bytes 1 | tf_op jit(solution)/shard_map/attention_weight_grad/pallas_call | solution.py:50
  280.6 5.3 %attention_weight_grad.6.refs_3_.refs_0_ = bf16[2,768,768]{2,1,0:T(8,128)(2,1)} custom-call(s32[16]{0:T(128)} %get-tuple-element.130.refs_0_.info, s32[1]{0:T(128)S(6)} %sub.7.which.refs_1_, bf16[512,768]{1,0:T(8,128)(2,1)} %get-tuple-element.131.refs_1_.refs_5_.refs_2_, bf16[512,768]{1,0:T(8,128)(2,1)} %get-tuple-element.188.refs_3_, ...), custom_call_target="tpu_custom_call" | custom-call | flops 1 | bytes 1 | tf_op jit(solution)/shard_map/attention_weight_grad/pallas_call | solution.py:50
  305.1 5.5 %attention_weight_grad.7 = (bf16[2,2,192,768]{3,2,1,0:T(8,128)(2,1)}, bf16[2,2,192,768]{3,2,1,0:T(8,128)(2,1)}) custom-call(s32[16]{0:T(128)} %get-tuple-element.130.refs_0_.info, s32[1]{0:T(128)} %bitcast.10.which.refs_1_, bf16[512,768]{1,0:T(8,128)(2,1)} %get-tuple-element.131.refs_1_.refs_5_.refs_2_, bf16[512,768]{1,0:T(8,128)(2,1)} %get-tuple-element.188.refs_3_, ...), custom_call_target="tpu_custom_call" | custom-call | flops 1 | bytes 1 | tf_op jit(solution)/shard_map/attention_weight_grad/pallas_call | solution.py:50
  310.6 9.3 %collective-permute-done.46.refs_3_ = bf16[128,768]{1,0:T(8,128)(2,1)} collective-permute-done((bf16[128,768]{1,0:T(8,128)(2,1)}, bf16[128,768]{1,0:T(8,128)(2,1)}, u32[]{:S(2)}, u32[]{:S(2)}) %collective-permute-start.46) | collective-permute-done | bytes 196640 | tf_op jit(solution)/shard_map/ppermute | solution.py:975
  329.8 11.6 %collective-permute-done.58.got_ref = bf16[2,2,192,768]{3,2,1,0:T(8,128)(2,1)S(1)} collective-permute-done((bf16[2,2,192,768]{3,2,1,0:T(8,128)(2,1)S(1)}, bf16[2,2,192,768]{3,2,1,0:T(8,128)(2,1)S(1)}, u32[]{:S(2)}, u32[]{:S(2)}) %collective-permute-start.58) | collective-permute-done | bytes 1179680 | tf_op jit(solution)/shard_map/ppermute | solution.py:979
  343.2 17.2 %collective-permute-done.57.got_ref = bf16[2,2,192,768]{3,2,1,0:T(8,128)(2,1)S(1)} collective-permute-done((bf16[2,2,192,768]{3,2,1,0:T(8,128)(2,1)S(1)}, bf16[2,2,192,768]{3,2,1,0:T(8,128)(2,1)S(1)}, u32[]{:S(2)}, u32[]{:S(2)}) %collective-permute-start.57) | collective-permute-done | bytes 1179680 | tf_op jit(solution)/shard_map/ppermute | solution.py:979
  367.7 5.3 %collective-permute-done.51.refs_2_ = bf16[128,768]{1,0:T(8,128)(2,1)S(1)} collective-permute-done((bf16[128,768]{1,0:T(8,128)(2,1)S(1)}, bf16[128,768]{1,0:T(8,128)(2,1)S(1)}, u32[]{:S(2)}, u32[]{:S(2)}) %collective-permute-start.51) | collective-permute-done | bytes 196640 | tf_op jit(solution)/shard_map/ppermute | solution.py:982
  379.8 5.9 %collective-permute-done.52.refs_3_ = bf16[128,768]{1,0:T(8,128)(2,1)S(1)} collective-permute-done((bf16[128,768]{1,0:T(8,128)(2,1)S(1)}, bf16[128,768]{1,0:T(8,128)(2,1)S(1)}, u32[]{:S(2)}, u32[]{:S(2)}) %collective-permute-start.52) | collective-permute-done | bytes 196640 | tf_op jit(solution)/shard_map/ppermute | solution.py:982
  385.7 9.1 %collective-permute-done.53.refs_4_ = bf16[128,768]{1,0:T(8,128)(2,1)S(1)} collective-permute-done((bf16[128,768]{1,0:T(8,128)(2,1)S(1)}, bf16[128,768]{1,0:T(8,128)(2,1)S(1)}, u32[]{:S(2)}, u32[]{:S(2)}) %collective-permute-start.53) | collective-permute-done | bytes 196640 | tf_op jit(solution)/shard_map/ppermute | solution.py:982
  407.8 7.5 %collective-permute-done.68.refs_2_ = bf16[2,192,192]{2,1,0:T(8,128)(2,1)S(1)} collective-permute-done((bf16[2,192,192]{2,1,0:T(8,128)(2,1)S(1)}, bf16[2,192,192]{2,1,0:T(8,128)(2,1)S(1)}, u32[]{:S(2)}, u32[]{:S(2)}) %collective-permute-start.68) | collective-permute-done | bytes 147488 | tf_op jit(solution)/shard_map/ppermute | solution.py:982
  (374 shorter events, 191.7 us)
Async XLA Ops:
  7.2 126.5 %all-gather.7.cloned.1.call-start = ((), (), s32[]{:S(2)}) async-start(), calls=%async_computation | async-start | bytes 6021120 | tf_op jit(solution)/shard_map/all_gather | solution.py:1142
  11.8 25.8 %collective-permute-start.5 = (bf16[4,48,768]{2,1,0:T(8,128)(2,1)}, bf16[4,48,768]{2,1,0:T(8,128)(2,1)S(1)}, u32[]{:S(2)}, u32[]{:S(2)}) collective-permute-start(bf16[4,48,768]{2,1,0:T(8,128)(2,1)} %get-tuple-element.134.refs_1_), channel_id=1, source_target_pairs={{0,2},{1,3},{2,0},{3,1},{4,6},{5,7},{6,4},{7,5},{8,10},{9,11},{10,... | collective-permute-start | bytes 884744 | tf_op jit(solution)/shard_map/ppermute | solution.py:982
  42.6 202.1 %all-gather.9.cloned.1.call-start = ((), (), s32[]{:S(2)}) async-start(), calls=%async_computation.1 | async-start | bytes 4915200 | tf_op jit(solution)/shard_map/all_gather | solution.py:1215
  91.3 22.1 %collective-permute-start.24 = (bf16[2,4,48,768]{3,2,1,0:T(8,128)(2,1)S(1)}, bf16[2,4,48,768]{3,2,1,0:T(8,128)(2,1)S(1)}, u32[]{:S(2)}, u32[]{:S(2)}) collective-permute-start(bf16[2,4,48,768]{3,2,1,0:T(8,128)(2,1)S(1)} %tie.12.refs_6_.refs_3_.refs_8_), channel_id=1, source_target_pairs={{0,4},{4,0},{8,12},{12,8},{16,20},{20,16},{24,28},{28,24},{1,5},{5... | collective-permute-start | bytes 1769480 | tf_op jit(solution)/shard_map/ppermute | solution.py:975
  91.9 22.1 %collective-permute-start.25 = (bf16[2,4,48,768]{3,2,1,0:T(8,128)(2,1)S(1)}, bf16[2,4,48,768]{3,2,1,0:T(8,128)(2,1)}, u32[]{:S(2)}, u32[]{:S(2)}) collective-permute-start(bf16[2,4,48,768]{3,2,1,0:T(8,128)(2,1)S(1)} %tie.13.refs_7_.refs_4_.refs_9_), channel_id=1, source_target_pairs={{0,4},{4,0},{8,12},{12,8},{16,20},{20,16},{24,28},{28,24},{1,5},{5... | collective-permute-start | bytes 1769480 | tf_op jit(solution)/shard_map/ppermute | solution.py:975
  99.9 22.9 %collective-permute-start.27 = (bf16[2,4,48,768]{3,2,1,0:T(8,128)(2,1)}, bf16[2,4,48,768]{3,2,1,0:T(8,128)(2,1)}, u32[]{:S(2)}, u32[]{:S(2)}) collective-permute-start(bf16[2,4,48,768]{3,2,1,0:T(8,128)(2,1)} %collective-permute-done.20.refs_19_.refs_9_.refs_6_.refs_11_), channel_id=1, source_target_pairs={{0,4},{4,0},{8,12},{12,8},{16,20},{20,16},{24,28},{28,24},{1,5},{5... | collective-permute-start | bytes 1769480 | tf_op jit(solution)/shard_map/ppermute | solution.py:975
  170.2 233.7 %all-gather.11.cloned.1.call-start = ((), (), s32[]{:S(2)}) async-start(), calls=%async_computation.2 | async-start | bytes 4055040 | tf_op jit(solution)/shard_map/all_gather | solution.py:1276
  248.1 26.4 %collective-permute-start.44 = (bf16[2,768,768]{2,1,0:T(8,128)(2,1)S(1)}, bf16[2,768,768]{2,1,0:T(8,128)(2,1)}, u32[]{:S(2)}, u32[]{:S(2)}) collective-permute-start(bf16[2,768,768]{2,1,0:T(8,128)(2,1)S(1)} %tie.16), channel_id=1, source_target_pairs={{0,4},{4,0},{8,12},{12,8},{16,20},{20,16},{24,28},{28,24},{1,5},{5... | collective-permute-start | bytes 7077896 | tf_op jit(solution)/shard_map/ppermute | solution.py:975
  272.7 22.2 %collective-permute-start.49 = (bf16[2,2,192,768]{3,2,1,0:T(8,128)(2,1)}, bf16[2,2,192,768]{3,2,1,0:T(8,128)(2,1)}, u32[]{:S(2)}, u32[]{:S(2)}) collective-permute-start(bf16[2,2,192,768]{3,2,1,0:T(8,128)(2,1)} %tie.18), channel_id=1, source_target_pairs={{0,8},{4,20},{8,0},{12,28},{16,24},{20,4},{24,16},{28,12},{1,9},{5... | collective-permute-start | bytes 3538952 | tf_op jit(solution)/shard_map/ppermute | solution.py:979
  297.9 29.2 %collective-permute-start.54 = (bf16[2,192,768]{2,1,0:T(8,128)(2,1)}, bf16[2,192,768]{2,1,0:T(8,128)(2,1)}, u32[]{:S(2)}, u32[]{:S(2)}) collective-permute-start(bf16[2,192,768]{2,1,0:T(8,128)(2,1)} %tie.20), channel_id=1, source_target_pairs={{0,16},{4,12},{8,24},{12,4},{16,0},{20,28},{24,8},{28,20},{1,17},{... | collective-permute-start | bytes 1769480 | tf_op jit(solution)/shard_map/ppermute | solution.py:979
  298.6 28.5 %collective-permute-start.55 = (bf16[2,192,768]{2,1,0:T(8,128)(2,1)}, bf16[2,192,768]{2,1,0:T(8,128)(2,1)}, u32[]{:S(2)}, u32[]{:S(2)}) collective-permute-start(bf16[2,192,768]{2,1,0:T(8,128)(2,1)} %get-tuple-element.203), channel_id=1, source_target_pairs={{0,16},{4,12},{8,24},{12,4},{16,0},{20,28},{24,8},{28,20},{1,17},{... | collective-permute-start | bytes 1769480 | tf_op jit(solution)/shard_map/ppermute | solution.py:979
  299.3 20.5 %collective-permute-start.46 = (bf16[128,768]{1,0:T(8,128)(2,1)}, bf16[128,768]{1,0:T(8,128)(2,1)}, u32[]{:S(2)}, u32[]{:S(2)}) collective-permute-start(bf16[128,768]{1,0:T(8,128)(2,1)} %get-tuple-element.195), channel_id=1, source_target_pairs={{0,8},{4,12},{8,0},{12,4},{16,24},{20,28},{24,16},{28,20},{1,9},{5... | collective-permute-start | bytes 589832 | tf_op jit(solution)/shard_map/ppermute | solution.py:975
  300.1 19.8 %collective-permute-start.47 = (bf16[128,768]{1,0:T(8,128)(2,1)}, bf16[128,768]{1,0:T(8,128)(2,1)}, u32[]{:S(2)}, u32[]{:S(2)}) collective-permute-start(bf16[128,768]{1,0:T(8,128)(2,1)} %get-tuple-element.196), channel_id=1, source_target_pairs={{0,16},{4,20},{8,24},{12,28},{16,0},{20,4},{24,8},{28,12},{1,17},{... | collective-permute-start | bytes 589832 | tf_op jit(solution)/shard_map/ppermute | solution.py:975
  303.0 19.0 %collective-permute-start.48 = (bf16[128,768]{1,0:T(8,128)(2,1)}, bf16[128,768]{1,0:T(8,128)(2,1)}, u32[]{:S(2)}, u32[]{:S(2)}) collective-permute-start(bf16[128,768]{1,0:T(8,128)(2,1)} %get-tuple-element.197), channel_id=1, source_target_pairs={{0,24},{4,28},{8,16},{12,20},{16,8},{20,12},{24,0},{28,4},{1,25},{... | collective-permute-start | bytes 589832 | tf_op jit(solution)/shard_map/ppermute | solution.py:975
  328.7 31.7 %collective-permute-start.57 = (bf16[2,2,192,768]{3,2,1,0:T(8,128)(2,1)S(1)}, bf16[2,2,192,768]{3,2,1,0:T(8,128)(2,1)S(1)}, u32[]{:S(2)}, u32[]{:S(2)}) collective-permute-start(bf16[2,2,192,768]{3,2,1,0:T(8,128)(2,1)S(1)} %tie.21), channel_id=1, source_target_pairs={{0,8},{4,20},{8,0},{12,28},{16,24},{20,4},{24,16},{28,12},{1,9},{5... | collective-permute-start | bytes 3538952 | tf_op jit(solution)/shard_map/ppermute | solution.py:979
  329.8 32.3 %collective-permute-start.56 = (bf16[2,192,768]{2,1,0:T(8,128)(2,1)S(1)}, bf16[2,192,768]{2,1,0:T(8,128)(2,1)S(1)}, u32[]{:S(2)}, u32[]{:S(2)}) collective-permute-start(bf16[2,192,768]{2,1,0:T(8,128)(2,1)S(1)} %get-tuple-element.205), channel_id=1, source_target_pairs={{0,1},{1,0},{2,3},{3,2},{4,5},{5,4},{6,7},{7,6},{8,9},{9,8},{10,11... | collective-permute-start | bytes 1769480 | tf_op jit(solution)/shard_map/ppermute | solution.py:982
  342.4 20.8 %collective-permute-start.61 = (bf16[2,192,768]{2,1,0:T(8,128)(2,1)S(1)}, bf16[2,192,768]{2,1,0:T(8,128)(2,1)S(1)}, u32[]{:S(2)}, u32[]{:S(2)}) collective-permute-start(bf16[2,192,768]{2,1,0:T(8,128)(2,1)S(1)} %get-tuple-element.213), channel_id=1, source_target_pairs={{0,16},{4,12},{8,24},{12,4},{16,0},{20,28},{24,8},{28,20},{1,17},{... | collective-permute-start | bytes 1769480 | tf_op jit(solution)/shard_map/ppermute | solution.py:979
  364.2 32.1 %collective-permute-start.63 = (bf16[2,2,192,192]{3,2,1,0:T(8,128)(2,1)S(1)}, bf16[2,2,192,192]{3,2,1,0:T(8,128)(2,1)S(1)}, u32[]{:S(2)}, u32[]{:S(2)}) collective-permute-start(bf16[2,2,192,192]{3,2,1,0:T(8,128)(2,1)S(1)} %get-tuple-element.218), channel_id=1, source_target_pairs={{0,1},{1,0},{2,3},{3,2},{4,5},{5,4},{6,7},{7,6},{8,9},{9,8},{10,11... | collective-permute-start | bytes 884744 | tf_op jit(solution)/shard_map/ppermute | solution.py:982
  365.4 20.3 %collective-permute-start.52 = (bf16[128,768]{1,0:T(8,128)(2,1)S(1)}, bf16[128,768]{1,0:T(8,128)(2,1)S(1)}, u32[]{:S(2)}, u32[]{:S(2)}) collective-permute-start(bf16[128,768]{1,0:T(8,128)(2,1)S(1)} %memory_total.1.refs_5_.refs_1_), channel_id=1, source_target_pairs={{0,2},{1,3},{2,0},{3,1},{4,6},{5,7},{6,4},{7,5},{8,10},{9,11},{10,... | collective-permute-start | bytes 589832 | tf_op jit(solution)/shard_map/ppermute | solution.py:982
  373.0 21.8 %collective-permute-start.53 = (bf16[128,768]{1,0:T(8,128)(2,1)S(1)}, bf16[128,768]{1,0:T(8,128)(2,1)S(1)}, u32[]{:S(2)}, u32[]{:S(2)}) collective-permute-start(bf16[128,768]{1,0:T(8,128)(2,1)S(1)} %collective-permute-done.51.refs_2_), channel_id=1, source_target_pairs={{0,2},{1,3},{2,0},{3,1},{4,6},{5,7},{6,4},{7,5},{8,10},{9,11},{10,... | collective-permute-start | bytes 589832 | tf_op jit(solution)/shard_map/ppermute | solution.py:982
  376.2 24.3 %collective-permute-start.62 = (bf16[2,2,192,192]{3,2,1,0:T(8,128)(2,1)S(1)}, bf16[2,2,192,192]{3,2,1,0:T(8,128)(2,1)S(1)}, u32[]{:S(2)}, u32[]{:S(2)}) collective-permute-start(bf16[2,2,192,192]{3,2,1,0:T(8,128)(2,1)S(1)} %get-tuple-element.217), channel_id=1, source_target_pairs={{0,1},{1,0},{2,3},{3,2},{4,5},{5,4},{6,7},{7,6},{8,9},{9,8},{10,11... | collective-permute-start | bytes 884744 | tf_op jit(solution)/shard_map/ppermute | solution.py:982
  378.6 23.8 %collective-permute-start.69 = (f32[96,768]{1,0:T(8,128)S(1)}, f32[96,768]{1,0:T(8,128)S(1)}, u32[]{:S(2)}, u32[]{:S(2)}) collective-permute-start(f32[96,768]{1,0:T(8,128)S(1)} %get-tuple-element.223), channel_id=1, source_target_pairs={{0,4},{4,0},{8,12},{12,8},{16,20},{20,16},{24,28},{28,24},{1,5},{5... | collective-permute-start | bytes 884744 | tf_op jit(solution)/shard_map/ppermute | solution.py:975
  398.1 18.8 %collective-permute-start.65 = (f32[16,768]{1,0:T(8,128)S(1)}, f32[16,768]{1,0:T(8,128)S(1)}, u32[]{:S(2)}, u32[]{:S(2)}) collective-permute-start(f32[16,768]{1,0:T(8,128)S(1)} %tie.23.refs_1_), channel_id=1, source_target_pairs={{0,1},{1,0},{2,3},{3,2},{4,5},{5,4},{6,7},{7,6},{8,9},{9,8},{10,11... | collective-permute-start | bytes 147464 | tf_op jit(solution)/shard_map/ppermute | solution.py:982
  402.4 19.3 %collective-permute-start.64 = (bf16[2,192,192]{2,1,0:T(8,128)(2,1)S(1)}, bf16[2,192,192]{2,1,0:T(8,128)(2,1)S(1)}, u32[]{:S(2)}, u32[]{:S(2)}) collective-permute-start(bf16[2,192,192]{2,1,0:T(8,128)(2,1)S(1)} %get-tuple-element.221), channel_id=1, source_target_pairs={{0,2},{1,3},{2,0},{3,1},{4,6},{5,7},{6,4},{7,5},{8,10},{9,11},{10,... | collective-permute-start | bytes 442376 | tf_op jit(solution)/shard_map/ppermute | solution.py:982
  (138 other events, 1119.7 us)
Sparse Core Ops, SparseCore 0:
  42.7 90.9 all-gather.6
  170.3 74.3 all-gather.8
  274.2 61.1 all-gather.10
